TPU v7x, 512 devices: a whole 4x8x8 slice. The times are simulated.
512 devices in a mesh: graph: 64 (over y, z_lo, core), fsdp: 8 (over z_hi, x).
Axes of the slice: x: 4, y: 8, z: 8 (z_hi: 2, z_lo: 4; z = z_hi * 4 + z_lo), core: 2. Of those that a mesh axis runs over, the one named last changes fastest.
Arguments:
- node_features: bfloat16 [8, 8192, 512], P('fsdp', 'graph'), may hold values from -6 to 6
- out_grad: bfloat16 [8, 8192, 512], P('fsdp', 'graph'), may hold values from -6 to 6
- send_weight: bfloat16 [2, 512, 512], P(None, 'fsdp'), may hold values from -0.25 to 0.25
- recv_weight: bfloat16 [2, 512, 512], P(None, 'fsdp'), may hold values from -0.25 to 0.25
- gain: float32 [2, 512], replicated, may hold values from 0.1 to 1.9
- senders: int32 [64, 512], P('graph'), may hold values from 0 to 143, as said below
- receivers: int32 [64, 512], P('graph'), may hold values from 0 to 127
- edge_count: int32 [64], P('graph'), may hold values from 256 to 512, as said below
- send_rows: int32 [64, 2, 8], P('graph'), may hold values from 0 to 127, as said below
Outputs:
- updated: bfloat16 [8, 8192, 512], P('fsdp', 'graph')
- feature_grad: bfloat16 [8, 8192, 512], P('fsdp', 'graph')
- send_grad: float32 [2, 512, 512], P(None, 'fsdp')
- recv_grad: float32 [2, 512, 512], P(None, 'fsdp')
- gain_grad: float32 [2, 512], replicated
Inputs may be any that keep to these rules, and one draw needn't show every extreme that they name: `senders`: rows 0 to 127 are the partition's own, the next 8 came from the previous partition, the last 8 from the next. The live slots of a partition are its first edge_count slots; some partition fills all 512. `send_rows`: the 16 rows of one partition are distinct.
All inputs are finite; a program needn't handle non-finite values.
Results may differ from a plain program's by a relative error of at most 0.019.
Values may be sent and summed in bfloat16 or wider, within the bound.
No kernel may reach another device: no remote copies, remote signals or barrier semaphores. Data moves between devices by JAX's collectives and lax.ppermute only.
A program may use at most 64 MiB of HBM per device.

v0:
```python
import jax
import jax.numpy as jnp
from jax import lax
from jax.sharding import PartitionSpec as P

EPSILON = 1e-05
loss_scale = 512.0


def from_behind(value, axis, steps):
    count = lax.axis_size(axis)
    pairs = [(source, (source + steps) % count) for source in range(count)]
    return lax.ppermute(value, axis, pairs)


def layer_tail(proj_send, own_rows, recv_matrix, gain_row, sender_ids, receiver_ids, live_mask):
    proj_recv = jnp.dot(own_rows, recv_matrix, preferred_element_type=jnp.float32)
    preact = jnp.take(proj_send, sender_ids, axis=0) + jnp.take(proj_recv, receiver_ids, axis=0)
    message = jax.nn.silu(preact) * live_mask[:, None]
    total = jax.ops.segment_sum(message, receiver_ids, num_segments=own_rows.shape[0])
    factor = lax.rsqrt(jnp.mean(total * total, axis=-1, keepdims=True) + EPSILON)
    return (own_rows.astype(jnp.float32) + gain_row[None, :] * total * factor).astype(jnp.bfloat16)


def layer_local(
    ext_rows, own_rows, send_matrix, recv_matrix, gain_row, sender_ids, receiver_ids, live_mask
):
    proj_send = jnp.dot(ext_rows, send_matrix, preferred_element_type=jnp.float32)
    return layer_tail(
        proj_send, own_rows, recv_matrix, gain_row, sender_ids, receiver_ids, live_mask
    )


def pullback_of(
    ext_rows, own_rows, send_matrix, recv_matrix, gain_row, sender_ids, receiver_ids, live_mask
):

    def local_map(ext_in, own_in, send_in, recv_in, gain_in):
        return layer_local(
            ext_in, own_in, send_in, recv_in, gain_in, sender_ids, receiver_ids, live_mask
        )

    return jax.vjp(local_map, ext_rows, own_rows, send_matrix, recv_matrix, gain_row)


def shards(
    node_features,
    out_grad,
    send_weight,
    recv_weight,
    gain,
    senders,
    receivers,
    edge_count,
    send_rows,
):
    layer_total = send_weight.shape[0]
    own_count = node_features.shape[1]
    halo_count = send_rows.shape[2]
    sender_ids = senders[0]
    receiver_ids = receivers[0]
    live_mask = (jnp.arange(senders.shape[1], dtype=jnp.int32) < edge_count[0]).astype(jnp.float32)
    upper_ids = send_rows[0, 0]
    lower_ids = send_rows[0, 1]
    features = node_features[0]
    stored = []
    for layer_index in range(layer_total):
        weight_pair = (
            lax.all_gather(send_weight[layer_index], "fsdp", axis=0, tiled=True),
            lax.all_gather(recv_weight[layer_index], "fsdp", axis=0, tiled=True),
        )
        from_prev = from_behind(jnp.take(features, upper_ids, axis=0), "graph", 1)
        from_next = from_behind(jnp.take(features, lower_ids, axis=0), "graph", -1)
        ext_rows = jnp.concatenate([features, from_prev, from_next], axis=0)
        result, pullback = pullback_of(
            ext_rows,
            features,
            weight_pair[0],
            weight_pair[1],
            gain[layer_index],
            sender_ids,
            receiver_ids,
            live_mask,
        )
        stored.append((ext_rows, features, pullback, weight_pair))
        features = result
    updated = features[None]
    cotangent = out_grad[0]
    send_parts = [None] * layer_total
    recv_parts = [None] * layer_total
    gain_parts = [None] * layer_total
    for layer_index in reversed(range(layer_total)):
        carried, own_rows, pullback, weight_pair = stored[layer_index]
        ext_grad, own_grad, send_term, recv_term, gain_term = pullback(cotangent)
        back_up = from_behind(ext_grad[own_count : own_count + halo_count], "graph", -1)
        back_down = from_behind(ext_grad[own_count + halo_count :], "graph", 1)
        merged = own_grad.astype(jnp.float32) + ext_grad[:own_count].astype(jnp.float32)
        merged = (
            merged.at[upper_ids]
            .add(back_up.astype(jnp.float32))
            .at[lower_ids]
            .add(back_down.astype(jnp.float32))
        )
        cotangent = merged.astype(jnp.bfloat16)
        gain_parts[layer_index] = gain_term
        send_parts[layer_index] = send_term
        recv_parts[layer_index] = recv_term
    feature_grad = cotangent[None]
    send_stack = jnp.stack(send_parts).astype(jnp.float32)
    recv_stack = jnp.stack(recv_parts).astype(jnp.float32)
    shares = (
        lax.psum_scatter(
            send_stack.astype(jnp.bfloat16), "fsdp", scatter_dimension=1, tiled=True
        ).astype(jnp.float32),
        lax.psum_scatter(
            recv_stack.astype(jnp.bfloat16), "fsdp", scatter_dimension=1, tiled=True
        ).astype(jnp.float32),
    )
    send_grad, recv_grad = lax.psum((shares[0], shares[1]), "graph")
    gain_grad = lax.psum(jnp.stack(gain_parts), ("graph", "fsdp"))
    return (
        updated,
        feature_grad,
        send_grad / loss_scale,
        recv_grad / loss_scale,
        gain_grad / loss_scale,
    )


def solution(mesh):
    in_specs = (
        P("fsdp", "graph", None),
        P("fsdp", "graph", None),
        P(None, "fsdp", None),
        P(None, "fsdp", None),
        P(),
        P("graph", None),
        P("graph", None),
        P("graph"),
        P("graph", None, None),
    )
    out_specs = (
        P("fsdp", "graph", None),
        P("fsdp", "graph", None),
        P(None, "fsdp", None),
        P(None, "fsdp", None),
        P(),
    )
    return jax.shard_map(shards, mesh=mesh, in_specs=in_specs, out_specs=out_specs, check_vma=False)
```

profile of v0, /device:TPU:1, one launch (start us, length us, event | category | flops | bytes accessed | tf_op | source)
XLA Modules:
  0.0 745.4 jit_solution(15699943627093834494)
XLA Ops:
  9.6 8.8 %collective-permute-start.1 = (bf16[8,512]{1,0:T(8,128)(2,1)S(1)}, bf16[8,512]{1,0:T(8,128)(2,1)S(1)}, u32[]{:S(2)}, u32[]{:S(2)}) collective-permute-start(bf16[8,512]{1,0:T(8,128)(2,1)S(1)} %broadcast_select_fusion.1), channel_id=1, source_target_pairs={{0,504},{8,0},{16,8},{24,16},{32,24},{40,32},{48,40},{56,48},{64,5... | collective-permute-start | bytes 24584 | tf_op jit(solution)/shard_map/ppermute | solution.py:13
  24.5 38.6 %all-gather.1 = bf16[1,512,512]{2,1,0:T(8,128)(2,1)S(1)} all-gather(bf16[1,64,512]{2,1,0:T(8,128)(2,1)S(1)} %get-tuple-element.42), channel_id=3, replica_groups=mesh['graph'=64,'fsdp'=8] {'fsdp'}, dimensions={1}, use_global_device_ids=true | all-gather | bytes 589824 | tf_op jit(solution)/shard_map/all_gather | solution.py:70
  64.1 39.3 %all-gather = bf16[1,512,512]{2,1,0:T(8,128)(2,1)S(1)} all-gather(bf16[1,64,512]{2,1,0:T(8,128)(2,1)S(1)} %get-tuple-element.40), channel_id=2, replica_groups=mesh['graph'=64,'fsdp'=8] {'fsdp'}, dimensions={1}, use_global_device_ids=true | all-gather | bytes 589824 | tf_op jit(solution)/shard_map/all_gather | solution.py:69
  104.1 38.5 %all-gather.3 = bf16[1,512,512]{2,1,0:T(8,128)(2,1)S(1)} all-gather(bf16[1,64,512]{2,1,0:T(8,128)(2,1)S(1)} %get-tuple-element.41), channel_id=5, replica_groups=mesh['graph'=64,'fsdp'=8] {'fsdp'}, dimensions={1}, use_global_device_ids=true | all-gather | bytes 589824 | tf_op jit(solution)/shard_map/all_gather | solution.py:70
  142.6 41.0 %all-gather.2 = bf16[1,512,512]{2,1,0:T(8,128)(2,1)} all-gather(bf16[1,64,512]{2,1,0:T(8,128)(2,1)S(1)} %get-tuple-element.39), channel_id=4, replica_groups=mesh['graph'=64,'fsdp'=8] {'fsdp'}, dimensions={1}, use_global_device_ids=true | all-gather | bytes 589824 | tf_op jit(solution)/shard_map/all_gather | solution.py:69
  187.7 4.1 scatter_custom_fusion
  194.4 30.3 %collective-permute-start.3 = (bf16[8,512]{1,0:T(8,128)(2,1)S(1)}, bf16[8,512]{1,0:T(8,128)(2,1)S(1)}, u32[]{:S(2)}, u32[]{:S(2)}) collective-permute-start(bf16[8,512]{1,0:T(8,128)(2,1)S(1)} %broadcast_select_fusion), channel_id=1, source_target_pairs={{0,504},{8,0},{16,8},{24,16},{32,24},{40,32},{48,40},{56,48},{64,5... | collective-permute-start | bytes 24584 | tf_op jit(solution)/shard_map/ppermute | solution.py:13
  230.1 2.3 gather_fusion.8
  232.4 4.9 scatter_custom_fusion.1
  241.0 2.5 gather_fusion
  244.2 2.8 fusion.11
  247.0 4.4 scatter_custom_fusion.2
  251.3 4.9 scatter_custom_fusion.3
  258.7 6.9 collective-permute-start.4
  265.7 2.1 collective-permute-start.5
  272.5 2.3 gather_fusion.1
  274.8 2.7 fusion.13
  277.5 4.4 scatter_custom_fusion.7
  284.4 4.3 scatter_custom_fusion.6
  291.5 7.4 collective-permute-start.6
  298.9 1.9 collective-permute-start.7
  301.5 103.6 %psum.23 = f32[2,512]{1,0:T(2,128)S(1)} all-reduce(f32[2,512]{1,0:T(2,128)S(1)} %pad_maximum_fusion.8), channel_id=1, replica_groups=mesh['graph'=64,'fsdp'=8] {'graph','fsdp'}, use_global_device_ids=true, to_apply=%region_20.24 | all-reduce | flops 1024 | bytes 8192 | tf_op jit(solution)/shard_map/psum | solution.py:120
  408.5 62.9 %reduce-scatter.5.cloned.1.call-done = bf16[2,64,512]{2,1,0:T(8,128)(2,1)} async-done(((bf16[2,512,512]{2,1,0:T(8,128)(2,1)}), bf16[2,64,512]{2,1,0:T(8,128)(2,1)}) %reduce-scatter.5.cloned.1.call-update) | async-done | bytes 131088 | tf_op jit(solution)/shard_map/reduce_scatter | solution.py:115
  471.3 265.8 %all-reduce.2 = (f32[2,64,512]{2,1,0:T(8,128)S(1)}, f32[2,64,512]{2,1,0:T(8,128)S(1)}) all-reduce(bf16[2,64,512]{2,1,0:T(8,128)(2,1)} %reduce-scatter.3.cloned.1.call-done, bf16[2,64,512]{2,1,0:T(8,128)(2,1)} %reduce-scatter.5.cloned.1.call-done), channel_id=1, replica_groups=mesh['graph'=64,'fsdp'=8] {'graph'}, use_global_device_ids=true, to_apply=%region_15.19 | all-reduce | flops 131072 | bytes 786432 | tf_op jit(solution)/shard_map/psum | solution.py:119
  (172 shorter events, 43.3 us)
Async XLA Ops:
  7.2 17.2 %copy-start.19 = (bf16[2,64,512]{2,1,0:T(8,128)(2,1)S(1)}, bf16[2,64,512]{2,1,0:T(8,128)(2,1)}, u32[]{:S(2)}) copy-start(bf16[2,64,512]{2,1,0:T(8,128)(2,1)} %param.18) | copy-start | bytes 393220
  7.2 401.3 %reduce-scatter.3.cloned.1.call-start = ((), (), s32[]{:S(2)}) async-start(), calls=%async_computation.2 | async-start | bytes 1179648 | tf_op jit(solution)/shard_map/reduce_scatter | solution.py:112
  9.6 175.7 %collective-permute-start.1 = (bf16[8,512]{1,0:T(8,128)(2,1)S(1)}, bf16[8,512]{1,0:T(8,128)(2,1)S(1)}, u32[]{:S(2)}, u32[]{:S(2)}) collective-permute-start(bf16[8,512]{1,0:T(8,128)(2,1)S(1)} %broadcast_select_fusion.1), channel_id=1, source_target_pairs={{0,504},{8,0},{16,8},{24,16},{32,24},{40,32},{48,40},{56,48},{64,5... | collective-permute-start | bytes 24584 | tf_op jit(solution)/shard_map/ppermute | solution.py:13
  19.9 165.3 %collective-permute-start = (bf16[8,512]{1,0:T(8,128)(2,1)S(1)}, bf16[8,512]{1,0:T(8,128)(2,1)S(1)}, u32[]{:S(2)}, u32[]{:S(2)}) collective-permute-start(bf16[8,512]{1,0:T(8,128)(2,1)S(1)} %broadcast_select_fusion.3), channel_id=1, source_target_pairs={{0,8},{8,16},{16,24},{24,32},{32,40},{40,48},{48,56},{56,64},{64,7... | collective-permute-start | bytes 24584 | tf_op jit(solution)/shard_map/ppermute | solution.py:13
  21.9 41.4 %copy-start.37 = (s32[512]{0:T(512)}, s32[512]{0:T(512)S(1)}, u32[]{:S(2)}) copy-start(s32[512]{0:T(512)S(1)} %compare_select_fusion) | copy-start | bytes 6148
  22.4 210.0 %copy-start.33 = (pred[512]{0:T(512)(128)(4,1)}, pred[512]{0:T(512)(128)(4,1)S(1)}, u32[]{:S(2)}) copy-start(pred[512]{0:T(512)(128)(4,1)S(1)} %get-tuple-element.46) | copy-start | bytes 1540
  24.4 159.2 %copy-start.38 = (s32[512]{0:T(512)}, s32[512]{0:T(512)S(1)}, u32[]{:S(2)}) copy-start(s32[512]{0:T(512)S(1)} %compare_select_fusion.1) | copy-start | bytes 6148
  24.4 208.0 %copy-start.30 = (pred[512]{0:T(512)(128)(4,1)}, pred[512]{0:T(512)(128)(4,1)S(1)}, u32[]{:S(2)}) copy-start(pred[512]{0:T(512)(128)(4,1)S(1)} %get-tuple-element.52) | copy-start | bytes 1540
  24.4 38.6 %copy-start.11 = (bf16[1,128,512]{2,1,0:T(8,128)(2,1)S(1)}, bf16[1,128,512]{2,1,0:T(8,128)(2,1)}, u32[]{:S(2)}) copy-start(bf16[1,128,512]{2,1,0:T(8,128)(2,1)} %param.15) | copy-start | bytes 393220
  64.1 39.3 %copy-start.45 = (f32[2,512]{1,0:T(2,128)S(1)}, f32[2,512]{1,0:T(2,128)}, u32[]{:S(2)}) copy-start(f32[2,512]{1,0:T(2,128)} %param.19) | copy-start | bytes 12292
  103.5 81.8 %copy-start.8 = (bf16[1,512,512]{2,1,0:T(8,128)(2,1)}, bf16[1,512,512]{2,1,0:T(8,128)(2,1)S(1)}, u32[]{:S(2)}) copy-start(bf16[1,512,512]{2,1,0:T(8,128)(2,1)S(1)} %all-gather) | copy-start | bytes 1572868
  142.6 84.2 %copy-start.6 = (bf16[1,512,512]{2,1,0:T(8,128)(2,1)}, bf16[1,512,512]{2,1,0:T(8,128)(2,1)S(1)}, u32[]{:S(2)}) copy-start(bf16[1,512,512]{2,1,0:T(8,128)(2,1)S(1)} %all-gather.3) | copy-start | bytes 1572868
  193.2 33.6 %copy-start.2 = (bf16[128,512]{1,0:T(8,128)(2,1)}, bf16[128,512]{1,0:T(8,128)(2,1)S(1)}, u32[]{:S(2)}) copy-start(bf16[128,512]{1,0:T(8,128)(2,1)S(1)} %add_convert_fusion.1) | copy-start | bytes 393220
  194.4 34.2 %collective-permute-start.3 = (bf16[8,512]{1,0:T(8,128)(2,1)S(1)}, bf16[8,512]{1,0:T(8,128)(2,1)S(1)}, u32[]{:S(2)}, u32[]{:S(2)}) collective-permute-start(bf16[8,512]{1,0:T(8,128)(2,1)S(1)} %broadcast_select_fusion), channel_id=1, source_target_pairs={{0,504},{8,0},{16,8},{24,16},{32,24},{40,32},{48,40},{56,48},{64,5... | collective-permute-start | bytes 24584 | tf_op jit(solution)/shard_map/ppermute | solution.py:13
  224.8 3.8 collective-permute-start.2
  257.6 10.1 %copy-start.14 = (f32[144,512]{1,0:T(8,128)S(1)}, f32[144,512]{1,0:T(8,128)}, u32[]{:S(2)}) copy-start(f32[144,512]{1,0:T(8,128)} %scatter_custom_fusion.3) | copy-start | bytes 884740
  257.7 10.1 %copy-start.24 = (bf16[8,512]{1,0:T(8,128)(2,1)S(1)}, bf16[8,512]{1,0:T(8,128)(2,1)}, u32[]{:S(2)}) copy-start(bf16[8,512]{1,0:T(8,128)(2,1)} %copy-done.23) | copy-start | bytes 24580
  257.7 10.1 %copy-start.26 = (bf16[8,512]{1,0:T(8,128)(2,1)S(1)}, bf16[8,512]{1,0:T(8,128)(2,1)}, u32[]{:S(2)}) copy-start(bf16[8,512]{1,0:T(8,128)(2,1)} %copy-done.25) | copy-start | bytes 24580
  258.7 10.2 %collective-permute-start.4 = (bf16[8,512]{1,0:T(8,128)(2,1)S(1)}, bf16[8,512]{1,0:T(8,128)(2,1)S(1)}, u32[]{:S(2)}, u32[]{:S(2)}) collective-permute-start(bf16[8,512]{1,0:T(8,128)(2,1)S(1)} %get-tuple-element.38), channel_id=1, source_target_pairs={{0,504},{8,0},{16,8},{24,16},{32,24},{40,32},{48,40},{56,48},{64,5... | collective-permute-start | bytes 24584 | tf_op jit(solution)/shard_map/ppermute | solution.py:13
  265.7 4.1 collective-permute-start.5
  284.0 187.3 %reduce-scatter.5.cloned.1.call-start = ((), (), s32[]{:S(2)}) async-start(), calls=%async_computation.3 | async-start | bytes 1179648 | tf_op jit(solution)/shard_map/reduce_scatter | solution.py:115
  291.2 113.9 %copy-start.5 = (bf16[1,512,512]{2,1,0:T(8,128)(2,1)S(1)}, bf16[1,512,512]{2,1,0:T(8,128)(2,1)}, u32[]{:S(2)}) copy-start(bf16[1,512,512]{2,1,0:T(8,128)(2,1)} %copy-done.4) | copy-start | bytes 1572868
  291.5 114.5 %collective-permute-start.6 = (bf16[8,512]{1,0:T(8,128)(2,1)S(1)}, bf16[8,512]{1,0:T(8,128)(2,1)S(1)}, u32[]{:S(2)}, u32[]{:S(2)}) collective-permute-start(bf16[8,512]{1,0:T(8,128)(2,1)S(1)} %get-tuple-element.36), channel_id=1, source_target_pairs={{0,504},{8,0},{16,8},{24,16},{32,24},{40,32},{48,40},{56,48},{64,5... | collective-permute-start | bytes 24584 | tf_op jit(solution)/shard_map/ppermute | solution.py:13
  298.9 108.0 %collective-permute-start.7 = (bf16[8,512]{1,0:T(8,128)(2,1)S(1)}, bf16[8,512]{1,0:T(8,128)(2,1)S(1)}, u32[]{:S(2)}, u32[]{:S(2)}) collective-permute-start(bf16[8,512]{1,0:T(8,128)(2,1)S(1)} %get-tuple-element.35), channel_id=1, source_target_pairs={{0,8},{8,16},{16,24},{24,32},{32,40},{40,48},{48,56},{56,64},{64,7... | collective-permute-start | bytes 24584 | tf_op jit(solution)/shard_map/ppermute | solution.py:13
  (34 other events, 56.1 us)
Sparse Core Ops, SparseCore 0:
  284.1 93.3 reduce-scatter.2
  382.7 88.6 reduce-scatter.4
where the time goes:
time: 751 us; the launch traced here: 745 us
  blocking collectives  527 us (70%)
  waiting for transfers between devices  62.9 us (8%)
  starting transfers between devices  61.3 us (8%)
  other arithmetic  47 us (6%)
  local copies, waits for them, and re-layouts  24.8 us (3%)
  between operations  15.5 us (2%)
    psum x1, blocking collectives, shards(): send_grad, recv_grad = lax.psum((shares[0], shares[1]), 'graph')  266 us
    psum x1, blocking collectives, shards(): gain_grad = lax.psum(jnp.stack(gain_parts), ('graph', 'fsdp'))  104 us
    all_gather x2, blocking collectives, shards(): lax.all_gather(send_weight[layer_index], 'fsdp', axis=0, tiled=True)  80.3 us
    all_gather x2, blocking collectives, shards(): lax.all_gather(recv_weight[layer_index], 'fsdp', axis=0, tiled=True)  77.1 us
    reduce_scatter x1, waiting for transfers between devices, shards(): lax.psum_scatter(recv_stack.astype(jnp.bfloat16), 'fsdp', scatter_dimensi...  62.9 us
    ppermute x8, starting transfers between devices, from_behind(): return lax.ppermute(value, axis, pairs)  61.2 us
  transfers between devices with their start and end apart: 10, of which 1 were waited for; matrix products, arithmetic and copies ran while one was open for 3% of the time, Pallas kernels for 0%

commit v1 on v0

v1 whole, which is shorter than its diff:
```python
import functools

import jax
import jax.numpy as jnp
from jax import lax
from jax.experimental import pallas as pl
from jax.experimental.pallas import tpu as pltpu
from jax.sharding import Mesh
from jax.sharding import PartitionSpec as P

EPSILON = 1e-05
LOSS_SCALE = 512.0

D = 512
N = 128
H = 16
E = 512
EXT = N + 2 * H
ROWS = EXT + N
HALF = D // 2
DROWS = ROWS + 16
CHUNK_LANES = 4 * HALF + 128

BF = jnp.bfloat16
F32 = jnp.float32
VMEM = pl.BlockSpec(memory_space=pltpu.VMEM)
SMEM = pl.BlockSpec(memory_space=pltpu.SMEM)


def dot(a, b):
    return jnp.dot(a, b, preferred_element_type=F32)


def dot_tn(a, b):
    return lax.dot_general(a, b, (((0,), (0,)), ((), ())), preferred_element_type=F32)


def dot_nt(a, b):
    return lax.dot_general(a, b, (((1,), (1,)), ((), ())), preferred_element_type=F32)


def split(value):
    high = value.astype(BF)
    return high, (value - high.astype(F32)).astype(BF)


def call(kernel, outs, name, *args, flops=1e8):
    specs = [SMEM if a.dtype == jnp.int32 and a.size <= 2 else VMEM for a in args]
    return pl.pallas_call(
        kernel,
        out_shape=[jax.ShapeDtypeStruct(s, t) for s, t in outs],
        in_specs=specs,
        out_specs=[VMEM] * len(outs),
        compiler_params=pltpu.CompilerParams(vmem_limit_bytes=40 * 1024 * 1024),
        cost_estimate=pl.CostEstimate(flops=int(flops), bytes_accessed=2000000, transcendentals=0),
        name=name,
    )(*args)


def send_matrix_of(send_rows_ref):
    rows = lax.broadcasted_iota(jnp.int32, (N, H), 0)
    return (rows == send_rows_ref[...]).astype(F32).astype(BF)


def prepare_kernel(count, senders, receivers, send_rows, rows, by_row, by_edge, sent):
    live = lax.broadcasted_iota(jnp.int32, (1, E), 1) < count[0, 0]
    ids = senders[...]
    ids = jnp.where(ids >= N + H // 2, ids + H, ids)
    ids = jnp.where(live, ids, -1)
    receiver_ids = jnp.where(live, receivers[...], -1)
    row = lax.broadcasted_iota(jnp.int32, (EXT, E), 0)
    by_row[0:EXT, :] = (row == ids).astype(F32).astype(BF)
    row = lax.broadcasted_iota(jnp.int32, (N, E), 0)
    by_row[EXT:ROWS, :] = (row == receiver_ids).astype(F32).astype(BF)
    ids_down = jnp.broadcast_to(ids, (N, E)).T
    receivers_down = jnp.broadcast_to(receiver_ids, (N, E)).T
    lane = lax.broadcasted_iota(jnp.int32, (E, N), 1)
    by_edge[0] = (lane == ids_down).astype(F32).astype(BF)
    by_edge[1] = (lane == receivers_down).astype(F32).astype(BF)
    by_edge[2] = (lane == ids_down - N).astype(F32).astype(BF)
    sent[...] = dot_tn(send_matrix_of(send_rows), rows[...]).astype(BF)


def weights_of(core, own, peer):
    def whole(ref):
        return jnp.concatenate([ref[x, z] for z in range(2) for x in range(4)], axis=0)

    first, second = whole(own), whole(peer)
    is_first = core[0, 0] == 0
    return jnp.where(is_first, first, second), jnp.where(is_first, second, first)


def forward(rows, from_prev, from_next, send_matrix, recv_matrix, by_row, by_edge):
    ext = jnp.concatenate([rows, from_prev, from_next], axis=0)
    proj_send = dot(ext, send_matrix)
    proj_recv = dot(rows, recv_matrix)
    send_high, send_low = split(proj_send)
    recv_high, recv_low = split(proj_recv)
    halo = jnp.concatenate(
        [send_high[N:], send_low[N:], jnp.zeros((N - 4 * H, D), BF)], axis=0
    )
    halo_edges = by_edge[2]
    halo_edges = jnp.concatenate(
        [halo_edges[:, : 2 * H], halo_edges[:, : 2 * H], halo_edges[:, 4 * H :]], axis=1
    )
    edges = jnp.concatenate([by_edge[0], by_edge[1]], axis=1)
    own_high = jnp.concatenate([send_high[:N], recv_high], axis=0)
    own_low = jnp.concatenate([send_low[:N], recv_low], axis=0)
    preact = dot(edges, own_high) + dot(edges, own_low) + dot(halo_edges, halo)
    sigmoid = 1.0 / (1.0 + jnp.exp(-preact))
    message = preact * sigmoid
    slope = sigmoid * (1.0 + preact * (1.0 - sigmoid))
    high, low = split(message)
    receive = by_row[EXT:ROWS, :]
    return dot(receive, high) + dot(receive, low), slope


def factor_of(total):
    return lax.rsqrt(jnp.mean(total * total, axis=-1, keepdims=True) + EPSILON)


def backward(cotangent, total, slope, gain_row, send_matrix, recv_matrix, by_row, by_edge):
    factor = factor_of(total)
    normal = total * factor
    gain_term = jnp.sum(cotangent * normal, axis=0, keepdims=True)
    scaled = cotangent * gain_row
    inner = jnp.mean(scaled * normal, axis=-1, keepdims=True)
    total_grad = (scaled - normal * inner) * factor
    high, low = split(total_grad)
    receive = by_edge[1]
    preact_grad = ((dot(receive, high) + dot(receive, low)) * slope).astype(BF)
    row_grad = dot(by_row[...], preact_grad).astype(BF)
    send_rows_grad, recv_rows_grad = row_grad[:EXT], row_grad[EXT:]
    ext_grad = dot_nt(send_rows_grad, send_matrix)
    own_grad = dot_nt(recv_rows_grad, recv_matrix) + ext_grad[:N]
    halo_grad = ext_grad[N:].astype(BF)
    gain_block = jnp.concatenate([gain_term, jnp.zeros((15, D), F32)], axis=0).astype(BF)
    return own_grad, halo_grad[:H], halo_grad[H:], row_grad, gain_block


def halves(core, value):
    is_first = core[0, 0] == 0
    left, right = value[:, :HALF], value[:, HALF:]
    return jnp.where(is_first, left, right), jnp.where(is_first, right, left)


def first_layer_kernel(
    core, rows, from_prev, from_next, own, peer, gain, by_row, by_edge, send_rows,
    result, total_out, slope_out, sent,
):
    send_matrix, recv_matrix = weights_of(core, own, peer)
    total, slope = forward(
        rows[...], from_prev[...], from_next[...], send_matrix, recv_matrix, by_row, by_edge
    )
    total_out[...] = total
    slope_out[...] = slope
    new = (rows[...].astype(F32) + gain[0:1, :] * total * factor_of(total)).astype(BF)
    result[...] = new
    sent[...] = dot_tn(send_matrix_of(send_rows), new).astype(BF)


def last_layer_kernel(
    core, rows, from_prev, from_next, own, peer, gain, by_row, by_edge, out_grad,
    result, own_grad, to_prev, to_next, keep, give,
):
    send_matrix, recv_matrix = weights_of(core, own, peer)
    total, slope = forward(
        rows[...], from_prev[...], from_next[...], send_matrix, recv_matrix, by_row, by_edge
    )
    gain_row = gain[1:2, :]
    result[...] = (rows[...].astype(F32) + gain_row * total * factor_of(total)).astype(BF)
    cotangent = out_grad[...].astype(F32)
    grad, prev_grad, next_grad, row_grad, gain_block = backward(
        cotangent, total, slope, gain_row, send_matrix, recv_matrix, by_row, by_edge
    )
    own_grad[...] = grad + cotangent
    to_prev[...] = prev_grad
    to_next[...] = next_grad
    keep[0:ROWS, :], give[0:ROWS, :] = halves(core, row_grad)
    keep[ROWS:DROWS, :], give[ROWS:DROWS, :] = halves(core, gain_block)


def merged(own_grad, from_next, from_prev, send_rows):
    back = (from_next[...].astype(F32) + from_prev[...].astype(F32)).astype(BF)
    return (own_grad[...] + dot(send_matrix_of(send_rows), back)).astype(BF)


def back_kernel(
    core, later_grad, back_next, back_prev, total, slope, own, peer, gain, by_row, by_edge, send_rows,
    rows_0, prev_0, next_0, rows_1, prev_1, next_1, later_keep, later_give,
    own_grad, to_prev, to_next, keep, pack,
):
    send_matrix, recv_matrix = weights_of(core, own, peer)
    cotangent = merged(later_grad, back_next, back_prev, send_rows).astype(F32)
    grad, prev_grad, next_grad, row_grad, gain_block = backward(
        cotangent, total[...], slope[...], gain[0:1, :], send_matrix, recv_matrix, by_row, by_edge
    )
    own_grad[...] = grad + cotangent
    to_prev[...] = prev_grad
    to_next[...] = next_grad
    base = 2 * EXT
    keep_rows, give_rows = halves(core, row_grad)
    keep_gain, give_gain = halves(core, gain_block)
    keep[0:ROWS, 0:HALF] = keep_rows
    keep[ROWS:DROWS, 0:HALF] = keep_gain
    keep[:, HALF:D] = later_keep[...]
    pack[base : base + ROWS, 0:HALF] = give_rows
    pack[base + ROWS : base + DROWS, 0:HALF] = give_gain
    pack[base : base + DROWS, HALF:D] = later_give[...]
    for layer, parts in enumerate(((rows_0, prev_0, next_0), (rows_1, prev_1, next_1))):
        start = layer * EXT
        pack[start : start + N, :] = parts[0][...]
        pack[start + N : start + N + H, :] = parts[1][...]
        pack[start + N + H : start + EXT, :] = parts[2][...]


def merge_kernel(own_grad, back_next, back_prev, send_rows, result):
    result[...] = merged(own_grad, back_next, back_prev, send_rows)


def terms_kernel(pack, keep, peer, chunks):
    base = 2 * EXT
    gains = []
    for layer in range(2):
        lanes = slice(layer * HALF, (layer + 1) * HALF)
        mine = pack[layer * EXT : (layer + 1) * EXT, :]
        theirs = peer[layer * EXT : (layer + 1) * EXT, :]
        for kind in range(2):
            if kind == 0:
                left = jnp.concatenate([mine, theirs], axis=0)
                right = jnp.concatenate([keep[0:EXT, lanes], peer[base : base + EXT, lanes]], axis=0)
            else:
                left = jnp.concatenate([mine[:N], theirs[:N]], axis=0)
                right = jnp.concatenate(
                    [keep[EXT:ROWS, lanes], peer[base + EXT : base + ROWS, lanes]], axis=0
                )
            term = dot_tn(left, right).astype(BF)
            for block in range(8):
                for part in range(4):
                    start = block * 64 + part * 16
                    chunks[block, 2 * kind + layer, :, part * HALF : (part + 1) * HALF] = term[
                        start : start + 16
                    ]
        gain = keep[ROWS:DROWS, lanes].astype(F32) + peer[base + ROWS : base + DROWS, lanes].astype(F32)
        gains += [gain[0:1, :128], gain[0:1, 128:]]
    block = jnp.concatenate(gains + [jnp.zeros((12, 128), F32)], axis=0).astype(BF)
    for first in range(8):
        for second in range(4):
            chunks[first, second, :, 4 * HALF :] = block


def first_sum_kernel(parts, copies):
    total = parts[0].astype(F32)
    for source in range(1, 32):
        total = total + parts[source].astype(F32)
    total = total.astype(BF)
    for target in range(32):
        copies[target] = total


def second_sum_kernel(parts, result):
    for place in range(4):
        total = parts[place].astype(F32)
        for source in range(1, 8):
            total = total + parts[4 * source + place].astype(F32)
        result[place] = total.astype(BF)


def spread_kernel(core, own, peer, send_grad, recv_grad, gain_grad):
    is_first = core[0, 0] == 0
    scale = 1.0 / LOSS_SCALE
    mine, theirs = own[...].astype(F32) * scale, peer[...].astype(F32) * scale
    sides = (jnp.where(is_first, mine, theirs), jnp.where(is_first, theirs, mine))
    for side, value in enumerate(sides):
        for matrix in range(4):
            out = (send_grad, recv_grad)[matrix // 2]
            for part in range(4):
                out[matrix % 2, part * 16 : part * 16 + 16, side * HALF : (side + 1) * HALF] = value[
                    matrix, :, part * HALF : (part + 1) * HALF
                ]
        for layer in range(2):
            for half in range(2):
                start = side * HALF + half * 128
                row = layer * 2 + half
                gain_grad[layer : layer + 1, start : start + 128] = value[0, row : row + 1, 4 * HALF :]


GRAPH = ("y", "zl", "c")


def shift(value, steps):
    return lax.ppermute(value, GRAPH, [(i, (i + steps) % 64) for i in range(64)])


def swap(value, axis):
    return lax.ppermute(value, axis, [(0, 1), (1, 0)])


def shards(
    node_features, out_grad, send_weight, recv_weight, gain, senders, receivers, edge_count, send_rows
):
    core = lax.axis_index("c").astype(jnp.int32).reshape(1, 1)
    features = node_features[0]
    targets = send_rows.reshape(1, H)
    half = jnp.where(lax.axis_index("c") == 0, send_weight, recv_weight)
    other = swap(half, "zh")
    by_row, by_edge, sent_0 = call(
        prepare_kernel,
        [((ROWS, E), BF), ((3, E, N), BF), ((H, D), BF)],
        "prepare",
        edge_count.reshape(1, 1), senders, receivers, targets, features,
    )
    prev_0, next_0 = shift(sent_0, 1), shift(sent_0, -1)
    is_low = lax.axis_index("zh") == 0
    both = jnp.stack([jnp.where(is_low, half, other), jnp.where(is_low, other, half)], axis=1)
    copies = jnp.broadcast_to(both[None], (4,) + both.shape)
    gathered = lax.all_to_all(copies, ("x",), 0, 0, tiled=True)
    own = [gathered[:, layer] for layer in range(2)]
    peer = [swap(value, "c") for value in own]

    rows_1, total_0, slope_0, sent_1 = call(
        first_layer_kernel,
        [((N, D), BF), ((N, D), F32), ((E, D), F32), ((H, D), BF)],
        "first_layer",
        core, features, prev_0, next_0, own[0], peer[0], gain, by_row, by_edge, targets,
    )
    prev_1, next_1 = shift(sent_1, 1), shift(sent_1, -1)
    updated, grad_1, to_prev, to_next, keep_1, give_1 = call(
        last_layer_kernel,
        [((N, D), BF), ((N, D), F32), ((H, D), BF), ((H, D), BF), ((DROWS, HALF), BF), ((DROWS, HALF), BF)],
        "last_layer",
        core, rows_1, prev_1, next_1, own[1], peer[1], gain, by_row, by_edge, out_grad[0],
    )
    back_next, back_prev = shift(to_prev, -1), shift(to_next, 1)
    grad_0, to_prev, to_next, keep, pack = call(
        back_kernel,
        [((N, D), F32), ((H, D), BF), ((H, D), BF), ((DROWS, D), BF), ((2 * EXT + DROWS, D), BF)],
        "back",
        core, grad_1, back_next, back_prev, total_0, slope_0, own[0], peer[0], gain, by_row, by_edge,
        targets, features, prev_0, next_0, rows_1, prev_1, next_1, keep_1, give_1,
    )
    peer_pack = swap(pack, "c")
    back_next, back_prev = shift(to_prev, -1), shift(to_next, 1)
    (chunks,) = call(terms_kernel, [((8, 4, 16, CHUNK_LANES), BF)], "terms", pack, keep, peer_pack)
    chunks = chunks.reshape(32, 16, CHUNK_LANES)
    parts = lax.all_to_all(chunks, ("zh", "x", "zl"), 0, 0, tiled=True)
    (copies,) = call(first_sum_kernel, [((32, 16, CHUNK_LANES), BF)], "first_sum", parts)
    parts = lax.all_to_all(copies, ("y", "zl"), 0, 0, tiled=True)
    (mine,) = call(second_sum_kernel, [((4, 16, CHUNK_LANES), BF)], "second_sum", parts)
    theirs = swap(mine, "c")
    send_grad, recv_grad, gain_grad = call(
        spread_kernel, [((2, 64, D), F32), ((2, 64, D), F32), ((2, D), F32)], "spread", core, mine, theirs
    )
    (feature_grad,) = call(merge_kernel, [((N, D), BF)], "merge", grad_0, back_next, back_prev, targets)
    return updated[None], feature_grad[None], send_grad, recv_grad, gain_grad


def solution(mesh):
    graph, fsdp = GRAPH, ("zh", "x")
    wide = Mesh(mesh.devices.reshape(8, 4, 2, 2, 4), GRAPH + fsdp)
    in_specs = (
        P(fsdp, graph, None),
        P(fsdp, graph, None),
        P(None, fsdp, None),
        P(None, fsdp, None),
        P(),
        P(graph, None),
        P(graph, None),
        P(graph),
        P(graph, None, None),
    )
    out_specs = (
        P(fsdp, graph, None),
        P(fsdp, graph, None),
        P(None, fsdp, None),
        P(None, fsdp, None),
        P(),
    )
    return jax.shard_map(shards, mesh=wide, in_specs=in_specs, out_specs=out_specs, check_vma=False)
```

time: 751 us -> 183 us (0.24)
  blocking collectives: 527 us -> 92.3 us
  waiting for transfers between devices: 62.9 us -> 11.3 us
  other arithmetic: 47 us -> 0.98 us
  local copies, waits for them, and re-layouts: 24.8 us -> 0.31 us
  between operations: 15.5 us -> 1.53 us
  Pallas kernels: 0 us -> 8.84 us
    psum x2 -> x0, blocking collectives: 369 us -> none  [the longest x1 266 us: shards(): send_grad, recv_grad = lax.psum((shares[0], shares[1]), 'graph')]
    all_gather x4 -> x0, blocking collectives: 157 us -> none  [the longest x2 80.3 us: shards(): lax.all_gather(send_weight[layer_index], 'fsdp', axis=0, tiled=True)]
    all_to_all x0 -> x3, blocking collectives: none -> 92.3 us  [the longest x1 39.4 us: shards(): parts = lax.all_to_all(chunks, ('zh', 'x', 'zl'), 0, 0, tiled=True)]
    reduce_scatter x2 -> x0, waiting for transfers between devices: 62.9 us -> none  [the longest x1 62.9 us: shards(): lax.psum_scatter(recv_stack.astype(jnp.bfloat16), 'fsdp', scatter_dimensi...]
    scatter-add x10 -> x0, other arithmetic: 30.8 us -> none  [the longest x2 9.27 us: layer_tail(): jnp.take(proj_send, sender_ids, axis=0)]
    gather x10 -> x0, local copies, waits for them, and re-layouts: 16.1 us -> none  [the longest x2 4.81 us: layer_tail(): jax.ops.segment_sum(message, receiver_ids, num_segments=own_rows.shape[0])]
    ppermute x8 -> x13, waiting for transfers between devices: 0.02 us -> 11.3 us  [the longest x8 5.68 us: shift(): lax.ppermute(value, GRAPH, [(i, (i + steps) % 64) for i in range(64)])]
    pallas_call x0 -> x9, Pallas kernels: none -> 8.84 us  [call(): pl.pallas_call(kernel, out_shape=[jax.ShapeDtypeStruct(s, t) for s, t in...]
  transfers between devices with their start and end apart: 10 -> 13, of which waited for: 1 -> 6; matrix products, arithmetic and copies ran while one was open for 3% -> 0% of each run, Pallas kernels for 0% -> 2%
where the time goes in v1:
time: 183 us; the launch traced here: 180 us
  blocking collectives  92.3 us (50%)
  starting transfers between devices  64.5 us (35%)
  waiting for transfers between devices  11.3 us (6%)
  Pallas kernels  8.84 us (5%)
    all_to_all x1, blocking collectives, shards(): parts = lax.all_to_all(chunks, ('zh', 'x', 'zl'), 0, 0, tiled=True)  39.4 us
    all_to_all x1, blocking collectives, shards(): parts = lax.all_to_all(copies, ('y', 'zl'), 0, 0, tiled=True)  36.2 us
    ppermute x8, starting transfers between devices, shift(): lax.ppermute(value, GRAPH, [(i, (i + steps) % 64) for i in range(64)])  33.7 us
    ppermute x5, starting transfers between devices, swap(): return lax.ppermute(value, axis, [(0, 1), (1, 0)])  30.8 us
    all_to_all x1, blocking collectives, shards(): gathered = lax.all_to_all(copies, ('x',), 0, 0, tiled=True)  16.6 us
    pallas_call x9, Pallas kernels, call(): pl.pallas_call(kernel, out_shape=[jax.ShapeDtypeStruct(s, t) for s, t in...  8.84 us
    ppermute x8, waiting for transfers between devices, shift(): lax.ppermute(value, GRAPH, [(i, (i + steps) % 64) for i in range(64)])  5.68 us
    ppermute x5, waiting for transfers between devices, swap(): return lax.ppermute(value, axis, [(0, 1), (1, 0)])  5.57 us
  transfers between devices with their start and end apart: 13, of which 6 were waited for; matrix products, arithmetic and copies ran while one was open for 0% of the time, Pallas kernels for 2%

profile of v1, /device:TPU:1, one launch (start us, length us, event | category | flops | bytes accessed | tf_op | source)
XLA Modules:
  0.0 179.7 jit_solution(3433640117286236031)
XLA Ops:
  1.6 11.5 %collective-permute-start.2 = (bf16[2,64,512]{2,1,0:T(8,128)(2,1)S(1)}, bf16[2,64,512]{2,1,0:T(8,128)(2,1)S(1)}, u32[]{:S(2)}, u32[]{:S(2)}) collective-permute-start(bf16[2,64,512]{2,1,0:T(8,128)(2,1)S(1)} %broadcast_select_fusion), channel_id=1, source_target_pairs={{0,4},{4,0},{1,5},{5,1},{2,6},{6,2},{3,7},{7,3},{8,12},{12,8},{9,1... | collective-permute-start | bytes 393224 | tf_op jit(solution)/shard_map/ppermute | solution.py:296
  13.1 3.9 %collective-permute-done.2 = bf16[2,64,512]{2,1,0:T(8,128)(2,1)S(1)} collective-permute-done((bf16[2,64,512]{2,1,0:T(8,128)(2,1)S(1)}, bf16[2,64,512]{2,1,0:T(8,128)(2,1)S(1)}, u32[]{:S(2)}, u32[]{:S(2)}) %collective-permute-start.2) | collective-permute-done | bytes 131104 | tf_op jit(solution)/shard_map/ppermute | solution.py:296
  17.1 16.6 %all_to_all.15 = bf16[4,2,2,64,512]{4,3,2,1,0:T(8,128)(2,1)S(1)} all-to-all(bf16[4,2,2,64,512]{4,3,2,1,0:T(8,128)(2,1)S(1)} %broadcast_in_dim.12), channel_id=1, replica_groups=mesh['y'=8,'zl'=4,'c'=2,'zh'=2,'x'=4] {'x'}, dimensions={0} | all-to-all | bytes 2097152 | tf_op jit(solution)/shard_map/all_to_all | solution.py:317
  33.8 4.6 %collective-permute-start.3 = (bf16[4,2,64,512]{3,2,1,0:T(8,128)(2,1)S(1)}, bf16[4,2,64,512]{3,2,1,0:T(8,128)(2,1)S(1)}, u32[]{:S(2)}, u32[]{:S(2)}) collective-permute-start(bf16[4,2,64,512]{3,2,1,0:T(8,128)(2,1)S(1)} %get-tuple-element.48.own), channel_id=1, source_target_pairs={{0,8},{8,0},{1,9},{9,1},{2,10},{10,2},{3,11},{11,3},{4,12},{12,4},... | collective-permute-start | bytes 1572872 | tf_op jit(solution)/shard_map/ppermute | solution.py:296
  38.5 1.9 %collective-permute-start.6 = (bf16[4,2,64,512]{3,2,1,0:T(8,128)(2,1)S(1)}, bf16[4,2,64,512]{3,2,1,0:T(8,128)(2,1)S(1)}, u32[]{:S(2)}, u32[]{:S(2)}) collective-permute-start(bf16[4,2,64,512]{3,2,1,0:T(8,128)(2,1)S(1)} %get-tuple-element.47.own), channel_id=1, source_target_pairs={{0,8},{8,0},{1,9},{9,1},{2,10},{10,2},{3,11},{11,3},{4,12},{12,4},... | collective-permute-start | bytes 1572872 | tf_op jit(solution)/shard_map/ppermute | solution.py:296
  41.4 2.4 %collective-permute-start.1 = (bf16[16,512]{1,0:T(8,128)(2,1)S(1)}, bf16[16,512]{1,0:T(8,128)(2,1)S(1)}, u32[]{:S(2)}, u32[]{:S(2)}) collective-permute-start(bf16[16,512]{1,0:T(8,128)(2,1)S(1)} %get-tuple-element.26), channel_id=1, source_target_pairs={{0,504},{8,0},{16,8},{24,16},{32,24},{40,32},{48,40},{56,48},{64,5... | collective-permute-start | bytes 49160 | tf_op jit(solution)/shard_map/ppermute | solution.py:292
  43.8 5.8 %collective-permute-start = (bf16[16,512]{1,0:T(8,128)(2,1)S(1)}, bf16[16,512]{1,0:T(8,128)(2,1)S(1)}, u32[]{:S(2)}, u32[]{:S(2)}) collective-permute-start(bf16[16,512]{1,0:T(8,128)(2,1)S(1)} %get-tuple-element.26), channel_id=1, source_target_pairs={{0,8},{8,16},{16,24},{24,32},{32,40},{40,48},{48,56},{56,64},{64,7... | collective-permute-start | bytes 49160 | tf_op jit(solution)/shard_map/ppermute | solution.py:292
  49.7 2.6 %collective-permute-done.from_prev.prev_0 = bf16[16,512]{1,0:T(8,128)(2,1)S(1)} collective-permute-done((bf16[16,512]{1,0:T(8,128)(2,1)S(1)}, bf16[16,512]{1,0:T(8,128)(2,1)S(1)}, u32[]{:S(2)}, u32[]{:S(2)}) %collective-permute-start) | collective-permute-done | bytes 16416 | tf_op jit(solution)/shard_map/ppermute | solution.py:292
  52.2 1.7 first_layer.1
  53.9 8.3 %collective-permute-start.5 = (bf16[16,512]{1,0:T(8,128)(2,1)S(1)}, bf16[16,512]{1,0:T(8,128)(2,1)S(1)}, u32[]{:S(2)}, u32[]{:S(2)}) collective-permute-start(bf16[16,512]{1,0:T(8,128)(2,1)S(1)} %get-tuple-element.30), channel_id=1, source_target_pairs={{0,504},{8,0},{16,8},{24,16},{32,24},{40,32},{48,40},{56,48},{64,5... | collective-permute-start | bytes 49160 | tf_op jit(solution)/shard_map/ppermute | solution.py:292
  62.2 1.9 %collective-permute-start.4 = (bf16[16,512]{1,0:T(8,128)(2,1)S(1)}, bf16[16,512]{1,0:T(8,128)(2,1)S(1)}, u32[]{:S(2)}, u32[]{:S(2)}) collective-permute-start(bf16[16,512]{1,0:T(8,128)(2,1)S(1)} %get-tuple-element.30), channel_id=1, source_target_pairs={{0,8},{8,16},{16,24},{24,32},{32,40},{40,48},{48,56},{56,64},{64,7... | collective-permute-start | bytes 49160 | tf_op jit(solution)/shard_map/ppermute | solution.py:292
  64.1 1.1 collective-permute-done.4.from_prev.prev_1
  65.3 3.0 %last_layer.1 = (bf16[128,512]{1,0:T(8,128)(2,1)}, f32[128,512]{1,0:T(8,128)S(1)}, bf16[16,512]{1,0:T(8,128)(2,1)S(1)}, bf16[16,512]{1,0:T(8,128)(2,1)S(1)}, bf1...) custom-call(s32[1,1]{1,0:T(1,128)} %bitcast.core, bf16[128,512]{1,0:T(8,128)(2,1)S(1)} %get-tuple-element.29.rows.rows_1, ...), custom_call_target="tpu_custom_call" | custom-call | flops 100000000 | bytes 2000000 | tf_op jit(solution)/shard_map/last_layer/pallas_call | solution.py:49
  68.3 7.8 %collective-permute-start.7 = (bf16[16,512]{1,0:T(8,128)(2,1)S(1)}, bf16[16,512]{1,0:T(8,128)(2,1)S(1)}, u32[]{:S(2)}, u32[]{:S(2)}) collective-permute-start(bf16[16,512]{1,0:T(8,128)(2,1)S(1)} %get-tuple-element.33), channel_id=1, source_target_pairs={{0,504},{8,0},{16,8},{24,16},{32,24},{40,32},{48,40},{56,48},{64,5... | collective-permute-start | bytes 49160 | tf_op jit(solution)/shard_map/ppermute | solution.py:292
  76.1 1.9 %collective-permute-start.8 = (bf16[16,512]{1,0:T(8,128)(2,1)S(1)}, bf16[16,512]{1,0:T(8,128)(2,1)S(1)}, u32[]{:S(2)}, u32[]{:S(2)}) collective-permute-start(bf16[16,512]{1,0:T(8,128)(2,1)S(1)} %get-tuple-element.34), channel_id=1, source_target_pairs={{0,8},{8,16},{16,24},{24,32},{32,40},{40,48},{48,56},{56,64},{64,7... | collective-permute-start | bytes 49160 | tf_op jit(solution)/shard_map/ppermute | solution.py:292
  78.0 1.1 collective-permute-done.8.back_prev
  79.2 1.3 back.1
  80.5 7.8 %collective-permute-start.11 = (bf16[624,512]{1,0:T(8,128)(2,1)S(1)}, bf16[624,512]{1,0:T(8,128)(2,1)S(1)}, u32[]{:S(2)}, u32[]{:S(2)}) collective-permute-start(bf16[624,512]{1,0:T(8,128)(2,1)S(1)} %get-tuple-element.42.pack), channel_id=1, source_target_pairs={{0,8},{8,0},{1,9},{9,1},{2,10},{10,2},{3,11},{11,3},{4,12},{12,4},... | collective-permute-start | bytes 1916936 | tf_op jit(solution)/shard_map/ppermute | solution.py:296
  88.3 1.7 collective-permute-done.11.peer
  90.6 39.4 %all_to_all.16.parts = bf16[32,16,1152]{2,1,0:T(8,128)(2,1)S(1)} all-to-all(bf16[32,16,1152]{2,1,0:T(8,128)(2,1)S(1)} %bitcast.20), channel_id=1, replica_groups=mesh['y'=8,'zl'=4,'c'=2,'zh'=2,'x'=4] {'zh','x','zl'}, dimensions={0} | all-to-all | bytes 2359296 | tf_op jit(solution)/shard_map/all_to_all | solution.py:346
  130.2 36.2 %all_to_all.17.parts = bf16[32,16,1152]{2,1,0:T(8,128)(2,1)S(1)} all-to-all(bf16[32,16,1152]{2,1,0:T(8,128)(2,1)S(1)} %first_sum.1), channel_id=1, replica_groups=mesh['y'=8,'zl'=4,'c'=2,'zh'=2,'x'=4] {'y','zl'}, dimensions={0} | all-to-all | bytes 2359296 | tf_op jit(solution)/shard_map/all_to_all | solution.py:348
  166.6 5.0 %collective-permute-start.12 = (bf16[4,16,1152]{2,1,0:T(8,128)(2,1)S(1)}, bf16[4,16,1152]{2,1,0:T(8,128)(2,1)S(1)}, u32[]{:S(2)}, u32[]{:S(2)}) collective-permute-start(bf16[4,16,1152]{2,1,0:T(8,128)(2,1)S(1)} %second_sum.1.own), channel_id=1, source_target_pairs={{0,8},{8,0},{1,9},{9,1},{2,10},{10,2},{3,11},{11,3},{4,12},{12,4},... | collective-permute-start | bytes 442376 | tf_op jit(solution)/shard_map/ppermute | solution.py:296
  171.6 1.9 %collective-permute-start.9 = (bf16[16,512]{1,0:T(8,128)(2,1)S(1)}, bf16[16,512]{1,0:T(8,128)(2,1)S(1)}, u32[]{:S(2)}, u32[]{:S(2)}) collective-permute-start(bf16[16,512]{1,0:T(8,128)(2,1)S(1)} %get-tuple-element.40), channel_id=1, source_target_pairs={{0,504},{8,0},{16,8},{24,16},{32,24},{40,32},{48,40},{56,48},{64,5... | collective-permute-start | bytes 49160 | tf_op jit(solution)/shard_map/ppermute | solution.py:292
  173.6 3.6 %collective-permute-start.10 = (bf16[16,512]{1,0:T(8,128)(2,1)S(1)}, bf16[16,512]{1,0:T(8,128)(2,1)S(1)}, u32[]{:S(2)}, u32[]{:S(2)}) collective-permute-start(bf16[16,512]{1,0:T(8,128)(2,1)S(1)} %get-tuple-element.41), channel_id=1, source_target_pairs={{0,8},{8,16},{16,24},{24,32},{32,40},{40,48},{48,56},{56,64},{64,7... | collective-permute-start | bytes 49160 | tf_op jit(solution)/shard_map/ppermute | solution.py:292
  (33 shorter events, 5.0 us)
Async XLA Ops:
  1.6 15.4 %collective-permute-start.2 = (bf16[2,64,512]{2,1,0:T(8,128)(2,1)S(1)}, bf16[2,64,512]{2,1,0:T(8,128)(2,1)S(1)}, u32[]{:S(2)}, u32[]{:S(2)}) collective-permute-start(bf16[2,64,512]{2,1,0:T(8,128)(2,1)S(1)} %broadcast_select_fusion), channel_id=1, source_target_pairs={{0,4},{4,0},{1,5},{5,1},{2,6},{6,2},{3,7},{7,3},{8,12},{12,8},{9,1... | collective-permute-start | bytes 393224 | tf_op jit(solution)/shard_map/ppermute | solution.py:296
  33.7 7.4 %copy-start.5 = (s32[1,2,8]{2,1,0:T(2,128)S(1)}, s32[1,2,8]{2,1,0:T(2,128)}, u32[]{:S(2)}) copy-start(s32[1,2,8]{2,1,0:T(2,128)} %param.17) | copy-start | bytes 196
  33.7 7.4 %copy-start = (bf16[1,128,512]{2,1,0:T(8,128)(2,1)S(1)}, bf16[1,128,512]{2,1,0:T(8,128)(2,1)}, u32[]{:S(2)}) copy-start(bf16[1,128,512]{2,1,0:T(8,128)(2,1)} %param.9) | copy-start | bytes 393220
  33.7 7.4 %copy-start.3 = (s32[1,512]{1,0:T(1,128)S(1)}, s32[1,512]{1,0:T(1,128)}, u32[]{:S(2)}) copy-start(s32[1,512]{1,0:T(1,128)} %senders.1) | copy-start | bytes 6148
  33.7 7.4 %copy-start.4 = (s32[1,512]{1,0:T(1,128)S(1)}, s32[1,512]{1,0:T(1,128)}, u32[]{:S(2)}) copy-start(s32[1,512]{1,0:T(1,128)} %receivers.1) | copy-start | bytes 6148
  33.7 18.5 %copy-start.2 = (f32[2,512]{1,0:T(2,128)S(1)}, f32[2,512]{1,0:T(2,128)}, u32[]{:S(2)}) copy-start(f32[2,512]{1,0:T(2,128)} %gain.5) | copy-start | bytes 12292
  33.8 31.4 %copy-start.1 = (bf16[1,128,512]{2,1,0:T(8,128)(2,1)S(1)}, bf16[1,128,512]{2,1,0:T(8,128)(2,1)}, u32[]{:S(2)}) copy-start(bf16[1,128,512]{2,1,0:T(8,128)(2,1)} %param.10) | copy-start | bytes 393220
  33.8 18.4 %collective-permute-start.3 = (bf16[4,2,64,512]{3,2,1,0:T(8,128)(2,1)S(1)}, bf16[4,2,64,512]{3,2,1,0:T(8,128)(2,1)S(1)}, u32[]{:S(2)}, u32[]{:S(2)}) collective-permute-start(bf16[4,2,64,512]{3,2,1,0:T(8,128)(2,1)S(1)} %get-tuple-element.48.own), channel_id=1, source_target_pairs={{0,8},{8,0},{1,9},{9,1},{2,10},{10,2},{3,11},{11,3},{4,12},{12,4},... | collective-permute-start | bytes 1572872 | tf_op jit(solution)/shard_map/ppermute | solution.py:296
  38.5 25.6 %collective-permute-start.6 = (bf16[4,2,64,512]{3,2,1,0:T(8,128)(2,1)S(1)}, bf16[4,2,64,512]{3,2,1,0:T(8,128)(2,1)S(1)}, u32[]{:S(2)}, u32[]{:S(2)}) collective-permute-start(bf16[4,2,64,512]{3,2,1,0:T(8,128)(2,1)S(1)} %get-tuple-element.47.own), channel_id=1, source_target_pairs={{0,8},{8,0},{1,9},{9,1},{2,10},{10,2},{3,11},{11,3},{4,12},{12,4},... | collective-permute-start | bytes 1572872 | tf_op jit(solution)/shard_map/ppermute | solution.py:296
  41.4 8.2 %collective-permute-start.1 = (bf16[16,512]{1,0:T(8,128)(2,1)S(1)}, bf16[16,512]{1,0:T(8,128)(2,1)S(1)}, u32[]{:S(2)}, u32[]{:S(2)}) collective-permute-start(bf16[16,512]{1,0:T(8,128)(2,1)S(1)} %get-tuple-element.26), channel_id=1, source_target_pairs={{0,504},{8,0},{16,8},{24,16},{32,24},{40,32},{48,40},{56,48},{64,5... | collective-permute-start | bytes 49160 | tf_op jit(solution)/shard_map/ppermute | solution.py:292
  43.8 8.4 %collective-permute-start = (bf16[16,512]{1,0:T(8,128)(2,1)S(1)}, bf16[16,512]{1,0:T(8,128)(2,1)S(1)}, u32[]{:S(2)}, u32[]{:S(2)}) collective-permute-start(bf16[16,512]{1,0:T(8,128)(2,1)S(1)} %get-tuple-element.26), channel_id=1, source_target_pairs={{0,8},{8,16},{16,24},{24,32},{32,40},{40,48},{48,56},{56,64},{64,7... | collective-permute-start | bytes 49160 | tf_op jit(solution)/shard_map/ppermute | solution.py:292
  53.9 10.2 %collective-permute-start.5 = (bf16[16,512]{1,0:T(8,128)(2,1)S(1)}, bf16[16,512]{1,0:T(8,128)(2,1)S(1)}, u32[]{:S(2)}, u32[]{:S(2)}) collective-permute-start(bf16[16,512]{1,0:T(8,128)(2,1)S(1)} %get-tuple-element.30), channel_id=1, source_target_pairs={{0,504},{8,0},{16,8},{24,16},{32,24},{40,32},{48,40},{56,48},{64,5... | collective-permute-start | bytes 49160 | tf_op jit(solution)/shard_map/ppermute | solution.py:292
  62.2 3.1 %collective-permute-start.4 = (bf16[16,512]{1,0:T(8,128)(2,1)S(1)}, bf16[16,512]{1,0:T(8,128)(2,1)S(1)}, u32[]{:S(2)}, u32[]{:S(2)}) collective-permute-start(bf16[16,512]{1,0:T(8,128)(2,1)S(1)} %get-tuple-element.30), channel_id=1, source_target_pairs={{0,8},{8,16},{16,24},{24,32},{32,40},{40,48},{48,56},{56,64},{64,7... | collective-permute-start | bytes 49160 | tf_op jit(solution)/shard_map/ppermute | solution.py:292
  68.3 9.7 %collective-permute-start.7 = (bf16[16,512]{1,0:T(8,128)(2,1)S(1)}, bf16[16,512]{1,0:T(8,128)(2,1)S(1)}, u32[]{:S(2)}, u32[]{:S(2)}) collective-permute-start(bf16[16,512]{1,0:T(8,128)(2,1)S(1)} %get-tuple-element.33), channel_id=1, source_target_pairs={{0,504},{8,0},{16,8},{24,16},{32,24},{40,32},{48,40},{56,48},{64,5... | collective-permute-start | bytes 49160 | tf_op jit(solution)/shard_map/ppermute | solution.py:292
  76.1 3.1 %collective-permute-start.8 = (bf16[16,512]{1,0:T(8,128)(2,1)S(1)}, bf16[16,512]{1,0:T(8,128)(2,1)S(1)}, u32[]{:S(2)}, u32[]{:S(2)}) collective-permute-start(bf16[16,512]{1,0:T(8,128)(2,1)S(1)} %get-tuple-element.34), channel_id=1, source_target_pairs={{0,8},{8,16},{16,24},{24,32},{32,40},{40,48},{48,56},{56,64},{64,7... | collective-permute-start | bytes 49160 | tf_op jit(solution)/shard_map/ppermute | solution.py:292
  80.5 9.5 %collective-permute-start.11 = (bf16[624,512]{1,0:T(8,128)(2,1)S(1)}, bf16[624,512]{1,0:T(8,128)(2,1)S(1)}, u32[]{:S(2)}, u32[]{:S(2)}) collective-permute-start(bf16[624,512]{1,0:T(8,128)(2,1)S(1)} %get-tuple-element.42.pack), channel_id=1, source_target_pairs={{0,8},{8,0},{1,9},{9,1},{2,10},{10,2},{3,11},{11,3},{4,12},{12,4},... | collective-permute-start | bytes 1916936 | tf_op jit(solution)/shard_map/ppermute | solution.py:296
  166.6 12.3 %collective-permute-start.12 = (bf16[4,16,1152]{2,1,0:T(8,128)(2,1)S(1)}, bf16[4,16,1152]{2,1,0:T(8,128)(2,1)S(1)}, u32[]{:S(2)}, u32[]{:S(2)}) collective-permute-start(bf16[4,16,1152]{2,1,0:T(8,128)(2,1)S(1)} %second_sum.1.own), channel_id=1, source_target_pairs={{0,8},{8,0},{1,9},{9,1},{2,10},{10,2},{3,11},{11,3},{4,12},{12,4},... | collective-permute-start | bytes 442376 | tf_op jit(solution)/shard_map/ppermute | solution.py:296
  171.6 5.6 %collective-permute-start.9 = (bf16[16,512]{1,0:T(8,128)(2,1)S(1)}, bf16[16,512]{1,0:T(8,128)(2,1)S(1)}, u32[]{:S(2)}, u32[]{:S(2)}) collective-permute-start(bf16[16,512]{1,0:T(8,128)(2,1)S(1)} %get-tuple-element.40), channel_id=1, source_target_pairs={{0,504},{8,0},{16,8},{24,16},{32,24},{40,32},{48,40},{56,48},{64,5... | collective-permute-start | bytes 49160 | tf_op jit(solution)/shard_map/ppermute | solution.py:292
  173.6 4.5 %collective-permute-start.10 = (bf16[16,512]{1,0:T(8,128)(2,1)S(1)}, bf16[16,512]{1,0:T(8,128)(2,1)S(1)}, u32[]{:S(2)}, u32[]{:S(2)}) collective-permute-start(bf16[16,512]{1,0:T(8,128)(2,1)S(1)} %get-tuple-element.41), channel_id=1, source_target_pairs={{0,8},{8,16},{16,24},{24,32},{32,40},{40,48},{48,56},{56,64},{64,7... | collective-permute-start | bytes 49160 | tf_op jit(solution)/shard_map/ppermute | solution.py:292

commit v2 on v1

--- a/solution.py
+++ b/solution.py
@@ -19,7 +19,7 @@
 ROWS = EXT + N
 HALF = D // 2
 DROWS = ROWS + 16
-CHUNK_LANES = 4 * HALF + 128
+PARTS = 64
 
 BF = jnp.bfloat16
 F32 = jnp.float32
@@ -81,9 +81,9 @@
     sent[...] = dot_tn(send_matrix_of(send_rows), rows[...]).astype(BF)
 
 
-def weights_of(core, own, peer):
+def weights_of(core, own, peer, layer):
     def whole(ref):
-        return jnp.concatenate([ref[x, z] for z in range(2) for x in range(4)], axis=0)
+        return jnp.concatenate([ref[x, z, layer] for z in range(2) for x in range(4)], axis=0)
 
     first, second = whole(own), whole(peer)
     is_first = core[0, 0] == 0
@@ -148,7 +148,7 @@
     core, rows, from_prev, from_next, own, peer, gain, by_row, by_edge, send_rows,
     result, total_out, slope_out, sent,
 ):
-    send_matrix, recv_matrix = weights_of(core, own, peer)
+    send_matrix, recv_matrix = weights_of(core, own, peer, 0)
     total, slope = forward(
         rows[...], from_prev[...], from_next[...], send_matrix, recv_matrix, by_row, by_edge
     )
@@ -163,7 +163,7 @@
     core, rows, from_prev, from_next, own, peer, gain, by_row, by_edge, out_grad,
     result, own_grad, to_prev, to_next, keep, give,
 ):
-    send_matrix, recv_matrix = weights_of(core, own, peer)
+    send_matrix, recv_matrix = weights_of(core, own, peer, 1)
     total, slope = forward(
         rows[...], from_prev[...], from_next[...], send_matrix, recv_matrix, by_row, by_edge
     )
@@ -190,7 +190,7 @@
     rows_0, prev_0, next_0, rows_1, prev_1, next_1, later_keep, later_give,
     own_grad, to_prev, to_next, keep, pack,
 ):
-    send_matrix, recv_matrix = weights_of(core, own, peer)
+    send_matrix, recv_matrix = weights_of(core, own, peer, 0)
     cotangent = merged(later_grad, back_next, back_prev, send_rows).astype(F32)
     grad, prev_grad, next_grad, row_grad, gain_block = backward(
         cotangent, total[...], slope[...], gain[0:1, :], send_matrix, recv_matrix, by_row, by_edge
@@ -235,35 +235,38 @@
                     [keep[EXT:ROWS, lanes], peer[base + EXT : base + ROWS, lanes]], axis=0
                 )
             term = dot_tn(left, right).astype(BF)
-            for block in range(8):
-                for part in range(4):
-                    start = block * 64 + part * 16
-                    chunks[block, 2 * kind + layer, :, part * HALF : (part + 1) * HALF] = term[
-                        start : start + 16
-                    ]
+            for z in range(2):
+                for x in range(4):
+                    start = (z * 4 + x) * 64
+                    place = (z * 4 + 2 * kind + layer) * 64
+                    chunks[x, place : place + 64, :] = term[start : start + 64]
         gain = keep[ROWS:DROWS, lanes].astype(F32) + peer[base + ROWS : base + DROWS, lanes].astype(F32)
-        gains += [gain[0:1, :128], gain[0:1, 128:]]
-    block = jnp.concatenate(gains + [jnp.zeros((12, 128), F32)], axis=0).astype(BF)
-    for first in range(8):
-        for second in range(4):
-            chunks[first, second, :, 4 * HALF :] = block
-
-
-def first_sum_kernel(parts, copies):
+        gains.append(gain[0:1, :])
+    block = jnp.concatenate(gains + [jnp.zeros((14, HALF), F32)], axis=0).astype(BF)
+    for x in range(4):
+        chunks[x, 512:528, :] = block
+
+
+def first_sum_kernel(parts, pieces):
     total = parts[0].astype(F32)
-    for source in range(1, 32):
+    for source in range(1, 4):
+        total = total + parts[source].astype(F32)
+    gains = [total[512 + layer : 513 + layer, half : half + 128] for layer in range(2) for half in (0, 128)]
+    gain = jnp.concatenate(gains + [jnp.zeros((4, 128), F32)], axis=0).astype(BF)
+    for y in range(8):
+        for z in range(8):
+            start = z * 64 + y * 8
+            pieces[y * 8 + z, :, 0:HALF] = total[start : start + 8].astype(BF)
+            pieces[y * 8 + z, :, HALF:] = gain
+
+
+def second_sum_kernel(parts, copies):
+    total = parts[0].astype(F32)
+    for source in range(1, PARTS):
         total = total + parts[source].astype(F32)
     total = total.astype(BF)
     for target in range(32):
         copies[target] = total
-
-
-def second_sum_kernel(parts, result):
-    for place in range(4):
-        total = parts[place].astype(F32)
-        for source in range(1, 8):
-            total = total + parts[4 * source + place].astype(F32)
-        result[place] = total.astype(BF)
 
 
 def spread_kernel(core, own, peer, send_grad, recv_grad, gain_grad):
@@ -272,17 +275,16 @@
     mine, theirs = own[...].astype(F32) * scale, peer[...].astype(F32) * scale
     sides = (jnp.where(is_first, mine, theirs), jnp.where(is_first, theirs, mine))
     for side, value in enumerate(sides):
+        columns = slice(side * HALF, (side + 1) * HALF)
         for matrix in range(4):
             out = (send_grad, recv_grad)[matrix // 2]
-            for part in range(4):
-                out[matrix % 2, part * 16 : part * 16 + 16, side * HALF : (side + 1) * HALF] = value[
-                    matrix, :, part * HALF : (part + 1) * HALF
-                ]
+            for y in range(8):
+                out[matrix % 2, y * 8 : y * 8 + 8, columns] = value[y * 4 + matrix, :, 0:HALF]
         for layer in range(2):
             for half in range(2):
                 start = side * HALF + half * 128
                 row = layer * 2 + half
-                gain_grad[layer : layer + 1, start : start + 128] = value[0, row : row + 1, 4 * HALF :]
+                gain_grad[layer : layer + 1, start : start + 128] = value[0, row : row + 1, HALF:]
 
 
 GRAPH = ("y", "zl", "c")
@@ -303,50 +305,50 @@
     features = node_features[0]
     targets = send_rows.reshape(1, H)
     half = jnp.where(lax.axis_index("c") == 0, send_weight, recv_weight)
-    other = swap(half, "zh")
+    other = lax.ppermute(half, ("zl", "zh"), [(i, 7 - i) for i in range(8)])
     by_row, by_edge, sent_0 = call(
         prepare_kernel,
         [((ROWS, E), BF), ((3, E, N), BF), ((H, D), BF)],
         "prepare",
         edge_count.reshape(1, 1), senders, receivers, targets, features,
     )
-    prev_0, next_0 = shift(sent_0, 1), shift(sent_0, -1)
+    other, prev_0, next_0 = lax.optimization_barrier((other, shift(sent_0, 1), shift(sent_0, -1)))
     is_low = lax.axis_index("zh") == 0
-    both = jnp.stack([jnp.where(is_low, half, other), jnp.where(is_low, other, half)], axis=1)
+    both = jnp.stack([jnp.where(is_low, half, other), jnp.where(is_low, other, half)])
     copies = jnp.broadcast_to(both[None], (4,) + both.shape)
-    gathered = lax.all_to_all(copies, ("x",), 0, 0, tiled=True)
-    own = [gathered[:, layer] for layer in range(2)]
-    peer = [swap(value, "c") for value in own]
+    own = lax.all_to_all(copies, ("x",), 0, 0, tiled=True)
+    peer = swap(own, "c")
 
     rows_1, total_0, slope_0, sent_1 = call(
         first_layer_kernel,
         [((N, D), BF), ((N, D), F32), ((E, D), F32), ((H, D), BF)],
         "first_layer",
-        core, features, prev_0, next_0, own[0], peer[0], gain, by_row, by_edge, targets,
+        core, features, prev_0, next_0, own, peer, gain, by_row, by_edge, targets,
     )
     prev_1, next_1 = shift(sent_1, 1), shift(sent_1, -1)
     updated, grad_1, to_prev, to_next, keep_1, give_1 = call(
         last_layer_kernel,
         [((N, D), BF), ((N, D), F32), ((H, D), BF), ((H, D), BF), ((DROWS, HALF), BF), ((DROWS, HALF), BF)],
         "last_layer",
-        core, rows_1, prev_1, next_1, own[1], peer[1], gain, by_row, by_edge, out_grad[0],
+        core, rows_1, prev_1, next_1, own, peer, gain, by_row, by_edge, out_grad[0],
     )
     back_next, back_prev = shift(to_prev, -1), shift(to_next, 1)
     grad_0, to_prev, to_next, keep, pack = call(
         back_kernel,
         [((N, D), F32), ((H, D), BF), ((H, D), BF), ((DROWS, D), BF), ((2 * EXT + DROWS, D), BF)],
         "back",
-        core, grad_1, back_next, back_prev, total_0, slope_0, own[0], peer[0], gain, by_row, by_edge,
+        core, grad_1, back_next, back_prev, total_0, slope_0, own, peer, gain, by_row, by_edge,
         targets, features, prev_0, next_0, rows_1, prev_1, next_1, keep_1, give_1,
     )
     peer_pack = swap(pack, "c")
     back_next, back_prev = shift(to_prev, -1), shift(to_next, 1)
-    (chunks,) = call(terms_kernel, [((8, 4, 16, CHUNK_LANES), BF)], "terms", pack, keep, peer_pack)
-    chunks = chunks.reshape(32, 16, CHUNK_LANES)
-    parts = lax.all_to_all(chunks, ("zh", "x", "zl"), 0, 0, tiled=True)
-    (copies,) = call(first_sum_kernel, [((32, 16, CHUNK_LANES), BF)], "first_sum", parts)
-    parts = lax.all_to_all(copies, ("y", "zl"), 0, 0, tiled=True)
-    (mine,) = call(second_sum_kernel, [((4, 16, CHUNK_LANES), BF)], "second_sum", parts)
+    peer_pack, back_next, back_prev = lax.optimization_barrier((peer_pack, back_next, back_prev))
+    (chunks,) = call(terms_kernel, [((4, 528, HALF), BF)], "terms", pack, keep, peer_pack)
+    parts = lax.all_to_all(chunks, ("x",), 0, 0, tiled=True)
+    (pieces,) = call(first_sum_kernel, [((PARTS, 8, HALF + 128), BF)], "first_sum", parts)
+    parts = lax.all_to_all(pieces, ("y", "zh", "zl"), 0, 0, tiled=True)
+    (copies,) = call(second_sum_kernel, [((32, 8, HALF + 128), BF)], "second_sum", parts)
+    mine = lax.all_to_all(copies, ("y", "zl"), 0, 0, tiled=True)
     theirs = swap(mine, "c")
     send_grad, recv_grad, gain_grad = call(
         spread_kernel, [((2, 64, D), F32), ((2, 64, D), F32), ((2, D), F32)], "spread", core, mine, theirs

time: 183 us -> 151 us (0.83); the launches traced: 180 us -> 150 us
  blocking collectives: 92.3 us -> 63.1 us
  local copies, waits for them, and re-layouts: 0.31 us -> 3.14 us
    all_to_all x3 -> x4, blocking collectives: 92.3 us -> 63.1 us  [the longest x1 21.2 us: shards(): parts = lax.all_to_all(pieces, ('y', 'zh', 'zl'), 0, 0, tiled=True)]
    ppermute x0 -> x1, starting transfers between devices: none -> 11.5 us  [shards(): other = lax.ppermute(half, ('zl', 'zh'), [(i, 7 - i) for i in range(8)])]
    ppermute x5 -> x3, starting transfers between devices: 30.8 us -> 24.1 us  [swap(): return lax.ppermute(value, axis, [(0, 1), (1, 0)])]
    ppermute x8, starting transfers between devices: 33.7 us -> 27.2 us  [shift(): lax.ppermute(value, GRAPH, [(i, (i + steps) % 64) for i in range(64)])]
    ppermute x5 -> x3, waiting for transfers between devices: 5.57 us -> 2.49 us  [swap(): return lax.ppermute(value, axis, [(0, 1), (1, 0)])]
    unnamed x12, local copies, waits for them, and re-layouts: 0.03 us -> 2.28 us
  transfers between devices with their start and end apart: 13 -> 12, of which waited for: 6 -> 6; matrix products, arithmetic and copies ran while one was open for 0% -> 1% of each run, Pallas kernels for 2% -> 1%
where the time goes in v2:
time: 151 us; the launch traced here: 150 us
  blocking collectives  63.1 us (42%)
  starting transfers between devices  62.9 us (42%)
  waiting for transfers between devices  9.63 us (6%)
  Pallas kernels  8.71 us (6%)
  local copies, waits for them, and re-layouts  3.14 us (2%)
    ppermute x8, starting transfers between devices, shift(): lax.ppermute(value, GRAPH, [(i, (i + steps) % 64) for i in range(64)])  27.2 us
    ppermute x3, starting transfers between devices, swap(): return lax.ppermute(value, axis, [(0, 1), (1, 0)])  24.1 us
    all_to_all x1, blocking collectives, shards(): parts = lax.all_to_all(pieces, ('y', 'zh', 'zl'), 0, 0, tiled=True)  21.2 us
    all_to_all x1, blocking collectives, shards(): mine = lax.all_to_all(copies, ('y', 'zl'), 0, 0, tiled=True)  15 us
    all_to_all x1, blocking collectives, shards(): own = lax.all_to_all(copies, ('x',), 0, 0, tiled=True)  13.7 us
    all_to_all x1, blocking collectives, shards(): parts = lax.all_to_all(chunks, ('x',), 0, 0, tiled=True)  13.2 us
    ppermute x1, starting transfers between devices, shards(): other = lax.ppermute(half, ('zl', 'zh'), [(i, 7 - i) for i in range(8)])  11.5 us
    pallas_call x9, Pallas kernels, call(): pl.pallas_call(kernel, out_shape=[jax.ShapeDtypeStruct(s, t) for s, t in...  8.71 us
  transfers between devices with their start and end apart: 12, of which 6 were waited for; matrix products, arithmetic and copies ran while one was open for 1% of the time, Pallas kernels for 1%

profile of v2, /device:TPU:1, one launch (start us, length us, event | category | flops | bytes accessed | tf_op | source)
XLA Modules:
  0.0 149.9 jit_solution(9312450670532201208)
XLA Ops:
  0.6 0.9 broadcast_select_fusion
  1.6 11.5 %collective-permute-start = (bf16[2,64,512]{2,1,0:T(8,128)(2,1)S(1)}, bf16[2,64,512]{2,1,0:T(8,128)(2,1)S(1)}, u32[]{:S(2)}, u32[]{:S(2)}) collective-permute-start(bf16[2,64,512]{2,1,0:T(8,128)(2,1)S(1)} %broadcast_select_fusion), channel_id=1, source_target_pairs={{0,52},{4,48},{16,36},{20,32},{32,20},{36,16},{48,4},{52,0},{1,53}... | collective-permute-start | bytes 393224 | tf_op jit(solution)/shard_map/ppermute | solution.py:308
  17.0 2.9 %collective-permute-start.2 = (bf16[16,512]{1,0:T(8,128)(2,1)S(1)}, bf16[16,512]{1,0:T(8,128)(2,1)S(1)}, u32[]{:S(2)}, u32[]{:S(2)}) collective-permute-start(bf16[16,512]{1,0:T(8,128)(2,1)S(1)} %get-tuple-element.32), channel_id=1, source_target_pairs={{0,504},{8,0},{16,8},{24,16},{32,24},{40,32},{48,40},{56,48},{64,5... | collective-permute-start | bytes 49160 | tf_op jit(solution)/shard_map/ppermute | solution.py:294
  19.9 3.0 %collective-permute-start.1 = (bf16[16,512]{1,0:T(8,128)(2,1)S(1)}, bf16[16,512]{1,0:T(8,128)(2,1)S(1)}, u32[]{:S(2)}, u32[]{:S(2)}) collective-permute-start(bf16[16,512]{1,0:T(8,128)(2,1)S(1)} %get-tuple-element.32), channel_id=1, source_target_pairs={{0,8},{8,16},{16,24},{24,32},{32,40},{40,48},{48,56},{56,64},{64,7... | collective-permute-start | bytes 49160 | tf_op jit(solution)/shard_map/ppermute | solution.py:294
  22.9 2.2 %collective-permute-done.1.from_prev.prev_0 = bf16[16,512]{1,0:T(8,128)(2,1)S(1)} collective-permute-done((bf16[16,512]{1,0:T(8,128)(2,1)S(1)}, bf16[16,512]{1,0:T(8,128)(2,1)S(1)}, u32[]{:S(2)}, u32[]{:S(2)}) %collective-permute-start.1) | collective-permute-done | bytes 16416 | tf_op jit(solution)/shard_map/ppermute | solution.py:294
  25.2 13.7 %all_to_all.20.own = bf16[4,2,2,64,512]{4,3,2,1,0:T(8,128)(2,1)S(1)} all-to-all(bf16[4,2,2,64,512]{4,3,2,1,0:T(8,128)(2,1)S(1)} %broadcast_in_dim.12), channel_id=1, replica_groups=mesh['y'=8,'zl'=4,'c'=2,'zh'=2,'x'=4] {'x'}, dimensions={0} | all-to-all | bytes 2097152 | tf_op jit(solution)/shard_map/all_to_all | solution.py:319
  38.9 9.7 %collective-permute-start.3 = (bf16[4,2,2,64,512]{4,3,2,1,0:T(8,128)(2,1)S(1)}, bf16[4,2,2,64,512]{4,3,2,1,0:T(8,128)(2,1)S(1)}, u32[]{:S(2)}, u32[]{:S(2)}) collective-permute-start(bf16[4,2,2,64,512]{4,3,2,1,0:T(8,128)(2,1)S(1)} %all_to_all.20.own), channel_id=1, source_target_pairs={{0,8},{8,0},{1,9},{9,1},{2,10},{10,2},{3,11},{11,3},{4,12},{12,4},... | collective-permute-start | bytes 3145736 | tf_op jit(solution)/shard_map/ppermute | solution.py:298
  48.7 2.3 %collective-permute-done.3.peer = bf16[4,2,2,64,512]{4,3,2,1,0:T(8,128)(2,1)S(1)} collective-permute-done((bf16[4,2,2,64,512]{4,3,2,1,0:T(8,128)(2,1)S(1)}, bf16[4,2,2,64,512]{4,3,2,1,0:T(8,128)(2,1)S(1)}, u32[]{:S(2)}, u32[]{:S(2)}) %collective-permute-start.3) | collective-permute-done | bytes 1048608 | tf_op jit(solution)/shard_map/ppermute | solution.py:298
  50.9 1.7 %first_layer.1 = (bf16[128,512]{1,0:T(8,128)(2,1)S(1)}, f32[128,512]{1,0:T(8,128)S(1)}, f32[512,512]{1,0:T(8,128)S(1)}, bf16[16,512]{1,0:T(8,128)(2,1)S(1)}) custom-call(s32[1,1]{1,0:T(1,128)} %bitcast.core, bf16[128,512]{1,0:T(8,128)(2,1)S(1)} %bitcast.12, bf16[16,512]{1,0:T(8,128)(2,1)S(1)} %collective-permute-done.1.from_prev.prev_0, ...), custom_call_target="tpu_custom_call" | custom-call | flops 100000000 | bytes 2000000 | tf_op jit(solution)/shard_map/first_layer/pallas_call | solution.py:49
  52.6 2.3 %collective-permute-start.5 = (bf16[16,512]{1,0:T(8,128)(2,1)S(1)}, bf16[16,512]{1,0:T(8,128)(2,1)S(1)}, u32[]{:S(2)}, u32[]{:S(2)}) collective-permute-start(bf16[16,512]{1,0:T(8,128)(2,1)S(1)} %get-tuple-element.39), channel_id=1, source_target_pairs={{0,504},{8,0},{16,8},{24,16},{32,24},{40,32},{48,40},{56,48},{64,5... | collective-permute-start | bytes 49160 | tf_op jit(solution)/shard_map/ppermute | solution.py:294
  54.9 3.3 %collective-permute-start.4 = (bf16[16,512]{1,0:T(8,128)(2,1)S(1)}, bf16[16,512]{1,0:T(8,128)(2,1)S(1)}, u32[]{:S(2)}, u32[]{:S(2)}) collective-permute-start(bf16[16,512]{1,0:T(8,128)(2,1)S(1)} %get-tuple-element.39), channel_id=1, source_target_pairs={{0,8},{8,16},{16,24},{24,32},{32,40},{40,48},{48,56},{56,64},{64,7... | collective-permute-start | bytes 49160 | tf_op jit(solution)/shard_map/ppermute | solution.py:294
  58.2 3.0 %collective-permute-done.4.from_prev.prev_1 = bf16[16,512]{1,0:T(8,128)(2,1)S(1)} collective-permute-done((bf16[16,512]{1,0:T(8,128)(2,1)S(1)}, bf16[16,512]{1,0:T(8,128)(2,1)S(1)}, u32[]{:S(2)}, u32[]{:S(2)}) %collective-permute-start.4) | collective-permute-done | bytes 16416 | tf_op jit(solution)/shard_map/ppermute | solution.py:294
  61.1 3.0 %last_layer.1 = (bf16[128,512]{1,0:T(8,128)(2,1)}, f32[128,512]{1,0:T(8,128)S(1)}, bf16[16,512]{1,0:T(8,128)(2,1)S(1)}, bf16[16,512]{1,0:T(8,128)(2,1)S(1)}, bf1...) custom-call(s32[1,1]{1,0:T(1,128)} %bitcast.core, bf16[128,512]{1,0:T(8,128)(2,1)S(1)} %get-tuple-element.38.rows.rows_1, ...), custom_call_target="tpu_custom_call" | custom-call | flops 100000000 | bytes 2000000 | tf_op jit(solution)/shard_map/last_layer/pallas_call | solution.py:49
  64.2 8.4 %collective-permute-start.6 = (bf16[16,512]{1,0:T(8,128)(2,1)S(1)}, bf16[16,512]{1,0:T(8,128)(2,1)S(1)}, u32[]{:S(2)}, u32[]{:S(2)}) collective-permute-start(bf16[16,512]{1,0:T(8,128)(2,1)S(1)} %get-tuple-element.42), channel_id=1, source_target_pairs={{0,504},{8,0},{16,8},{24,16},{32,24},{40,32},{48,40},{56,48},{64,5... | collective-permute-start | bytes 49160 | tf_op jit(solution)/shard_map/ppermute | solution.py:294
  72.5 1.9 %collective-permute-start.7 = (bf16[16,512]{1,0:T(8,128)(2,1)S(1)}, bf16[16,512]{1,0:T(8,128)(2,1)S(1)}, u32[]{:S(2)}, u32[]{:S(2)}) collective-permute-start(bf16[16,512]{1,0:T(8,128)(2,1)S(1)} %get-tuple-element.43), channel_id=1, source_target_pairs={{0,8},{8,16},{16,24},{24,32},{32,40},{40,48},{48,56},{56,64},{64,7... | collective-permute-start | bytes 49160 | tf_op jit(solution)/shard_map/ppermute | solution.py:294
  74.5 1.1 collective-permute-done.7.back_prev
  75.6 1.3 back.1
  76.9 7.8 %collective-permute-start.8 = (bf16[624,512]{1,0:T(8,128)(2,1)S(1)}, bf16[624,512]{1,0:T(8,128)(2,1)S(1)}, u32[]{:S(2)}, u32[]{:S(2)}) collective-permute-start(bf16[624,512]{1,0:T(8,128)(2,1)S(1)} %get-tuple-element.49.pack), channel_id=1, source_target_pairs={{0,8},{8,0},{1,9},{9,1},{2,10},{10,2},{3,11},{11,3},{4,12},{12,4},... | collective-permute-start | bytes 1916936 | tf_op jit(solution)/shard_map/ppermute | solution.py:298
  84.7 1.9 %collective-permute-start.9 = (bf16[16,512]{1,0:T(8,128)(2,1)S(1)}, bf16[16,512]{1,0:T(8,128)(2,1)S(1)}, u32[]{:S(2)}, u32[]{:S(2)}) collective-permute-start(bf16[16,512]{1,0:T(8,128)(2,1)S(1)} %get-tuple-element.50), channel_id=1, source_target_pairs={{0,504},{8,0},{16,8},{24,16},{32,24},{40,32},{48,40},{56,48},{64,5... | collective-permute-start | bytes 49160 | tf_op jit(solution)/shard_map/ppermute | solution.py:294
  86.6 3.6 %collective-permute-start.10 = (bf16[16,512]{1,0:T(8,128)(2,1)S(1)}, bf16[16,512]{1,0:T(8,128)(2,1)S(1)}, u32[]{:S(2)}, u32[]{:S(2)}) collective-permute-start(bf16[16,512]{1,0:T(8,128)(2,1)S(1)} %get-tuple-element.51), channel_id=1, source_target_pairs={{0,8},{8,16},{16,24},{24,32},{32,40},{40,48},{48,56},{56,64},{64,7... | collective-permute-start | bytes 49160 | tf_op jit(solution)/shard_map/ppermute | solution.py:294
  91.8 13.2 %all_to_all.21.parts = bf16[4,528,256]{2,1,0:T(8,128)(2,1)S(1)} all-to-all(bf16[4,528,256]{2,1,0:T(8,128)(2,1)S(1)} %terms.1), channel_id=1, replica_groups=mesh['y'=8,'zl'=4,'c'=2,'zh'=2,'x'=4] {'x'}, dimensions={0} | all-to-all | bytes 2162688 | tf_op jit(solution)/shard_map/all_to_all | solution.py:347
  105.1 21.2 %all_to_all.22.parts = bf16[64,8,384]{2,1,0:T(8,128)(2,1)S(1)} all-to-all(bf16[64,8,384]{2,1,0:T(8,128)(2,1)S(1)} %first_sum.1), channel_id=1, replica_groups=mesh['y'=8,'zl'=4,'c'=2,'zh'=2,'x'=4] {'y','zh','zl'}, dimensions={0} | all-to-all | bytes 786432 | tf_op jit(solution)/shard_map/all_to_all | solution.py:349
  126.4 15.0 %all_to_all.23.own = bf16[32,8,384]{2,1,0:T(8,128)(2,1)S(1)} all-to-all(bf16[32,8,384]{2,1,0:T(8,128)(2,1)S(1)} %second_sum.1), channel_id=1, replica_groups=mesh['y'=8,'zl'=4,'c'=2,'zh'=2,'x'=4] {'y','zl'}, dimensions={0} | all-to-all | bytes 393216 | tf_op jit(solution)/shard_map/all_to_all | solution.py:351
  141.5 6.6 %collective-permute-start.11 = (bf16[32,8,384]{2,1,0:T(8,128)(2,1)S(1)}, bf16[32,8,384]{2,1,0:T(8,128)(2,1)S(1)}, u32[]{:S(2)}, u32[]{:S(2)}) collective-permute-start(bf16[32,8,384]{2,1,0:T(8,128)(2,1)S(1)} %all_to_all.23.own), channel_id=1, source_target_pairs={{0,8},{8,0},{1,9},{9,1},{2,10},{10,2},{3,11},{11,3},{4,12},{12,4},... | collective-permute-start | bytes 589832 | tf_op jit(solution)/shard_map/ppermute | solution.py:298
  (30 shorter events, 7.0 us)
Async XLA Ops:
  1.6 23.5 %collective-permute-start = (bf16[2,64,512]{2,1,0:T(8,128)(2,1)S(1)}, bf16[2,64,512]{2,1,0:T(8,128)(2,1)S(1)}, u32[]{:S(2)}, u32[]{:S(2)}) collective-permute-start(bf16[2,64,512]{2,1,0:T(8,128)(2,1)S(1)} %broadcast_select_fusion), channel_id=1, source_target_pairs={{0,52},{4,48},{16,36},{20,32},{32,20},{36,16},{48,4},{52,0},{1,53}... | collective-permute-start | bytes 393224 | tf_op jit(solution)/shard_map/ppermute | solution.py:308
  14.5 0.9 copy-start
  15.4 0.7 copy-start.4
  16.1 0.7 copy-start.5
  17.0 5.9 %collective-permute-start.2 = (bf16[16,512]{1,0:T(8,128)(2,1)S(1)}, bf16[16,512]{1,0:T(8,128)(2,1)S(1)}, u32[]{:S(2)}, u32[]{:S(2)}) collective-permute-start(bf16[16,512]{1,0:T(8,128)(2,1)S(1)} %get-tuple-element.32), channel_id=1, source_target_pairs={{0,504},{8,0},{16,8},{24,16},{32,24},{40,32},{48,40},{56,48},{64,5... | collective-permute-start | bytes 49160 | tf_op jit(solution)/shard_map/ppermute | solution.py:294
  19.9 5.2 %collective-permute-start.1 = (bf16[16,512]{1,0:T(8,128)(2,1)S(1)}, bf16[16,512]{1,0:T(8,128)(2,1)S(1)}, u32[]{:S(2)}, u32[]{:S(2)}) collective-permute-start(bf16[16,512]{1,0:T(8,128)(2,1)S(1)} %get-tuple-element.32), channel_id=1, source_target_pairs={{0,8},{8,16},{16,24},{24,32},{32,40},{40,48},{48,56},{56,64},{64,7... | collective-permute-start | bytes 49160 | tf_op jit(solution)/shard_map/ppermute | solution.py:294
  25.2 25.7 %copy-start.1 = (bf16[1,128,512]{2,1,0:T(8,128)(2,1)S(1)}, bf16[1,128,512]{2,1,0:T(8,128)(2,1)}, u32[]{:S(2)}) copy-start(bf16[1,128,512]{2,1,0:T(8,128)(2,1)} %param.9) | copy-start | bytes 393220
  25.2 25.7 %copy-start.3 = (f32[2,512]{1,0:T(2,128)S(1)}, f32[2,512]{1,0:T(2,128)}, u32[]{:S(2)}) copy-start(f32[2,512]{1,0:T(2,128)} %gain.5) | copy-start | bytes 12292
  38.9 12.0 %collective-permute-start.3 = (bf16[4,2,2,64,512]{4,3,2,1,0:T(8,128)(2,1)S(1)}, bf16[4,2,2,64,512]{4,3,2,1,0:T(8,128)(2,1)S(1)}, u32[]{:S(2)}, u32[]{:S(2)}) collective-permute-start(bf16[4,2,2,64,512]{4,3,2,1,0:T(8,128)(2,1)S(1)} %all_to_all.20.own), channel_id=1, source_target_pairs={{0,8},{8,0},{1,9},{9,1},{2,10},{10,2},{3,11},{11,3},{4,12},{12,4},... | collective-permute-start | bytes 3145736 | tf_op jit(solution)/shard_map/ppermute | solution.py:298
  50.9 10.2 %copy-start.2 = (bf16[1,128,512]{2,1,0:T(8,128)(2,1)S(1)}, bf16[1,128,512]{2,1,0:T(8,128)(2,1)}, u32[]{:S(2)}) copy-start(bf16[1,128,512]{2,1,0:T(8,128)(2,1)} %param.10) | copy-start | bytes 393220
  52.6 5.6 %collective-permute-start.5 = (bf16[16,512]{1,0:T(8,128)(2,1)S(1)}, bf16[16,512]{1,0:T(8,128)(2,1)S(1)}, u32[]{:S(2)}, u32[]{:S(2)}) collective-permute-start(bf16[16,512]{1,0:T(8,128)(2,1)S(1)} %get-tuple-element.39), channel_id=1, source_target_pairs={{0,504},{8,0},{16,8},{24,16},{32,24},{40,32},{48,40},{56,48},{64,5... | collective-permute-start | bytes 49160 | tf_op jit(solution)/shard_map/ppermute | solution.py:294
  54.9 6.3 %collective-permute-start.4 = (bf16[16,512]{1,0:T(8,128)(2,1)S(1)}, bf16[16,512]{1,0:T(8,128)(2,1)S(1)}, u32[]{:S(2)}, u32[]{:S(2)}) collective-permute-start(bf16[16,512]{1,0:T(8,128)(2,1)S(1)} %get-tuple-element.39), channel_id=1, source_target_pairs={{0,8},{8,16},{16,24},{24,32},{32,40},{40,48},{48,56},{56,64},{64,7... | collective-permute-start | bytes 49160 | tf_op jit(solution)/shard_map/ppermute | solution.py:294
  64.2 10.3 %collective-permute-start.6 = (bf16[16,512]{1,0:T(8,128)(2,1)S(1)}, bf16[16,512]{1,0:T(8,128)(2,1)S(1)}, u32[]{:S(2)}, u32[]{:S(2)}) collective-permute-start(bf16[16,512]{1,0:T(8,128)(2,1)S(1)} %get-tuple-element.42), channel_id=1, source_target_pairs={{0,504},{8,0},{16,8},{24,16},{32,24},{40,32},{48,40},{56,48},{64,5... | collective-permute-start | bytes 49160 | tf_op jit(solution)/shard_map/ppermute | solution.py:294
  72.5 3.1 %collective-permute-start.7 = (bf16[16,512]{1,0:T(8,128)(2,1)S(1)}, bf16[16,512]{1,0:T(8,128)(2,1)S(1)}, u32[]{:S(2)}, u32[]{:S(2)}) collective-permute-start(bf16[16,512]{1,0:T(8,128)(2,1)S(1)} %get-tuple-element.43), channel_id=1, source_target_pairs={{0,8},{8,16},{16,24},{24,32},{32,40},{40,48},{48,56},{56,64},{64,7... | collective-permute-start | bytes 49160 | tf_op jit(solution)/shard_map/ppermute | solution.py:294
  76.9 14.2 %collective-permute-start.8 = (bf16[624,512]{1,0:T(8,128)(2,1)S(1)}, bf16[624,512]{1,0:T(8,128)(2,1)S(1)}, u32[]{:S(2)}, u32[]{:S(2)}) collective-permute-start(bf16[624,512]{1,0:T(8,128)(2,1)S(1)} %get-tuple-element.49.pack), channel_id=1, source_target_pairs={{0,8},{8,0},{1,9},{9,1},{2,10},{10,2},{3,11},{11,3},{4,12},{12,4},... | collective-permute-start | bytes 1916936 | tf_op jit(solution)/shard_map/ppermute | solution.py:298
  84.7 5.6 %collective-permute-start.9 = (bf16[16,512]{1,0:T(8,128)(2,1)S(1)}, bf16[16,512]{1,0:T(8,128)(2,1)S(1)}, u32[]{:S(2)}, u32[]{:S(2)}) collective-permute-start(bf16[16,512]{1,0:T(8,128)(2,1)S(1)} %get-tuple-element.50), channel_id=1, source_target_pairs={{0,504},{8,0},{16,8},{24,16},{32,24},{40,32},{48,40},{56,48},{64,5... | collective-permute-start | bytes 49160 | tf_op jit(solution)/shard_map/ppermute | solution.py:294
  86.6 4.5 %collective-permute-start.10 = (bf16[16,512]{1,0:T(8,128)(2,1)S(1)}, bf16[16,512]{1,0:T(8,128)(2,1)S(1)}, u32[]{:S(2)}, u32[]{:S(2)}) collective-permute-start(bf16[16,512]{1,0:T(8,128)(2,1)S(1)} %get-tuple-element.51), channel_id=1, source_target_pairs={{0,8},{8,16},{16,24},{24,32},{32,40},{40,48},{48,56},{56,64},{64,7... | collective-permute-start | bytes 49160 | tf_op jit(solution)/shard_map/ppermute | solution.py:294
  141.5 7.7 %collective-permute-start.11 = (bf16[32,8,384]{2,1,0:T(8,128)(2,1)S(1)}, bf16[32,8,384]{2,1,0:T(8,128)(2,1)S(1)}, u32[]{:S(2)}, u32[]{:S(2)}) collective-permute-start(bf16[32,8,384]{2,1,0:T(8,128)(2,1)S(1)} %all_to_all.23.own), channel_id=1, source_target_pairs={{0,8},{8,0},{1,9},{9,1},{2,10},{10,2},{3,11},{11,3},{4,12},{12,4},... | collective-permute-start | bytes 589832 | tf_op jit(solution)/shard_map/ppermute | solution.py:298

commit v3 on v2

--- a/solution.py
+++ b/solution.py
@@ -57,12 +57,22 @@
     )(*args)
 
 
-def send_matrix_of(send_rows_ref):
-    rows = lax.broadcasted_iota(jnp.int32, (N, H), 0)
-    return (rows == send_rows_ref[...]).astype(F32).astype(BF)
-
-
-def prepare_kernel(count, senders, receivers, send_rows, rows, by_row, by_edge, sent):
+def ordered(core, outer, inner):
+    is_first = core[0, 0] == 0
+    outer, inner = outer[...], inner[...]
+    return jnp.where(is_first, outer, inner), jnp.where(is_first, inner, outer)
+
+
+def send_matrices_of(send_rows):
+    rows = lax.broadcasted_iota(jnp.int32, (N, H // 2), 0)
+    return [(rows == send_rows[0, i : i + 1, :]).astype(F32).astype(BF) for i in range(2)]
+
+
+def sent_of(send_rows, rows):
+    return jnp.concatenate([dot_tn(m, rows) for m in send_matrices_of(send_rows)], axis=0).astype(BF)
+
+
+def prepare_kernel(count, senders, receivers, send_rows, rows, by_row, by_edge, outer, inner):
     live = lax.broadcasted_iota(jnp.int32, (1, E), 1) < count[0, 0]
     ids = senders[...]
     ids = jnp.where(ids >= N + H // 2, ids + H, ids)
@@ -78,7 +88,9 @@
     by_edge[0] = (lane == ids_down).astype(F32).astype(BF)
     by_edge[1] = (lane == receivers_down).astype(F32).astype(BF)
     by_edge[2] = (lane == ids_down - N).astype(F32).astype(BF)
-    sent[...] = dot_tn(send_matrix_of(send_rows), rows[...]).astype(BF)
+    sent = sent_of(send_rows, rows[...])
+    outer[...] = sent
+    inner[...] = sent
 
 
 def weights_of(core, own, peer, layer):
@@ -145,27 +157,31 @@
 
 
 def first_layer_kernel(
-    core, rows, from_prev, from_next, own, peer, gain, by_row, by_edge, send_rows,
-    result, total_out, slope_out, sent,
+    core, rows, outer, inner, own, peer, gain, by_row, by_edge, send_rows,
+    result, total_out, slope_out, outer_out, inner_out,
 ):
+    from_prev, from_next = ordered(core, outer, inner)
     send_matrix, recv_matrix = weights_of(core, own, peer, 0)
     total, slope = forward(
-        rows[...], from_prev[...], from_next[...], send_matrix, recv_matrix, by_row, by_edge
+        rows[...], from_prev, from_next, send_matrix, recv_matrix, by_row, by_edge
     )
     total_out[...] = total
     slope_out[...] = slope
     new = (rows[...].astype(F32) + gain[0:1, :] * total * factor_of(total)).astype(BF)
     result[...] = new
-    sent[...] = dot_tn(send_matrix_of(send_rows), new).astype(BF)
+    sent = sent_of(send_rows, new)
+    outer_out[...] = sent
+    inner_out[...] = sent
 
 
 def last_layer_kernel(
-    core, rows, from_prev, from_next, own, peer, gain, by_row, by_edge, out_grad,
-    result, own_grad, to_prev, to_next, keep, give,
+    core, rows, outer, inner, own, peer, gain, by_row, by_edge, out_grad,
+    result, own_grad, outer_out, inner_out, keep, give,
 ):
+    from_prev, from_next = ordered(core, outer, inner)
     send_matrix, recv_matrix = weights_of(core, own, peer, 1)
     total, slope = forward(
-        rows[...], from_prev[...], from_next[...], send_matrix, recv_matrix, by_row, by_edge
+        rows[...], from_prev, from_next, send_matrix, recv_matrix, by_row, by_edge
     )
     gain_row = gain[1:2, :]
     result[...] = (rows[...].astype(F32) + gain_row * total * factor_of(total)).astype(BF)
@@ -174,30 +190,30 @@
         cotangent, total, slope, gain_row, send_matrix, recv_matrix, by_row, by_edge
     )
     own_grad[...] = grad + cotangent
-    to_prev[...] = prev_grad
-    to_next[...] = next_grad
+    outer_out[...], inner_out[...] = ordered(core, prev_grad, next_grad)
     keep[0:ROWS, :], give[0:ROWS, :] = halves(core, row_grad)
     keep[ROWS:DROWS, :], give[ROWS:DROWS, :] = halves(core, gain_block)
 
 
-def merged(own_grad, from_next, from_prev, send_rows):
-    back = (from_next[...].astype(F32) + from_prev[...].astype(F32)).astype(BF)
-    return (own_grad[...] + dot(send_matrix_of(send_rows), back)).astype(BF)
+def merged(own_grad, outer, inner, send_rows):
+    back = outer[...].astype(F32) + inner[...].astype(F32)
+    upper, lower = send_matrices_of(send_rows)
+    back = dot(upper, back[: H // 2].astype(BF)) + dot(lower, back[H // 2 :].astype(BF))
+    return (own_grad[...] + back).astype(BF)
 
 
 def back_kernel(
-    core, later_grad, back_next, back_prev, total, slope, own, peer, gain, by_row, by_edge, send_rows,
-    rows_0, prev_0, next_0, rows_1, prev_1, next_1, later_keep, later_give,
-    own_grad, to_prev, to_next, keep, pack,
+    core, later_grad, outer, inner, total, slope, own, peer, gain, by_row, by_edge, send_rows,
+    rows_0, outer_0, inner_0, rows_1, outer_1, inner_1, later_keep, later_give,
+    own_grad, outer_out, inner_out, keep, pack,
 ):
     send_matrix, recv_matrix = weights_of(core, own, peer, 0)
-    cotangent = merged(later_grad, back_next, back_prev, send_rows).astype(F32)
+    cotangent = merged(later_grad, outer, inner, send_rows).astype(F32)
     grad, prev_grad, next_grad, row_grad, gain_block = backward(
         cotangent, total[...], slope[...], gain[0:1, :], send_matrix, recv_matrix, by_row, by_edge
     )
     own_grad[...] = grad + cotangent
-    to_prev[...] = prev_grad
-    to_next[...] = next_grad
+    outer_out[...], inner_out[...] = ordered(core, prev_grad, next_grad)
     base = 2 * EXT
     keep_rows, give_rows = halves(core, row_grad)
     keep_gain, give_gain = halves(core, gain_block)
@@ -207,15 +223,16 @@
     pack[base : base + ROWS, 0:HALF] = give_rows
     pack[base + ROWS : base + DROWS, 0:HALF] = give_gain
     pack[base : base + DROWS, HALF:D] = later_give[...]
-    for layer, parts in enumerate(((rows_0, prev_0, next_0), (rows_1, prev_1, next_1))):
+    for layer, parts in enumerate(((rows_0, outer_0, inner_0), (rows_1, outer_1, inner_1))):
         start = layer * EXT
         pack[start : start + N, :] = parts[0][...]
-        pack[start + N : start + N + H, :] = parts[1][...]
-        pack[start + N + H : start + EXT, :] = parts[2][...]
-
-
-def merge_kernel(own_grad, back_next, back_prev, send_rows, result):
-    result[...] = merged(own_grad, back_next, back_prev, send_rows)
+        from_prev, from_next = ordered(core, *parts[1:])
+        pack[start + N : start + N + H, :] = from_prev
+        pack[start + N + H : start + EXT, :] = from_next
+
+
+def merge_kernel(own_grad, outer, inner, send_rows, result):
+    result[...] = merged(own_grad, outer, inner, send_rows)
 
 
 def terms_kernel(pack, keep, peer, chunks):
@@ -290,12 +307,13 @@
 GRAPH = ("y", "zl", "c")
 
 
-def shift(value, steps):
-    return lax.ppermute(value, GRAPH, [(i, (i + steps) % 64) for i in range(64)])
-
-
 def swap(value, axis):
     return lax.ppermute(value, axis, [(0, 1), (1, 0)])
+
+
+def exchange(outer, inner):
+    pairs = [(i, (i + 1) % 64 if i % 2 else (i - 1) % 64) for i in range(64)]
+    return lax.ppermute(outer, GRAPH, pairs), swap(inner, "c")
 
 
 def shards(
@@ -303,57 +321,56 @@
 ):
     core = lax.axis_index("c").astype(jnp.int32).reshape(1, 1)
     features = node_features[0]
-    targets = send_rows.reshape(1, H)
     half = jnp.where(lax.axis_index("c") == 0, send_weight, recv_weight)
     other = lax.ppermute(half, ("zl", "zh"), [(i, 7 - i) for i in range(8)])
-    by_row, by_edge, sent_0 = call(
+    by_row, by_edge, *sent = call(
         prepare_kernel,
-        [((ROWS, E), BF), ((3, E, N), BF), ((H, D), BF)],
+        [((ROWS, E), BF), ((3, E, N), BF), ((H, D), BF), ((H, D), BF)],
         "prepare",
-        edge_count.reshape(1, 1), senders, receivers, targets, features,
-    )
-    other, prev_0, next_0 = lax.optimization_barrier((other, shift(sent_0, 1), shift(sent_0, -1)))
+        edge_count.reshape(1, 1), senders, receivers, send_rows, features,
+    )
     is_low = lax.axis_index("zh") == 0
     both = jnp.stack([jnp.where(is_low, half, other), jnp.where(is_low, other, half)])
     copies = jnp.broadcast_to(both[None], (4,) + both.shape)
     own = lax.all_to_all(copies, ("x",), 0, 0, tiled=True)
+    own, *halo_0 = lax.optimization_barrier((own, *exchange(*sent)))
     peer = swap(own, "c")
 
-    rows_1, total_0, slope_0, sent_1 = call(
+    rows_1, total_0, slope_0, *sent = call(
         first_layer_kernel,
-        [((N, D), BF), ((N, D), F32), ((E, D), F32), ((H, D), BF)],
+        [((N, D), BF), ((N, D), F32), ((E, D), F32), ((H, D), BF), ((H, D), BF)],
         "first_layer",
-        core, features, prev_0, next_0, own, peer, gain, by_row, by_edge, targets,
-    )
-    prev_1, next_1 = shift(sent_1, 1), shift(sent_1, -1)
-    updated, grad_1, to_prev, to_next, keep_1, give_1 = call(
+        core, features, *halo_0, own, peer, gain, by_row, by_edge, send_rows,
+    )
+    halo_1 = exchange(*sent)
+    updated, grad_1, outer, inner, keep_1, give_1 = call(
         last_layer_kernel,
         [((N, D), BF), ((N, D), F32), ((H, D), BF), ((H, D), BF), ((DROWS, HALF), BF), ((DROWS, HALF), BF)],
         "last_layer",
-        core, rows_1, prev_1, next_1, own, peer, gain, by_row, by_edge, out_grad[0],
-    )
-    back_next, back_prev = shift(to_prev, -1), shift(to_next, 1)
-    grad_0, to_prev, to_next, keep, pack = call(
+        core, rows_1, *halo_1, own, peer, gain, by_row, by_edge, out_grad[0],
+    )
+    back = exchange(outer, inner)
+    grad_0, outer, inner, keep, pack = call(
         back_kernel,
         [((N, D), F32), ((H, D), BF), ((H, D), BF), ((DROWS, D), BF), ((2 * EXT + DROWS, D), BF)],
         "back",
-        core, grad_1, back_next, back_prev, total_0, slope_0, own, peer, gain, by_row, by_edge,
-        targets, features, prev_0, next_0, rows_1, prev_1, next_1, keep_1, give_1,
+        core, grad_1, *back, total_0, slope_0, own, peer, gain, by_row, by_edge,
+        send_rows, features, *halo_0, rows_1, *halo_1, keep_1, give_1,
     )
     peer_pack = swap(pack, "c")
-    back_next, back_prev = shift(to_prev, -1), shift(to_next, 1)
-    peer_pack, back_next, back_prev = lax.optimization_barrier((peer_pack, back_next, back_prev))
     (chunks,) = call(terms_kernel, [((4, 528, HALF), BF)], "terms", pack, keep, peer_pack)
     parts = lax.all_to_all(chunks, ("x",), 0, 0, tiled=True)
     (pieces,) = call(first_sum_kernel, [((PARTS, 8, HALF + 128), BF)], "first_sum", parts)
     parts = lax.all_to_all(pieces, ("y", "zh", "zl"), 0, 0, tiled=True)
+    parts, outer, inner = lax.optimization_barrier((parts, outer, inner))
     (copies,) = call(second_sum_kernel, [((32, 8, HALF + 128), BF)], "second_sum", parts)
     mine = lax.all_to_all(copies, ("y", "zl"), 0, 0, tiled=True)
+    mine, *back = lax.optimization_barrier((mine, *exchange(outer, inner)))
     theirs = swap(mine, "c")
     send_grad, recv_grad, gain_grad = call(
         spread_kernel, [((2, 64, D), F32), ((2, 64, D), F32), ((2, D), F32)], "spread", core, mine, theirs
     )
-    (feature_grad,) = call(merge_kernel, [((N, D), BF)], "merge", grad_0, back_next, back_prev, targets)
+    (feature_grad,) = call(merge_kernel, [((N, D), BF)], "merge", grad_0, *back, send_rows)
     return updated[None], feature_grad[None], send_grad, recv_grad, gain_grad
 
 

time: 151 us -> 139 us (0.921)
  blocking collectives: 63.1 us -> 39.2 us
  waiting for transfers between devices: 9.63 us -> 20.4 us
  starting transfers between devices: 62.9 us -> 65.3 us
  local copies, waits for them, and re-layouts: 3.14 us -> 1.14 us
    all_to_all x2 -> x0, blocking collectives: 28.7 us -> none  [the longest x1 15 us: shards(): mine = lax.all_to_all(copies, ('y', 'zl'), 0, 0, tiled=True)]
    ppermute x8 -> x4, starting transfers between devices: 27.2 us -> 10.5 us  [exchange(): return (lax.ppermute(outer, GRAPH, pairs), swap(inner, 'c'))]
    all_to_all x0 -> x2, starting transfers between devices: none -> 10.9 us  [the longest x1 6.73 us: shards(): mine = lax.all_to_all(copies, ('y', 'zl'), 0, 0, tiled=True)]
    ppermute x3 -> x7, starting transfers between devices: 24.1 us -> 32.4 us  [swap(): return lax.ppermute(value, axis, [(0, 1), (1, 0)])]
    ppermute x8 -> x4, waiting for transfers between devices: 7.13 us -> 0.01 us  [exchange(): return (lax.ppermute(outer, GRAPH, pairs), swap(inner, 'c'))]
    ppermute x1, waiting for transfers between devices: 0.01 us -> 6.75 us  [shards(): other = lax.ppermute(half, ('zl', 'zh'), [(i, 7 - i) for i in range(8)])]
    all_to_all x0 -> x2, waiting for transfers between devices: none -> 6.29 us  [the longest x1 6 us: shards(): own = lax.all_to_all(copies, ('x',), 0, 0, tiled=True)]
    ppermute x3 -> x7, waiting for transfers between devices: 2.49 us -> 7.35 us  [swap(): return lax.ppermute(value, axis, [(0, 1), (1, 0)])]
  transfers between devices with their start and end apart: 12 -> 14, of which waited for: 6 -> 10; matrix products, arithmetic and copies ran while one was open for 1% -> 0% of each run, Pallas kernels for 1% -> 1%
where the time goes in v3:
time: 139 us; the launch traced here: 138 us
  starting transfers between devices  65.3 us (47%)
  blocking collectives  39.2 us (28%)
  waiting for transfers between devices  20.4 us (15%)
  Pallas kernels  9.52 us (7%)
  between operations  1.52 us (1%)
    ppermute x7, starting transfers between devices, swap(): return lax.ppermute(value, axis, [(0, 1), (1, 0)])  32.4 us
    all_to_all x1, blocking collectives, shards(): parts = lax.all_to_all(pieces, ('y', 'zh', 'zl'), 0, 0, tiled=True)  21.8 us
    all_to_all x1, blocking collectives, shards(): parts = lax.all_to_all(chunks, ('x',), 0, 0, tiled=True)  17.4 us
    ppermute x1, starting transfers between devices, shards(): other = lax.ppermute(half, ('zl', 'zh'), [(i, 7 - i) for i in range(8)])  11.5 us
    ppermute x4, starting transfers between devices, exchange(): return (lax.ppermute(outer, GRAPH, pairs), swap(inner, 'c'))  10.5 us
    pallas_call x9, Pallas kernels, call(): pl.pallas_call(kernel, out_shape=[jax.ShapeDtypeStruct(s, t) for s, t in...  9.52 us
    ppermute x7, waiting for transfers between devices, swap(): return lax.ppermute(value, axis, [(0, 1), (1, 0)])  7.35 us
    ppermute x1, waiting for transfers between devices, shards(): other = lax.ppermute(half, ('zl', 'zh'), [(i, 7 - i) for i in range(8)])  6.75 us
  transfers between devices with their start and end apart: 14, of which 10 were waited for; matrix products, arithmetic and copies ran while one was open for 0% of the time, Pallas kernels for 1%

profile of v3, /device:TPU:1, one launch (start us, length us, event | category | flops | bytes accessed | tf_op | source)
XLA Modules:
  0.0 138.1 jit_solution(4511317528672885761)
XLA Ops:
  1.6 11.5 %collective-permute-start = (bf16[2,64,512]{2,1,0:T(8,128)(2,1)S(1)}, bf16[2,64,512]{2,1,0:T(8,128)(2,1)S(1)}, u32[]{:S(2)}, u32[]{:S(2)}) collective-permute-start(bf16[2,64,512]{2,1,0:T(8,128)(2,1)S(1)} %broadcast_select_fusion), channel_id=1, source_target_pairs={{0,52},{4,48},{16,36},{20,32},{32,20},{36,16},{48,4},{52,0},{1,53}... | collective-permute-start | bytes 393224 | tf_op jit(solution)/shard_map/ppermute | solution.py:325
  13.1 6.8 %collective-permute-done = bf16[2,64,512]{2,1,0:T(8,128)(2,1)S(1)} collective-permute-done((bf16[2,64,512]{2,1,0:T(8,128)(2,1)S(1)}, bf16[2,64,512]{2,1,0:T(8,128)(2,1)S(1)}, u32[]{:S(2)}, u32[]{:S(2)}) %collective-permute-start) | collective-permute-done | bytes 131104 | tf_op jit(solution)/shard_map/ppermute | solution.py:325
  19.9 1.1 broadcast_in_dim.12
  21.0 4.2 %all-to-all-start = ((bf16[4,2,2,64,512]{4,3,2,1,0:T(8,128)(2,1)}), bf16[4,2,2,64,512]{4,3,2,1,0:T(8,128)(2,1)S(1)}, u32[]{:S(2)}, u32[]{:S(2)}) async-start(bf16[4,2,2,64,512]{4,3,2,1,0:T(8,128)(2,1)} %broadcast_in_dim.12), calls=%async_computation | async-start | bytes 2097152 | tf_op jit(solution)/shard_map/all_to_all | solution.py:335
  26.1 1.9 %collective-permute-start.1 = (bf16[16,512]{1,0:T(8,128)(2,1)S(1)}, bf16[16,512]{1,0:T(8,128)(2,1)S(1)}, u32[]{:S(2)}, u32[]{:S(2)}) collective-permute-start(bf16[16,512]{1,0:T(8,128)(2,1)S(1)} %get-tuple-element.37), channel_id=1, source_target_pairs={{0,504},{8,16},{16,8},{24,32},{32,24},{40,48},{48,40},{56,64},{64,... | collective-permute-start | bytes 49160 | tf_op jit(solution)/shard_map/ppermute | solution.py:316
  28.1 4.7 %collective-permute-start.2 = (bf16[16,512]{1,0:T(8,128)(2,1)S(1)}, bf16[16,512]{1,0:T(8,128)(2,1)S(1)}, u32[]{:S(2)}, u32[]{:S(2)}) collective-permute-start(bf16[16,512]{1,0:T(8,128)(2,1)S(1)} %get-tuple-element.38), channel_id=1, source_target_pairs={{0,8},{8,0},{1,9},{9,1},{2,10},{10,2},{3,11},{11,3},{4,12},{12,4},... | collective-permute-start | bytes 49160 | tf_op jit(solution)/shard_map/ppermute | solution.py:311
  33.6 6.0 %all-to-all-done.own = bf16[4,2,2,64,512]{4,3,2,1,0:T(8,128)(2,1)S(1)} async-done(((bf16[4,2,2,64,512]{4,3,2,1,0:T(8,128)(2,1)}), bf16[4,2,2,64,512]{4,3,2,1,0:T(8,128)(2,1)S(1)}, u32[]{:S(2)}, u32[]{:S(2)}) %all-to-all-start) | async-done | bytes 1048608 | tf_op jit(solution)/shard_map/all_to_all | solution.py:335
  39.6 3.5 %collective-permute-start.3 = (bf16[4,2,2,64,512]{4,3,2,1,0:T(8,128)(2,1)S(1)}, bf16[4,2,2,64,512]{4,3,2,1,0:T(8,128)(2,1)S(1)}, u32[]{:S(2)}, u32[]{:S(2)}) collective-permute-start(bf16[4,2,2,64,512]{4,3,2,1,0:T(8,128)(2,1)S(1)} %all-to-all-done.own), channel_id=1, source_target_pairs={{0,8},{8,0},{1,9},{9,1},{2,10},{10,2},{3,11},{11,3},{4,12},{12,4},... | collective-permute-start | bytes 3145736 | tf_op jit(solution)/shard_map/ppermute | solution.py:311
  43.2 2.3 %collective-permute-done.3.peer = bf16[4,2,2,64,512]{4,3,2,1,0:T(8,128)(2,1)S(1)} collective-permute-done((bf16[4,2,2,64,512]{4,3,2,1,0:T(8,128)(2,1)S(1)}, bf16[4,2,2,64,512]{4,3,2,1,0:T(8,128)(2,1)S(1)}, u32[]{:S(2)}, u32[]{:S(2)}) %collective-permute-start.3) | collective-permute-done | bytes 1048608 | tf_op jit(solution)/shard_map/ppermute | solution.py:311
  45.4 1.7 %first_layer.1 = (bf16[128,512]{1,0:T(8,128)(2,1)S(1)}, f32[128,512]{1,0:T(8,128)S(1)}, f32[512,512]{1,0:T(8,128)S(1)}, bf16[16,512]{1,0:T(8,128)(2,1)S(1)}, bf16[16,512]{1,0:T(8,128)(2,1)S(1)}) custom-call(s32[1,1]{1,0:T(1,128)} %bitcast.core, bf16[128,512]{1,0:T(8,128)(2,1)S(1)} %bitcast.12, bf16[16,512]{1,0:T(8,128)(2,1)S(1)} %collective-permute-done.1.outer.outer_0, ...), custom_call_target="tpu_custom_call" | custom-call | flops 100000000 | bytes 2000000 | tf_op jit(solution)/shard_map/first_layer/pallas_call | solution.py:49
  47.1 1.9 %collective-permute-start.4 = (bf16[16,512]{1,0:T(8,128)(2,1)S(1)}, bf16[16,512]{1,0:T(8,128)(2,1)S(1)}, u32[]{:S(2)}, u32[]{:S(2)}) collective-permute-start(bf16[16,512]{1,0:T(8,128)(2,1)S(1)} %get-tuple-element.45), channel_id=1, source_target_pairs={{0,504},{8,16},{16,8},{24,32},{32,24},{40,48},{48,40},{56,64},{64,... | collective-permute-start | bytes 49160 | tf_op jit(solution)/shard_map/ppermute | solution.py:316
  49.0 4.7 %collective-permute-start.5 = (bf16[16,512]{1,0:T(8,128)(2,1)S(1)}, bf16[16,512]{1,0:T(8,128)(2,1)S(1)}, u32[]{:S(2)}, u32[]{:S(2)}) collective-permute-start(bf16[16,512]{1,0:T(8,128)(2,1)S(1)} %get-tuple-element.46), channel_id=1, source_target_pairs={{0,8},{8,0},{1,9},{9,1},{2,10},{10,2},{3,11},{11,3},{4,12},{12,4},... | collective-permute-start | bytes 49160 | tf_op jit(solution)/shard_map/ppermute | solution.py:311
  54.6 3.0 %last_layer.1 = (bf16[128,512]{1,0:T(8,128)(2,1)}, f32[128,512]{1,0:T(8,128)S(1)}, bf16[16,512]{1,0:T(8,128)(2,1)S(1)}, bf16[16,512]{1,0:T(8,128)(2,1)S(1)}, bf1...) custom-call(s32[1,1]{1,0:T(1,128)} %bitcast.core, bf16[128,512]{1,0:T(8,128)(2,1)S(1)} %get-tuple-element.44.rows.rows_1, ...), custom_call_target="tpu_custom_call" | custom-call | flops 100000000 | bytes 2000000 | tf_op jit(solution)/shard_map/last_layer/pallas_call | solution.py:49
  57.6 1.9 %collective-permute-start.6 = (bf16[16,512]{1,0:T(8,128)(2,1)S(1)}, bf16[16,512]{1,0:T(8,128)(2,1)S(1)}, u32[]{:S(2)}, u32[]{:S(2)}) collective-permute-start(bf16[16,512]{1,0:T(8,128)(2,1)S(1)} %get-tuple-element.49), channel_id=1, source_target_pairs={{0,504},{8,16},{16,8},{24,32},{32,24},{40,48},{48,40},{56,64},{64,... | collective-permute-start | bytes 49160 | tf_op jit(solution)/shard_map/ppermute | solution.py:316
  59.5 6.2 %collective-permute-start.7 = (bf16[16,512]{1,0:T(8,128)(2,1)S(1)}, bf16[16,512]{1,0:T(8,128)(2,1)S(1)}, u32[]{:S(2)}, u32[]{:S(2)}) collective-permute-start(bf16[16,512]{1,0:T(8,128)(2,1)S(1)} %get-tuple-element.50), channel_id=1, source_target_pairs={{0,8},{8,0},{1,9},{9,1},{2,10},{10,2},{3,11},{11,3},{4,12},{12,4},... | collective-permute-start | bytes 49160 | tf_op jit(solution)/shard_map/ppermute | solution.py:311
  66.6 1.3 back.1
  67.9 3.8 %collective-permute-start.8 = (bf16[624,512]{1,0:T(8,128)(2,1)S(1)}, bf16[624,512]{1,0:T(8,128)(2,1)S(1)}, u32[]{:S(2)}, u32[]{:S(2)}) collective-permute-start(bf16[624,512]{1,0:T(8,128)(2,1)S(1)} %get-tuple-element.56.pack), channel_id=1, source_target_pairs={{0,8},{8,0},{1,9},{9,1},{2,10},{10,2},{3,11},{11,3},{4,12},{12,4},... | collective-permute-start | bytes 1916936 | tf_op jit(solution)/shard_map/ppermute | solution.py:311
  71.7 1.7 %collective-permute-done.8.peer = bf16[624,512]{1,0:T(8,128)(2,1)S(1)} collective-permute-done((bf16[624,512]{1,0:T(8,128)(2,1)S(1)}, bf16[624,512]{1,0:T(8,128)(2,1)S(1)}, u32[]{:S(2)}, u32[]{:S(2)}) %collective-permute-start.8) | collective-permute-done | bytes 639008 | tf_op jit(solution)/shard_map/ppermute | solution.py:311
  74.0 17.4 %all_to_all.20.parts = bf16[4,528,256]{2,1,0:T(8,128)(2,1)S(1)} all-to-all(bf16[4,528,256]{2,1,0:T(8,128)(2,1)S(1)} %terms.1), channel_id=1, replica_groups=mesh['y'=8,'zl'=4,'c'=2,'zh'=2,'x'=4] {'x'}, dimensions={0} | all-to-all | bytes 2162688 | tf_op jit(solution)/shard_map/all_to_all | solution.py:362
  91.6 21.8 %all_to_all.21.parts = bf16[64,8,384]{2,1,0:T(8,128)(2,1)S(1)} all-to-all(bf16[64,8,384]{2,1,0:T(8,128)(2,1)S(1)} %first_sum.1), channel_id=1, replica_groups=mesh['y'=8,'zl'=4,'c'=2,'zh'=2,'x'=4] {'y','zh','zl'}, dimensions={0} | all-to-all | bytes 786432 | tf_op jit(solution)/shard_map/all_to_all | solution.py:364
  114.2 6.7 %all-to-all-start.3 = ((bf16[32,8,384]{2,1,0:T(8,128)(2,1)}), bf16[32,8,384]{2,1,0:T(8,128)(2,1)S(1)}, u32[]{:S(2)}, u32[]{:S(2)}) async-start(bf16[32,8,384]{2,1,0:T(8,128)(2,1)} %second_sum.1), calls=%async_computation.3 | async-start | bytes 393216 | tf_op jit(solution)/shard_map/all_to_all | solution.py:367
  120.9 4.8 %collective-permute-start.9 = (bf16[16,512]{1,0:T(8,128)(2,1)S(1)}, bf16[16,512]{1,0:T(8,128)(2,1)S(1)}, u32[]{:S(2)}, u32[]{:S(2)}) collective-permute-start(bf16[16,512]{1,0:T(8,128)(2,1)S(1)} %get-tuple-element.61), channel_id=1, source_target_pairs={{0,504},{8,16},{16,8},{24,32},{32,24},{40,48},{48,40},{56,64},{64,... | collective-permute-start | bytes 49160 | tf_op jit(solution)/shard_map/ppermute | solution.py:316
  125.7 4.7 %collective-permute-start.10 = (bf16[16,512]{1,0:T(8,128)(2,1)S(1)}, bf16[16,512]{1,0:T(8,128)(2,1)S(1)}, u32[]{:S(2)}, u32[]{:S(2)}) collective-permute-start(bf16[16,512]{1,0:T(8,128)(2,1)S(1)} %get-tuple-element.62), channel_id=1, source_target_pairs={{0,8},{8,0},{1,9},{9,1},{2,10},{10,2},{3,11},{11,3},{4,12},{12,4},... | collective-permute-start | bytes 49160 | tf_op jit(solution)/shard_map/ppermute | solution.py:311
  131.5 4.8 %collective-permute-start.11 = (bf16[32,8,384]{2,1,0:T(8,128)(2,1)S(1)}, bf16[32,8,384]{2,1,0:T(8,128)(2,1)S(1)}, u32[]{:S(2)}, u32[]{:S(2)}) collective-permute-start(bf16[32,8,384]{2,1,0:T(8,128)(2,1)S(1)} %all-to-all-done.3.own), channel_id=1, source_target_pairs={{0,8},{8,0},{1,9},{9,1},{2,10},{10,2},{3,11},{11,3},{4,12},{12,4},... | collective-permute-start | bytes 589832 | tf_op jit(solution)/shard_map/ppermute | solution.py:311
  (31 shorter events, 8.2 us)
Async XLA Ops:
  1.6 18.3 %collective-permute-start = (bf16[2,64,512]{2,1,0:T(8,128)(2,1)S(1)}, bf16[2,64,512]{2,1,0:T(8,128)(2,1)S(1)}, u32[]{:S(2)}, u32[]{:S(2)}) collective-permute-start(bf16[2,64,512]{2,1,0:T(8,128)(2,1)S(1)} %broadcast_select_fusion), channel_id=1, source_target_pairs={{0,52},{4,48},{16,36},{20,32},{32,20},{36,16},{48,4},{52,0},{1,53}... | collective-permute-start | bytes 393224 | tf_op jit(solution)/shard_map/ppermute | solution.py:325
  21.0 4.8 %copy-start = (bf16[1,128,512]{2,1,0:T(8,128)(2,1)S(1)}, bf16[1,128,512]{2,1,0:T(8,128)(2,1)}, u32[]{:S(2)}) copy-start(bf16[1,128,512]{2,1,0:T(8,128)(2,1)} %param.9) | copy-start | bytes 393220
  21.0 4.8 %copy-start.3 = (s32[1,2,8]{2,1,0:T(2,128)S(1)}, s32[1,2,8]{2,1,0:T(2,128)}, u32[]{:S(2)}) copy-start(s32[1,2,8]{2,1,0:T(2,128)} %send_rows.7) | copy-start | bytes 196
  21.0 4.8 %copy-start.4 = (s32[1,512]{1,0:T(1,128)S(1)}, s32[1,512]{1,0:T(1,128)}, u32[]{:S(2)}) copy-start(s32[1,512]{1,0:T(1,128)} %senders.1) | copy-start | bytes 6148
  21.0 4.9 %copy-start.5 = (s32[1,512]{1,0:T(1,128)S(1)}, s32[1,512]{1,0:T(1,128)}, u32[]{:S(2)}) copy-start(s32[1,512]{1,0:T(1,128)} %receivers.1) | copy-start | bytes 6148
  21.0 24.4 %copy-start.2 = (f32[2,512]{1,0:T(2,128)S(1)}, f32[2,512]{1,0:T(2,128)}, u32[]{:S(2)}) copy-start(f32[2,512]{1,0:T(2,128)} %gain.5) | copy-start | bytes 12292
  21.0 18.6 %all-to-all-start = ((bf16[4,2,2,64,512]{4,3,2,1,0:T(8,128)(2,1)}), bf16[4,2,2,64,512]{4,3,2,1,0:T(8,128)(2,1)S(1)}, u32[]{:S(2)}, u32[]{:S(2)}) async-start(bf16[4,2,2,64,512]{4,3,2,1,0:T(8,128)(2,1)} %broadcast_in_dim.12), calls=%async_computation | async-start | bytes 2097152 | tf_op jit(solution)/shard_map/all_to_all | solution.py:335
  26.1 6.6 %collective-permute-start.1 = (bf16[16,512]{1,0:T(8,128)(2,1)S(1)}, bf16[16,512]{1,0:T(8,128)(2,1)S(1)}, u32[]{:S(2)}, u32[]{:S(2)}) collective-permute-start(bf16[16,512]{1,0:T(8,128)(2,1)S(1)} %get-tuple-element.37), channel_id=1, source_target_pairs={{0,504},{8,16},{16,8},{24,32},{32,24},{40,48},{48,40},{56,64},{64,... | collective-permute-start | bytes 49160 | tf_op jit(solution)/shard_map/ppermute | solution.py:316
  28.1 5.5 %collective-permute-start.2 = (bf16[16,512]{1,0:T(8,128)(2,1)S(1)}, bf16[16,512]{1,0:T(8,128)(2,1)S(1)}, u32[]{:S(2)}, u32[]{:S(2)}) collective-permute-start(bf16[16,512]{1,0:T(8,128)(2,1)S(1)} %get-tuple-element.38), channel_id=1, source_target_pairs={{0,8},{8,0},{1,9},{9,1},{2,10},{10,2},{3,11},{11,3},{4,12},{12,4},... | collective-permute-start | bytes 49160 | tf_op jit(solution)/shard_map/ppermute | solution.py:311
  39.6 5.8 %collective-permute-start.3 = (bf16[4,2,2,64,512]{4,3,2,1,0:T(8,128)(2,1)S(1)}, bf16[4,2,2,64,512]{4,3,2,1,0:T(8,128)(2,1)S(1)}, u32[]{:S(2)}, u32[]{:S(2)}) collective-permute-start(bf16[4,2,2,64,512]{4,3,2,1,0:T(8,128)(2,1)S(1)} %all-to-all-done.own), channel_id=1, source_target_pairs={{0,8},{8,0},{1,9},{9,1},{2,10},{10,2},{3,11},{11,3},{4,12},{12,4},... | collective-permute-start | bytes 3145736 | tf_op jit(solution)/shard_map/ppermute | solution.py:311
  45.4 9.1 %copy-start.1 = (bf16[1,128,512]{2,1,0:T(8,128)(2,1)S(1)}, bf16[1,128,512]{2,1,0:T(8,128)(2,1)}, u32[]{:S(2)}) copy-start(bf16[1,128,512]{2,1,0:T(8,128)(2,1)} %param.10) | copy-start | bytes 393220
  47.1 6.6 %collective-permute-start.4 = (bf16[16,512]{1,0:T(8,128)(2,1)S(1)}, bf16[16,512]{1,0:T(8,128)(2,1)S(1)}, u32[]{:S(2)}, u32[]{:S(2)}) collective-permute-start(bf16[16,512]{1,0:T(8,128)(2,1)S(1)} %get-tuple-element.45), channel_id=1, source_target_pairs={{0,504},{8,16},{16,8},{24,32},{32,24},{40,48},{48,40},{56,64},{64,... | collective-permute-start | bytes 49160 | tf_op jit(solution)/shard_map/ppermute | solution.py:316
  49.0 5.5 %collective-permute-start.5 = (bf16[16,512]{1,0:T(8,128)(2,1)S(1)}, bf16[16,512]{1,0:T(8,128)(2,1)S(1)}, u32[]{:S(2)}, u32[]{:S(2)}) collective-permute-start(bf16[16,512]{1,0:T(8,128)(2,1)S(1)} %get-tuple-element.46), channel_id=1, source_target_pairs={{0,8},{8,0},{1,9},{9,1},{2,10},{10,2},{3,11},{11,3},{4,12},{12,4},... | collective-permute-start | bytes 49160 | tf_op jit(solution)/shard_map/ppermute | solution.py:311
  57.6 8.1 %collective-permute-start.6 = (bf16[16,512]{1,0:T(8,128)(2,1)S(1)}, bf16[16,512]{1,0:T(8,128)(2,1)S(1)}, u32[]{:S(2)}, u32[]{:S(2)}) collective-permute-start(bf16[16,512]{1,0:T(8,128)(2,1)S(1)} %get-tuple-element.49), channel_id=1, source_target_pairs={{0,504},{8,16},{16,8},{24,32},{32,24},{40,48},{48,40},{56,64},{64,... | collective-permute-start | bytes 49160 | tf_op jit(solution)/shard_map/ppermute | solution.py:316
  59.5 7.0 %collective-permute-start.7 = (bf16[16,512]{1,0:T(8,128)(2,1)S(1)}, bf16[16,512]{1,0:T(8,128)(2,1)S(1)}, u32[]{:S(2)}, u32[]{:S(2)}) collective-permute-start(bf16[16,512]{1,0:T(8,128)(2,1)S(1)} %get-tuple-element.50), channel_id=1, source_target_pairs={{0,8},{8,0},{1,9},{9,1},{2,10},{10,2},{3,11},{11,3},{4,12},{12,4},... | collective-permute-start | bytes 49160 | tf_op jit(solution)/shard_map/ppermute | solution.py:311
  67.9 5.5 %collective-permute-start.8 = (bf16[624,512]{1,0:T(8,128)(2,1)S(1)}, bf16[624,512]{1,0:T(8,128)(2,1)S(1)}, u32[]{:S(2)}, u32[]{:S(2)}) collective-permute-start(bf16[624,512]{1,0:T(8,128)(2,1)S(1)} %get-tuple-element.56.pack), channel_id=1, source_target_pairs={{0,8},{8,0},{1,9},{9,1},{2,10},{10,2},{3,11},{11,3},{4,12},{12,4},... | collective-permute-start | bytes 1916936 | tf_op jit(solution)/shard_map/ppermute | solution.py:311
  114.2 17.3 %all-to-all-start.3 = ((bf16[32,8,384]{2,1,0:T(8,128)(2,1)}), bf16[32,8,384]{2,1,0:T(8,128)(2,1)S(1)}, u32[]{:S(2)}, u32[]{:S(2)}) async-start(bf16[32,8,384]{2,1,0:T(8,128)(2,1)} %second_sum.1), calls=%async_computation.3 | async-start | bytes 393216 | tf_op jit(solution)/shard_map/all_to_all | solution.py:367
  120.9 9.5 %collective-permute-start.9 = (bf16[16,512]{1,0:T(8,128)(2,1)S(1)}, bf16[16,512]{1,0:T(8,128)(2,1)S(1)}, u32[]{:S(2)}, u32[]{:S(2)}) collective-permute-start(bf16[16,512]{1,0:T(8,128)(2,1)S(1)} %get-tuple-element.61), channel_id=1, source_target_pairs={{0,504},{8,16},{16,8},{24,32},{32,24},{40,48},{48,40},{56,64},{64,... | collective-permute-start | bytes 49160 | tf_op jit(solution)/shard_map/ppermute | solution.py:316
  125.7 5.5 %collective-permute-start.10 = (bf16[16,512]{1,0:T(8,128)(2,1)S(1)}, bf16[16,512]{1,0:T(8,128)(2,1)S(1)}, u32[]{:S(2)}, u32[]{:S(2)}) collective-permute-start(bf16[16,512]{1,0:T(8,128)(2,1)S(1)} %get-tuple-element.62), channel_id=1, source_target_pairs={{0,8},{8,0},{1,9},{9,1},{2,10},{10,2},{3,11},{11,3},{4,12},{12,4},... | collective-permute-start | bytes 49160 | tf_op jit(solution)/shard_map/ppermute | solution.py:311
  131.5 5.8 %collective-permute-start.11 = (bf16[32,8,384]{2,1,0:T(8,128)(2,1)S(1)}, bf16[32,8,384]{2,1,0:T(8,128)(2,1)S(1)}, u32[]{:S(2)}, u32[]{:S(2)}) collective-permute-start(bf16[32,8,384]{2,1,0:T(8,128)(2,1)S(1)} %all-to-all-done.3.own), channel_id=1, source_target_pairs={{0,8},{8,0},{1,9},{9,1},{2,10},{10,2},{3,11},{11,3},{4,12},{12,4},... | collective-permute-start | bytes 589832 | tf_op jit(solution)/shard_map/ppermute | solution.py:311

commit v4 on v3

--- a/solution.py
+++ b/solution.py
@@ -19,6 +19,7 @@
 ROWS = EXT + N
 HALF = D // 2
 DROWS = ROWS + 16
+CHUNK = 32
 PARTS = 64
 
 BF = jnp.bfloat16
@@ -85,9 +86,14 @@
     ids_down = jnp.broadcast_to(ids, (N, E)).T
     receivers_down = jnp.broadcast_to(receiver_ids, (N, E)).T
     lane = lax.broadcasted_iota(jnp.int32, (E, N), 1)
-    by_edge[0] = (lane == ids_down).astype(F32).astype(BF)
-    by_edge[1] = (lane == receivers_down).astype(F32).astype(BF)
-    by_edge[2] = (lane == ids_down - N).astype(F32).astype(BF)
+    own = (lane == ids_down).astype(F32).astype(BF)
+    receive = (lane == receivers_down).astype(F32).astype(BF)
+    by_edge[:, 0:N] = own
+    by_edge[:, N : 2 * N] = own
+    by_edge[:, 2 * N : 3 * N] = receive
+    by_edge[:, 3 * N : 4 * N] = receive
+    halo = (ids_down >= N) & ((lane == ids_down - N) | (lane == ids_down - N + 2 * H))
+    by_edge[:, 4 * N :] = halo.astype(F32).astype(BF)
     sent = sent_of(send_rows, rows[...])
     outer[...] = sent
     inner[...] = sent
@@ -108,23 +114,20 @@
     proj_recv = dot(rows, recv_matrix)
     send_high, send_low = split(proj_send)
     recv_high, recv_low = split(proj_recv)
-    halo = jnp.concatenate(
-        [send_high[N:], send_low[N:], jnp.zeros((N - 4 * H, D), BF)], axis=0
-    )
-    halo_edges = by_edge[2]
-    halo_edges = jnp.concatenate(
-        [halo_edges[:, : 2 * H], halo_edges[:, : 2 * H], halo_edges[:, 4 * H :]], axis=1
-    )
-    edges = jnp.concatenate([by_edge[0], by_edge[1]], axis=1)
-    own_high = jnp.concatenate([send_high[:N], recv_high], axis=0)
-    own_low = jnp.concatenate([send_low[:N], recv_low], axis=0)
-    preact = dot(edges, own_high) + dot(edges, own_low) + dot(halo_edges, halo)
-    sigmoid = 1.0 / (1.0 + jnp.exp(-preact))
-    message = preact * sigmoid
-    slope = sigmoid * (1.0 + preact * (1.0 - sigmoid))
-    high, low = split(message)
+    table = [send_high[:N], send_low[:N], recv_high, recv_low, send_high[N:], send_low[N:]]
+    table = jnp.concatenate(table + [jnp.zeros((N - 4 * H, D), BF)], axis=0)
+    preact = dot(by_edge[...], table)
+    highs, lows, slopes = [], [], []
+    for start in range(0, E, CHUNK):
+        part = preact[start : start + CHUNK]
+        sigmoid = 1.0 / (1.0 + jnp.exp(-part))
+        high, low = split(part * sigmoid)
+        highs.append(high)
+        lows.append(low)
+        slopes.append(sigmoid * (1.0 + part * (1.0 - sigmoid)))
     receive = by_row[EXT:ROWS, :]
-    return dot(receive, high) + dot(receive, low), slope
+    total = dot(jnp.concatenate([receive, receive], axis=1), jnp.concatenate(highs + lows, axis=0))
+    return total, jnp.concatenate(slopes, axis=0)
 
 
 def factor_of(total):
@@ -138,9 +141,12 @@
     scaled = cotangent * gain_row
     inner = jnp.mean(scaled * normal, axis=-1, keepdims=True)
     total_grad = (scaled - normal * inner) * factor
-    high, low = split(total_grad)
-    receive = by_edge[1]
-    preact_grad = ((dot(receive, high) + dot(receive, low)) * slope).astype(BF)
+    message_grad = dot(by_edge[:, 2 * N : 4 * N], jnp.concatenate(split(total_grad), axis=0))
+    preact_grad = [
+        (message_grad[start : start + CHUNK] * slope[start : start + CHUNK]).astype(BF)
+        for start in range(0, E, CHUNK)
+    ]
+    preact_grad = jnp.concatenate(preact_grad, axis=0)
     row_grad = dot(by_row[...], preact_grad).astype(BF)
     send_rows_grad, recv_rows_grad = row_grad[:EXT], row_grad[EXT:]
     ext_grad = dot_nt(send_rows_grad, send_matrix)
@@ -325,7 +331,7 @@
     other = lax.ppermute(half, ("zl", "zh"), [(i, 7 - i) for i in range(8)])
     by_row, by_edge, *sent = call(
         prepare_kernel,
-        [((ROWS, E), BF), ((3, E, N), BF), ((H, D), BF), ((H, D), BF)],
+        [((ROWS, E), BF), ((E, 5 * N), BF), ((H, D), BF), ((H, D), BF)],
         "prepare",
         edge_count.reshape(1, 1), senders, receivers, send_rows, features,
     )

time: 139 us -> 138 us (level)
  no operation moved by 1% of the time
where the time goes in v4:
time: 138 us
  starting transfers between devices  65.3 us (47%)
  blocking collectives  39.3 us (28%)
  waiting for transfers between devices  20.4 us (15%)
  Pallas kernels  9.16 us (7%)
  between operations  1.52 us (1%)
    ppermute x7, starting transfers between devices, swap(): return lax.ppermute(value, axis, [(0, 1), (1, 0)])  32.4 us
    all_to_all x1, blocking collectives, shards(): parts = lax.all_to_all(pieces, ('y', 'zh', 'zl'), 0, 0, tiled=True)  21.8 us
    all_to_all x1, blocking collectives, shards(): parts = lax.all_to_all(chunks, ('x',), 0, 0, tiled=True)  17.5 us
    ppermute x1, starting transfers between devices, shards(): other = lax.ppermute(half, ('zl', 'zh'), [(i, 7 - i) for i in range(8)])  11.5 us
    ppermute x4, starting transfers between devices, exchange(): return (lax.ppermute(outer, GRAPH, pairs), swap(inner, 'c'))  10.5 us
    pallas_call x9, Pallas kernels, call(): pl.pallas_call(kernel, out_shape=[jax.ShapeDtypeStruct(s, t) for s, t in...  9.16 us
    ppermute x7, waiting for transfers between devices, swap(): return lax.ppermute(value, axis, [(0, 1), (1, 0)])  7.35 us
    ppermute x1, waiting for transfers between devices, shards(): other = lax.ppermute(half, ('zl', 'zh'), [(i, 7 - i) for i in range(8)])  6.75 us
  transfers between devices with their start and end apart: 14, of which 10 were waited for; matrix products, arithmetic and copies ran while one was open for 0% of the time, Pallas kernels for 1%

profile of v4, /device:TPU:1, one launch (start us, length us, event | category | flops | bytes accessed | tf_op | source)
XLA Modules:
  0.0 137.8 jit_solution(6510621017327401257)
XLA Ops:
  1.6 11.5 %collective-permute-start = (bf16[2,64,512]{2,1,0:T(8,128)(2,1)S(1)}, bf16[2,64,512]{2,1,0:T(8,128)(2,1)S(1)}, u32[]{:S(2)}, u32[]{:S(2)}) collective-permute-start(bf16[2,64,512]{2,1,0:T(8,128)(2,1)S(1)} %broadcast_select_fusion), channel_id=1, source_target_pairs={{0,52},{4,48},{16,36},{20,32},{32,20},{36,16},{48,4},{52,0},{1,53}... | collective-permute-start | bytes 393224 | tf_op jit(solution)/shard_map/ppermute | solution.py:331
  13.1 6.8 %collective-permute-done = bf16[2,64,512]{2,1,0:T(8,128)(2,1)S(1)} collective-permute-done((bf16[2,64,512]{2,1,0:T(8,128)(2,1)S(1)}, bf16[2,64,512]{2,1,0:T(8,128)(2,1)S(1)}, u32[]{:S(2)}, u32[]{:S(2)}) %collective-permute-start) | collective-permute-done | bytes 131104 | tf_op jit(solution)/shard_map/ppermute | solution.py:331
  19.9 1.1 broadcast_in_dim.12
  21.0 4.2 %all-to-all-start = ((bf16[4,2,2,64,512]{4,3,2,1,0:T(8,128)(2,1)}), bf16[4,2,2,64,512]{4,3,2,1,0:T(8,128)(2,1)S(1)}, u32[]{:S(2)}, u32[]{:S(2)}) async-start(bf16[4,2,2,64,512]{4,3,2,1,0:T(8,128)(2,1)} %broadcast_in_dim.12), calls=%async_computation | async-start | bytes 2097152 | tf_op jit(solution)/shard_map/all_to_all | solution.py:341
  26.1 1.9 %collective-permute-start.1 = (bf16[16,512]{1,0:T(8,128)(2,1)S(1)}, bf16[16,512]{1,0:T(8,128)(2,1)S(1)}, u32[]{:S(2)}, u32[]{:S(2)}) collective-permute-start(bf16[16,512]{1,0:T(8,128)(2,1)S(1)} %get-tuple-element.37), channel_id=1, source_target_pairs={{0,504},{8,16},{16,8},{24,32},{32,24},{40,48},{48,40},{56,64},{64,... | collective-permute-start | bytes 49160 | tf_op jit(solution)/shard_map/ppermute | solution.py:322
  28.1 4.7 %collective-permute-start.2 = (bf16[16,512]{1,0:T(8,128)(2,1)S(1)}, bf16[16,512]{1,0:T(8,128)(2,1)S(1)}, u32[]{:S(2)}, u32[]{:S(2)}) collective-permute-start(bf16[16,512]{1,0:T(8,128)(2,1)S(1)} %get-tuple-element.38), channel_id=1, source_target_pairs={{0,8},{8,0},{1,9},{9,1},{2,10},{10,2},{3,11},{11,3},{4,12},{12,4},... | collective-permute-start | bytes 49160 | tf_op jit(solution)/shard_map/ppermute | solution.py:317
  33.6 6.0 %all-to-all-done.own = bf16[4,2,2,64,512]{4,3,2,1,0:T(8,128)(2,1)S(1)} async-done(((bf16[4,2,2,64,512]{4,3,2,1,0:T(8,128)(2,1)}), bf16[4,2,2,64,512]{4,3,2,1,0:T(8,128)(2,1)S(1)}, u32[]{:S(2)}, u32[]{:S(2)}) %all-to-all-start) | async-done | bytes 1048608 | tf_op jit(solution)/shard_map/all_to_all | solution.py:341
  39.6 3.5 %collective-permute-start.3 = (bf16[4,2,2,64,512]{4,3,2,1,0:T(8,128)(2,1)S(1)}, bf16[4,2,2,64,512]{4,3,2,1,0:T(8,128)(2,1)S(1)}, u32[]{:S(2)}, u32[]{:S(2)}) collective-permute-start(bf16[4,2,2,64,512]{4,3,2,1,0:T(8,128)(2,1)S(1)} %all-to-all-done.own), channel_id=1, source_target_pairs={{0,8},{8,0},{1,9},{9,1},{2,10},{10,2},{3,11},{11,3},{4,12},{12,4},... | collective-permute-start | bytes 3145736 | tf_op jit(solution)/shard_map/ppermute | solution.py:317
  43.2 2.3 %collective-permute-done.3.peer = bf16[4,2,2,64,512]{4,3,2,1,0:T(8,128)(2,1)S(1)} collective-permute-done((bf16[4,2,2,64,512]{4,3,2,1,0:T(8,128)(2,1)S(1)}, bf16[4,2,2,64,512]{4,3,2,1,0:T(8,128)(2,1)S(1)}, u32[]{:S(2)}, u32[]{:S(2)}) %collective-permute-start.3) | collective-permute-done | bytes 1048608 | tf_op jit(solution)/shard_map/ppermute | solution.py:317
  45.4 1.6 %first_layer.1 = (bf16[128,512]{1,0:T(8,128)(2,1)S(1)}, f32[128,512]{1,0:T(8,128)S(1)}, f32[512,512]{1,0:T(8,128)S(1)}, bf16[16,512]{1,0:T(8,128)(2,1)S(1)}, bf16[16,512]{1,0:T(8,128)(2,1)S(1)}) custom-call(s32[1,1]{1,0:T(1,128)} %bitcast.core, bf16[128,512]{1,0:T(8,128)(2,1)S(1)} %bitcast.12, bf16[16,512]{1,0:T(8,128)(2,1)S(1)} %collective-permute-done.1.outer.outer_0, ...), custom_call_target="tpu_custom_call" | custom-call | flops 100000000 | bytes 2000000 | tf_op jit(solution)/shard_map/first_layer/pallas_call | solution.py:50
  47.0 1.9 %collective-permute-start.4 = (bf16[16,512]{1,0:T(8,128)(2,1)S(1)}, bf16[16,512]{1,0:T(8,128)(2,1)S(1)}, u32[]{:S(2)}, u32[]{:S(2)}) collective-permute-start(bf16[16,512]{1,0:T(8,128)(2,1)S(1)} %get-tuple-element.45), channel_id=1, source_target_pairs={{0,504},{8,16},{16,8},{24,32},{32,24},{40,48},{48,40},{56,64},{64,... | collective-permute-start | bytes 49160 | tf_op jit(solution)/shard_map/ppermute | solution.py:322
  49.0 4.7 %collective-permute-start.5 = (bf16[16,512]{1,0:T(8,128)(2,1)S(1)}, bf16[16,512]{1,0:T(8,128)(2,1)S(1)}, u32[]{:S(2)}, u32[]{:S(2)}) collective-permute-start(bf16[16,512]{1,0:T(8,128)(2,1)S(1)} %get-tuple-element.46), channel_id=1, source_target_pairs={{0,8},{8,0},{1,9},{9,1},{2,10},{10,2},{3,11},{11,3},{4,12},{12,4},... | collective-permute-start | bytes 49160 | tf_op jit(solution)/shard_map/ppermute | solution.py:317
  54.5 2.9 %last_layer.1 = (bf16[128,512]{1,0:T(8,128)(2,1)}, f32[128,512]{1,0:T(8,128)S(1)}, bf16[16,512]{1,0:T(8,128)(2,1)S(1)}, bf16[16,512]{1,0:T(8,128)(2,1)S(1)}, bf1...) custom-call(s32[1,1]{1,0:T(1,128)} %bitcast.core, bf16[128,512]{1,0:T(8,128)(2,1)S(1)} %get-tuple-element.44.rows.rows_1, ...), custom_call_target="tpu_custom_call" | custom-call | flops 100000000 | bytes 2000000 | tf_op jit(solution)/shard_map/last_layer/pallas_call | solution.py:50
  57.4 1.9 %collective-permute-start.6 = (bf16[16,512]{1,0:T(8,128)(2,1)S(1)}, bf16[16,512]{1,0:T(8,128)(2,1)S(1)}, u32[]{:S(2)}, u32[]{:S(2)}) collective-permute-start(bf16[16,512]{1,0:T(8,128)(2,1)S(1)} %get-tuple-element.49), channel_id=1, source_target_pairs={{0,504},{8,16},{16,8},{24,32},{32,24},{40,48},{48,40},{56,64},{64,... | collective-permute-start | bytes 49160 | tf_op jit(solution)/shard_map/ppermute | solution.py:322
  59.3 6.2 %collective-permute-start.7 = (bf16[16,512]{1,0:T(8,128)(2,1)S(1)}, bf16[16,512]{1,0:T(8,128)(2,1)S(1)}, u32[]{:S(2)}, u32[]{:S(2)}) collective-permute-start(bf16[16,512]{1,0:T(8,128)(2,1)S(1)} %get-tuple-element.50), channel_id=1, source_target_pairs={{0,8},{8,0},{1,9},{9,1},{2,10},{10,2},{3,11},{11,3},{4,12},{12,4},... | collective-permute-start | bytes 49160 | tf_op jit(solution)/shard_map/ppermute | solution.py:317
  66.3 1.2 back.1
  67.5 3.8 %collective-permute-start.8 = (bf16[624,512]{1,0:T(8,128)(2,1)S(1)}, bf16[624,512]{1,0:T(8,128)(2,1)S(1)}, u32[]{:S(2)}, u32[]{:S(2)}) collective-permute-start(bf16[624,512]{1,0:T(8,128)(2,1)S(1)} %get-tuple-element.56.pack), channel_id=1, source_target_pairs={{0,8},{8,0},{1,9},{9,1},{2,10},{10,2},{3,11},{11,3},{4,12},{12,4},... | collective-permute-start | bytes 1916936 | tf_op jit(solution)/shard_map/ppermute | solution.py:317
  71.3 1.7 %collective-permute-done.8.peer = bf16[624,512]{1,0:T(8,128)(2,1)S(1)} collective-permute-done((bf16[624,512]{1,0:T(8,128)(2,1)S(1)}, bf16[624,512]{1,0:T(8,128)(2,1)S(1)}, u32[]{:S(2)}, u32[]{:S(2)}) %collective-permute-start.8) | collective-permute-done | bytes 639008 | tf_op jit(solution)/shard_map/ppermute | solution.py:317
  73.6 17.5 %all_to_all.20.parts = bf16[4,528,256]{2,1,0:T(8,128)(2,1)S(1)} all-to-all(bf16[4,528,256]{2,1,0:T(8,128)(2,1)S(1)} %terms.1), channel_id=1, replica_groups=mesh['y'=8,'zl'=4,'c'=2,'zh'=2,'x'=4] {'x'}, dimensions={0} | all-to-all | bytes 2162688 | tf_op jit(solution)/shard_map/all_to_all | solution.py:368
  91.2 21.8 %all_to_all.21.parts = bf16[64,8,384]{2,1,0:T(8,128)(2,1)S(1)} all-to-all(bf16[64,8,384]{2,1,0:T(8,128)(2,1)S(1)} %first_sum.1), channel_id=1, replica_groups=mesh['y'=8,'zl'=4,'c'=2,'zh'=2,'x'=4] {'y','zh','zl'}, dimensions={0} | all-to-all | bytes 786432 | tf_op jit(solution)/shard_map/all_to_all | solution.py:370
  113.8 6.7 %all-to-all-start.3 = ((bf16[32,8,384]{2,1,0:T(8,128)(2,1)}), bf16[32,8,384]{2,1,0:T(8,128)(2,1)S(1)}, u32[]{:S(2)}, u32[]{:S(2)}) async-start(bf16[32,8,384]{2,1,0:T(8,128)(2,1)} %second_sum.1), calls=%async_computation.3 | async-start | bytes 393216 | tf_op jit(solution)/shard_map/all_to_all | solution.py:373
  120.6 4.8 %collective-permute-start.9 = (bf16[16,512]{1,0:T(8,128)(2,1)S(1)}, bf16[16,512]{1,0:T(8,128)(2,1)S(1)}, u32[]{:S(2)}, u32[]{:S(2)}) collective-permute-start(bf16[16,512]{1,0:T(8,128)(2,1)S(1)} %get-tuple-element.61), channel_id=1, source_target_pairs={{0,504},{8,16},{16,8},{24,32},{32,24},{40,48},{48,40},{56,64},{64,... | collective-permute-start | bytes 49160 | tf_op jit(solution)/shard_map/ppermute | solution.py:322
  125.3 4.7 %collective-permute-start.10 = (bf16[16,512]{1,0:T(8,128)(2,1)S(1)}, bf16[16,512]{1,0:T(8,128)(2,1)S(1)}, u32[]{:S(2)}, u32[]{:S(2)}) collective-permute-start(bf16[16,512]{1,0:T(8,128)(2,1)S(1)} %get-tuple-element.62), channel_id=1, source_target_pairs={{0,8},{8,0},{1,9},{9,1},{2,10},{10,2},{3,11},{11,3},{4,12},{12,4},... | collective-permute-start | bytes 49160 | tf_op jit(solution)/shard_map/ppermute | solution.py:317
  131.1 4.8 %collective-permute-start.11 = (bf16[32,8,384]{2,1,0:T(8,128)(2,1)S(1)}, bf16[32,8,384]{2,1,0:T(8,128)(2,1)S(1)}, u32[]{:S(2)}, u32[]{:S(2)}) collective-permute-start(bf16[32,8,384]{2,1,0:T(8,128)(2,1)S(1)} %all-to-all-done.3.own), channel_id=1, source_target_pairs={{0,8},{8,0},{1,9},{9,1},{2,10},{10,2},{3,11},{11,3},{4,12},{12,4},... | collective-permute-start | bytes 589832 | tf_op jit(solution)/shard_map/ppermute | solution.py:317
  (31 shorter events, 8.2 us)
Async XLA Ops:
  1.6 18.3 %collective-permute-start = (bf16[2,64,512]{2,1,0:T(8,128)(2,1)S(1)}, bf16[2,64,512]{2,1,0:T(8,128)(2,1)S(1)}, u32[]{:S(2)}, u32[]{:S(2)}) collective-permute-start(bf16[2,64,512]{2,1,0:T(8,128)(2,1)S(1)} %broadcast_select_fusion), channel_id=1, source_target_pairs={{0,52},{4,48},{16,36},{20,32},{32,20},{36,16},{48,4},{52,0},{1,53}... | collective-permute-start | bytes 393224 | tf_op jit(solution)/shard_map/ppermute | solution.py:331
  21.0 4.8 %copy-start = (bf16[1,128,512]{2,1,0:T(8,128)(2,1)S(1)}, bf16[1,128,512]{2,1,0:T(8,128)(2,1)}, u32[]{:S(2)}) copy-start(bf16[1,128,512]{2,1,0:T(8,128)(2,1)} %param.9) | copy-start | bytes 393220
  21.0 4.8 %copy-start.3 = (s32[1,2,8]{2,1,0:T(2,128)S(1)}, s32[1,2,8]{2,1,0:T(2,128)}, u32[]{:S(2)}) copy-start(s32[1,2,8]{2,1,0:T(2,128)} %send_rows.7) | copy-start | bytes 196
  21.0 4.8 %copy-start.4 = (s32[1,512]{1,0:T(1,128)S(1)}, s32[1,512]{1,0:T(1,128)}, u32[]{:S(2)}) copy-start(s32[1,512]{1,0:T(1,128)} %senders.1) | copy-start | bytes 6148
  21.0 4.9 %copy-start.5 = (s32[1,512]{1,0:T(1,128)S(1)}, s32[1,512]{1,0:T(1,128)}, u32[]{:S(2)}) copy-start(s32[1,512]{1,0:T(1,128)} %receivers.1) | copy-start | bytes 6148
  21.0 24.4 %copy-start.2 = (f32[2,512]{1,0:T(2,128)S(1)}, f32[2,512]{1,0:T(2,128)}, u32[]{:S(2)}) copy-start(f32[2,512]{1,0:T(2,128)} %gain.5) | copy-start | bytes 12292
  21.0 18.6 %all-to-all-start = ((bf16[4,2,2,64,512]{4,3,2,1,0:T(8,128)(2,1)}), bf16[4,2,2,64,512]{4,3,2,1,0:T(8,128)(2,1)S(1)}, u32[]{:S(2)}, u32[]{:S(2)}) async-start(bf16[4,2,2,64,512]{4,3,2,1,0:T(8,128)(2,1)} %broadcast_in_dim.12), calls=%async_computation | async-start | bytes 2097152 | tf_op jit(solution)/shard_map/all_to_all | solution.py:341
  26.1 6.6 %collective-permute-start.1 = (bf16[16,512]{1,0:T(8,128)(2,1)S(1)}, bf16[16,512]{1,0:T(8,128)(2,1)S(1)}, u32[]{:S(2)}, u32[]{:S(2)}) collective-permute-start(bf16[16,512]{1,0:T(8,128)(2,1)S(1)} %get-tuple-element.37), channel_id=1, source_target_pairs={{0,504},{8,16},{16,8},{24,32},{32,24},{40,48},{48,40},{56,64},{64,... | collective-permute-start | bytes 49160 | tf_op jit(solution)/shard_map/ppermute | solution.py:322
  28.1 5.5 %collective-permute-start.2 = (bf16[16,512]{1,0:T(8,128)(2,1)S(1)}, bf16[16,512]{1,0:T(8,128)(2,1)S(1)}, u32[]{:S(2)}, u32[]{:S(2)}) collective-permute-start(bf16[16,512]{1,0:T(8,128)(2,1)S(1)} %get-tuple-element.38), channel_id=1, source_target_pairs={{0,8},{8,0},{1,9},{9,1},{2,10},{10,2},{3,11},{11,3},{4,12},{12,4},... | collective-permute-start | bytes 49160 | tf_op jit(solution)/shard_map/ppermute | solution.py:317
  39.6 5.8 %collective-permute-start.3 = (bf16[4,2,2,64,512]{4,3,2,1,0:T(8,128)(2,1)S(1)}, bf16[4,2,2,64,512]{4,3,2,1,0:T(8,128)(2,1)S(1)}, u32[]{:S(2)}, u32[]{:S(2)}) collective-permute-start(bf16[4,2,2,64,512]{4,3,2,1,0:T(8,128)(2,1)S(1)} %all-to-all-done.own), channel_id=1, source_target_pairs={{0,8},{8,0},{1,9},{9,1},{2,10},{10,2},{3,11},{11,3},{4,12},{12,4},... | collective-permute-start | bytes 3145736 | tf_op jit(solution)/shard_map/ppermute | solution.py:317
  45.4 9.1 %copy-start.1 = (bf16[1,128,512]{2,1,0:T(8,128)(2,1)S(1)}, bf16[1,128,512]{2,1,0:T(8,128)(2,1)}, u32[]{:S(2)}) copy-start(bf16[1,128,512]{2,1,0:T(8,128)(2,1)} %param.10) | copy-start | bytes 393220
  47.0 6.6 %collective-permute-start.4 = (bf16[16,512]{1,0:T(8,128)(2,1)S(1)}, bf16[16,512]{1,0:T(8,128)(2,1)S(1)}, u32[]{:S(2)}, u32[]{:S(2)}) collective-permute-start(bf16[16,512]{1,0:T(8,128)(2,1)S(1)} %get-tuple-element.45), channel_id=1, source_target_pairs={{0,504},{8,16},{16,8},{24,32},{32,24},{40,48},{48,40},{56,64},{64,... | collective-permute-start | bytes 49160 | tf_op jit(solution)/shard_map/ppermute | solution.py:322
  49.0 5.5 %collective-permute-start.5 = (bf16[16,512]{1,0:T(8,128)(2,1)S(1)}, bf16[16,512]{1,0:T(8,128)(2,1)S(1)}, u32[]{:S(2)}, u32[]{:S(2)}) collective-permute-start(bf16[16,512]{1,0:T(8,128)(2,1)S(1)} %get-tuple-element.46), channel_id=1, source_target_pairs={{0,8},{8,0},{1,9},{9,1},{2,10},{10,2},{3,11},{11,3},{4,12},{12,4},... | collective-permute-start | bytes 49160 | tf_op jit(solution)/shard_map/ppermute | solution.py:317
  57.4 8.2 %collective-permute-start.6 = (bf16[16,512]{1,0:T(8,128)(2,1)S(1)}, bf16[16,512]{1,0:T(8,128)(2,1)S(1)}, u32[]{:S(2)}, u32[]{:S(2)}) collective-permute-start(bf16[16,512]{1,0:T(8,128)(2,1)S(1)} %get-tuple-element.49), channel_id=1, source_target_pairs={{0,504},{8,16},{16,8},{24,32},{32,24},{40,48},{48,40},{56,64},{64,... | collective-permute-start | bytes 49160 | tf_op jit(solution)/shard_map/ppermute | solution.py:322
  59.3 7.1 %collective-permute-start.7 = (bf16[16,512]{1,0:T(8,128)(2,1)S(1)}, bf16[16,512]{1,0:T(8,128)(2,1)S(1)}, u32[]{:S(2)}, u32[]{:S(2)}) collective-permute-start(bf16[16,512]{1,0:T(8,128)(2,1)S(1)} %get-tuple-element.50), channel_id=1, source_target_pairs={{0,8},{8,0},{1,9},{9,1},{2,10},{10,2},{3,11},{11,3},{4,12},{12,4},... | collective-permute-start | bytes 49160 | tf_op jit(solution)/shard_map/ppermute | solution.py:317
  67.5 5.5 %collective-permute-start.8 = (bf16[624,512]{1,0:T(8,128)(2,1)S(1)}, bf16[624,512]{1,0:T(8,128)(2,1)S(1)}, u32[]{:S(2)}, u32[]{:S(2)}) collective-permute-start(bf16[624,512]{1,0:T(8,128)(2,1)S(1)} %get-tuple-element.56.pack), channel_id=1, source_target_pairs={{0,8},{8,0},{1,9},{9,1},{2,10},{10,2},{3,11},{11,3},{4,12},{12,4},... | collective-permute-start | bytes 1916936 | tf_op jit(solution)/shard_map/ppermute | solution.py:317
  113.8 17.3 %all-to-all-start.3 = ((bf16[32,8,384]{2,1,0:T(8,128)(2,1)}), bf16[32,8,384]{2,1,0:T(8,128)(2,1)S(1)}, u32[]{:S(2)}, u32[]{:S(2)}) async-start(bf16[32,8,384]{2,1,0:T(8,128)(2,1)} %second_sum.1), calls=%async_computation.3 | async-start | bytes 393216 | tf_op jit(solution)/shard_map/all_to_all | solution.py:373
  120.6 9.5 %collective-permute-start.9 = (bf16[16,512]{1,0:T(8,128)(2,1)S(1)}, bf16[16,512]{1,0:T(8,128)(2,1)S(1)}, u32[]{:S(2)}, u32[]{:S(2)}) collective-permute-start(bf16[16,512]{1,0:T(8,128)(2,1)S(1)} %get-tuple-element.61), channel_id=1, source_target_pairs={{0,504},{8,16},{16,8},{24,32},{32,24},{40,48},{48,40},{56,64},{64,... | collective-permute-start | bytes 49160 | tf_op jit(solution)/shard_map/ppermute | solution.py:322
  125.3 5.5 %collective-permute-start.10 = (bf16[16,512]{1,0:T(8,128)(2,1)S(1)}, bf16[16,512]{1,0:T(8,128)(2,1)S(1)}, u32[]{:S(2)}, u32[]{:S(2)}) collective-permute-start(bf16[16,512]{1,0:T(8,128)(2,1)S(1)} %get-tuple-element.62), channel_id=1, source_target_pairs={{0,8},{8,0},{1,9},{9,1},{2,10},{10,2},{3,11},{11,3},{4,12},{12,4},... | collective-permute-start | bytes 49160 | tf_op jit(solution)/shard_map/ppermute | solution.py:317
  131.1 5.8 %collective-permute-start.11 = (bf16[32,8,384]{2,1,0:T(8,128)(2,1)S(1)}, bf16[32,8,384]{2,1,0:T(8,128)(2,1)S(1)}, u32[]{:S(2)}, u32[]{:S(2)}) collective-permute-start(bf16[32,8,384]{2,1,0:T(8,128)(2,1)S(1)} %all-to-all-done.3.own), channel_id=1, source_target_pairs={{0,8},{8,0},{1,9},{9,1},{2,10},{10,2},{3,11},{11,3},{4,12},{12,4},... | collective-permute-start | bytes 589832 | tf_op jit(solution)/shard_map/ppermute | solution.py:317

commit v5 on v4

--- a/solution.py
+++ b/solution.py
@@ -134,7 +134,7 @@
     return lax.rsqrt(jnp.mean(total * total, axis=-1, keepdims=True) + EPSILON)
 
 
-def backward(cotangent, total, slope, gain_row, send_matrix, recv_matrix, by_row, by_edge):
+def backward(cotangent, total, slope, gain_row, by_row, by_edge):
     factor = factor_of(total)
     normal = total * factor
     gain_term = jnp.sum(cotangent * normal, axis=0, keepdims=True)
@@ -146,14 +146,18 @@
         (message_grad[start : start + CHUNK] * slope[start : start + CHUNK]).astype(BF)
         for start in range(0, E, CHUNK)
     ]
-    preact_grad = jnp.concatenate(preact_grad, axis=0)
-    row_grad = dot(by_row[...], preact_grad).astype(BF)
-    send_rows_grad, recv_rows_grad = row_grad[:EXT], row_grad[EXT:]
-    ext_grad = dot_nt(send_rows_grad, send_matrix)
-    own_grad = dot_nt(recv_rows_grad, recv_matrix) + ext_grad[:N]
-    halo_grad = ext_grad[N:].astype(BF)
+    row_grad = dot(by_row[...], jnp.concatenate(preact_grad, axis=0)).astype(BF)
     gain_block = jnp.concatenate([gain_term, jnp.zeros((15, D), F32)], axis=0).astype(BF)
-    return own_grad, halo_grad[:H], halo_grad[H:], row_grad, gain_block
+    return row_grad, gain_block
+
+
+def halo_grads(core, row_grad, send_matrix):
+    grads = dot_nt(row_grad[N:EXT], send_matrix).astype(BF)
+    return ordered(core, grads[:H], grads[H:])
+
+
+def own_grad_of(cotangent, row_grad, send_matrix, recv_matrix):
+    return cotangent + dot_nt(row_grad[0:N, :], send_matrix) + dot_nt(row_grad[EXT:ROWS, :], recv_matrix)
 
 
 def halves(core, value):
@@ -182,23 +186,27 @@
 
 def last_layer_kernel(
     core, rows, outer, inner, own, peer, gain, by_row, by_edge, out_grad,
-    result, own_grad, outer_out, inner_out, keep, give,
+    outer_out, inner_out, total_out, row_grad_out,
 ):
     from_prev, from_next = ordered(core, outer, inner)
     send_matrix, recv_matrix = weights_of(core, own, peer, 1)
     total, slope = forward(
         rows[...], from_prev, from_next, send_matrix, recv_matrix, by_row, by_edge
     )
-    gain_row = gain[1:2, :]
-    result[...] = (rows[...].astype(F32) + gain_row * total * factor_of(total)).astype(BF)
+    total_out[...] = total
     cotangent = out_grad[...].astype(F32)
-    grad, prev_grad, next_grad, row_grad, gain_block = backward(
-        cotangent, total, slope, gain_row, send_matrix, recv_matrix, by_row, by_edge
-    )
-    own_grad[...] = grad + cotangent
-    outer_out[...], inner_out[...] = ordered(core, prev_grad, next_grad)
-    keep[0:ROWS, :], give[0:ROWS, :] = halves(core, row_grad)
-    keep[ROWS:DROWS, :], give[ROWS:DROWS, :] = halves(core, gain_block)
+    row_grad, gain_block = backward(cotangent, total, slope, gain[1:2, :], by_row, by_edge)
+    outer_out[...], inner_out[...] = halo_grads(core, row_grad, send_matrix)
+    row_grad_out[0:ROWS, :] = row_grad
+    row_grad_out[ROWS:DROWS, :] = gain_block
+
+
+def last_rest_kernel(core, rows, total, gain, out_grad, row_grad, own, peer, result, own_grad, keep, give):
+    send_matrix, recv_matrix = weights_of(core, own, peer, 1)
+    step = gain[1:2, :] * total[...] * factor_of(total[...])
+    result[...] = (rows[...].astype(F32) + step).astype(BF)
+    own_grad[...] = own_grad_of(out_grad[...].astype(F32), row_grad, send_matrix, recv_matrix)
+    keep[...], give[...] = halves(core, row_grad[...])
 
 
 def merged(own_grad, outer, inner, send_rows):
@@ -209,17 +217,14 @@
 
 
 def back_kernel(
-    core, later_grad, outer, inner, total, slope, own, peer, gain, by_row, by_edge, send_rows,
+    core, later_grad, outer, inner, total, slope, gain, by_row, by_edge, send_rows,
     rows_0, outer_0, inner_0, rows_1, outer_1, inner_1, later_keep, later_give,
-    own_grad, outer_out, inner_out, keep, pack,
+    cotangent_out, row_grad_out, keep, pack,
 ):
-    send_matrix, recv_matrix = weights_of(core, own, peer, 0)
     cotangent = merged(later_grad, outer, inner, send_rows).astype(F32)
-    grad, prev_grad, next_grad, row_grad, gain_block = backward(
-        cotangent, total[...], slope[...], gain[0:1, :], send_matrix, recv_matrix, by_row, by_edge
-    )
-    own_grad[...] = grad + cotangent
-    outer_out[...], inner_out[...] = ordered(core, prev_grad, next_grad)
+    cotangent_out[...] = cotangent
+    row_grad, gain_block = backward(cotangent, total[...], slope[...], gain[0:1, :], by_row, by_edge)
+    row_grad_out[...] = row_grad
     base = 2 * EXT
     keep_rows, give_rows = halves(core, row_grad)
     keep_gain, give_gain = halves(core, gain_block)
@@ -235,6 +240,12 @@
         from_prev, from_next = ordered(core, *parts[1:])
         pack[start + N : start + N + H, :] = from_prev
         pack[start + N + H : start + EXT, :] = from_next
+
+
+def back_rest_kernel(core, cotangent, row_grad, own, peer, own_grad, outer_out, inner_out):
+    send_matrix, recv_matrix = weights_of(core, own, peer, 0)
+    own_grad[...] = own_grad_of(cotangent[...], row_grad, send_matrix, recv_matrix)
+    outer_out[...], inner_out[...] = halo_grads(core, row_grad[...], send_matrix)
 
 
 def merge_kernel(own_grad, outer, inner, send_rows, result):
@@ -349,21 +360,34 @@
         core, features, *halo_0, own, peer, gain, by_row, by_edge, send_rows,
     )
     halo_1 = exchange(*sent)
-    updated, grad_1, outer, inner, keep_1, give_1 = call(
+    outer, inner, total_1, row_grad = call(
         last_layer_kernel,
-        [((N, D), BF), ((N, D), F32), ((H, D), BF), ((H, D), BF), ((DROWS, HALF), BF), ((DROWS, HALF), BF)],
+        [((H, D), BF), ((H, D), BF), ((N, D), F32), ((DROWS, D), BF)],
         "last_layer",
         core, rows_1, *halo_1, own, peer, gain, by_row, by_edge, out_grad[0],
     )
     back = exchange(outer, inner)
-    grad_0, outer, inner, keep, pack = call(
+    updated, grad_1, keep_1, give_1 = call(
+        last_rest_kernel,
+        [((N, D), BF), ((N, D), F32), ((DROWS, HALF), BF), ((DROWS, HALF), BF)],
+        "last_rest",
+        core, rows_1, total_1, gain, out_grad[0], row_grad, own, peer,
+    )
+    cotangent, row_grad, keep, pack = call(
         back_kernel,
-        [((N, D), F32), ((H, D), BF), ((H, D), BF), ((DROWS, D), BF), ((2 * EXT + DROWS, D), BF)],
+        [((N, D), F32), ((ROWS, D), BF), ((DROWS, D), BF), ((2 * EXT + DROWS, D), BF)],
         "back",
-        core, grad_1, *back, total_0, slope_0, own, peer, gain, by_row, by_edge,
+        core, grad_1, *back, total_0, slope_0, gain, by_row, by_edge,
         send_rows, features, *halo_0, rows_1, *halo_1, keep_1, give_1,
     )
+    grad_0, outer, inner = call(
+        back_rest_kernel,
+        [((N, D), F32), ((H, D), BF), ((H, D), BF)],
+        "back_rest",
+        core, cotangent, row_grad, own, peer,
+    )
     peer_pack = swap(pack, "c")
+    peer_pack, grad_0, outer, inner = lax.optimization_barrier((peer_pack, grad_0, outer, inner))
     (chunks,) = call(terms_kernel, [((4, 528, HALF), BF)], "terms", pack, keep, peer_pack)
     parts = lax.all_to_all(chunks, ("x",), 0, 0, tiled=True)
     (pieces,) = call(first_sum_kernel, [((PARTS, 8, HALF + 128), BF)], "first_sum", parts)

time: 138 us -> 138 us (level)
  waiting for transfers between devices: 20.4 us -> 19 us
    ppermute x7, waiting for transfers between devices: 7.35 us -> 5.94 us  [swap(): return lax.ppermute(value, axis, [(0, 1), (1, 0)])]
    pallas_call x9 -> x11, Pallas kernels: 9.16 us -> 9.75 us  [call(): pl.pallas_call(kernel, out_shape=[jax.ShapeDtypeStruct(s, t) for s, t in...]
  transfers between devices with their start and end apart: 14 -> 14, of which waited for: 10 -> 9; matrix products, arithmetic and copies ran while one was open for 0% -> 0% of each run, Pallas kernels for 1% -> 2%
where the time goes in v5:
time: 138 us; the launch traced here: 137 us
  starting transfers between devices  65 us (47%)
  blocking collectives  39.7 us (29%)
  waiting for transfers between devices  19 us (14%)
  Pallas kernels  9.75 us (7%)
  between operations  1.54 us (1%)
    ppermute x7, starting transfers between devices, swap(): return lax.ppermute(value, axis, [(0, 1), (1, 0)])  32.1 us
    all_to_all x1, blocking collectives, shards(): parts = lax.all_to_all(pieces, ('y', 'zh', 'zl'), 0, 0, tiled=True)  22.2 us
    all_to_all x1, blocking collectives, shards(): parts = lax.all_to_all(chunks, ('x',), 0, 0, tiled=True)  17.4 us
    ppermute x1, starting transfers between devices, shards(): other = lax.ppermute(half, ('zl', 'zh'), [(i, 7 - i) for i in range(8)])  11.5 us
    ppermute x4, starting transfers between devices, exchange(): return (lax.ppermute(outer, GRAPH, pairs), swap(inner, 'c'))  10.5 us
    pallas_call x11, Pallas kernels, call(): pl.pallas_call(kernel, out_shape=[jax.ShapeDtypeStruct(s, t) for s, t in...  9.75 us
    ppermute x1, waiting for transfers between devices, shards(): other = lax.ppermute(half, ('zl', 'zh'), [(i, 7 - i) for i in range(8)])  6.75 us
    all_to_all x1, starting transfers between devices, shards(): mine = lax.all_to_all(copies, ('y', 'zl'), 0, 0, tiled=True)  6.72 us
  transfers between devices with their start and end apart: 14, of which 9 were waited for; matrix products, arithmetic and copies ran while one was open for 0% of the time, Pallas kernels for 2%

profile of v5, /device:TPU:1, one launch (start us, length us, event | category | flops | bytes accessed | tf_op | source)
XLA Modules:
  0.0 137.1 jit_solution(3951838706575854687)
XLA Ops:
  1.6 11.5 %collective-permute-start = (bf16[2,64,512]{2,1,0:T(8,128)(2,1)S(1)}, bf16[2,64,512]{2,1,0:T(8,128)(2,1)S(1)}, u32[]{:S(2)}, u32[]{:S(2)}) collective-permute-start(bf16[2,64,512]{2,1,0:T(8,128)(2,1)S(1)} %broadcast_select_fusion), channel_id=1, source_target_pairs={{0,52},{4,48},{16,36},{20,32},{32,20},{36,16},{48,4},{52,0},{1,53}... | collective-permute-start | bytes 393224 | tf_op jit(solution)/shard_map/ppermute | solution.py:342
  13.1 6.8 %collective-permute-done = bf16[2,64,512]{2,1,0:T(8,128)(2,1)S(1)} collective-permute-done((bf16[2,64,512]{2,1,0:T(8,128)(2,1)S(1)}, bf16[2,64,512]{2,1,0:T(8,128)(2,1)S(1)}, u32[]{:S(2)}, u32[]{:S(2)}) %collective-permute-start) | collective-permute-done | bytes 131104 | tf_op jit(solution)/shard_map/ppermute | solution.py:342
  19.9 1.1 broadcast_in_dim.12
  21.0 4.2 %all-to-all-start = ((bf16[4,2,2,64,512]{4,3,2,1,0:T(8,128)(2,1)}), bf16[4,2,2,64,512]{4,3,2,1,0:T(8,128)(2,1)S(1)}, u32[]{:S(2)}, u32[]{:S(2)}) async-start(bf16[4,2,2,64,512]{4,3,2,1,0:T(8,128)(2,1)} %broadcast_in_dim.12), calls=%async_computation | async-start | bytes 2097152 | tf_op jit(solution)/shard_map/all_to_all | solution.py:352
  26.1 1.9 %collective-permute-start.1 = (bf16[16,512]{1,0:T(8,128)(2,1)S(1)}, bf16[16,512]{1,0:T(8,128)(2,1)S(1)}, u32[]{:S(2)}, u32[]{:S(2)}) collective-permute-start(bf16[16,512]{1,0:T(8,128)(2,1)S(1)} %get-tuple-element.45), channel_id=1, source_target_pairs={{0,504},{8,16},{16,8},{24,32},{32,24},{40,48},{48,40},{56,64},{64,... | collective-permute-start | bytes 49160 | tf_op jit(solution)/shard_map/ppermute | solution.py:333
  28.1 4.7 %collective-permute-start.2 = (bf16[16,512]{1,0:T(8,128)(2,1)S(1)}, bf16[16,512]{1,0:T(8,128)(2,1)S(1)}, u32[]{:S(2)}, u32[]{:S(2)}) collective-permute-start(bf16[16,512]{1,0:T(8,128)(2,1)S(1)} %get-tuple-element.46), channel_id=1, source_target_pairs={{0,8},{8,0},{1,9},{9,1},{2,10},{10,2},{3,11},{11,3},{4,12},{12,4},... | collective-permute-start | bytes 49160 | tf_op jit(solution)/shard_map/ppermute | solution.py:328
  33.6 6.0 %all-to-all-done.own = bf16[4,2,2,64,512]{4,3,2,1,0:T(8,128)(2,1)S(1)} async-done(((bf16[4,2,2,64,512]{4,3,2,1,0:T(8,128)(2,1)}), bf16[4,2,2,64,512]{4,3,2,1,0:T(8,128)(2,1)S(1)}, u32[]{:S(2)}, u32[]{:S(2)}) %all-to-all-start) | async-done | bytes 1048608 | tf_op jit(solution)/shard_map/all_to_all | solution.py:352
  39.6 3.5 %collective-permute-start.3 = (bf16[4,2,2,64,512]{4,3,2,1,0:T(8,128)(2,1)S(1)}, bf16[4,2,2,64,512]{4,3,2,1,0:T(8,128)(2,1)S(1)}, u32[]{:S(2)}, u32[]{:S(2)}) collective-permute-start(bf16[4,2,2,64,512]{4,3,2,1,0:T(8,128)(2,1)S(1)} %all-to-all-done.own), channel_id=1, source_target_pairs={{0,8},{8,0},{1,9},{9,1},{2,10},{10,2},{3,11},{11,3},{4,12},{12,4},... | collective-permute-start | bytes 3145736 | tf_op jit(solution)/shard_map/ppermute | solution.py:328
  43.1 2.3 %collective-permute-done.3.peer = bf16[4,2,2,64,512]{4,3,2,1,0:T(8,128)(2,1)S(1)} collective-permute-done((bf16[4,2,2,64,512]{4,3,2,1,0:T(8,128)(2,1)S(1)}, bf16[4,2,2,64,512]{4,3,2,1,0:T(8,128)(2,1)S(1)}, u32[]{:S(2)}, u32[]{:S(2)}) %collective-permute-start.3) | collective-permute-done | bytes 1048608 | tf_op jit(solution)/shard_map/ppermute | solution.py:328
  45.4 1.6 %first_layer.1 = (bf16[128,512]{1,0:T(8,128)(2,1)S(1)}, f32[128,512]{1,0:T(8,128)S(1)}, f32[512,512]{1,0:T(8,128)S(1)}, bf16[16,512]{1,0:T(8,128)(2,1)S(1)}, bf16[16,512]{1,0:T(8,128)(2,1)S(1)}) custom-call(s32[1,1]{1,0:T(1,128)} %bitcast.core, bf16[128,512]{1,0:T(8,128)(2,1)S(1)} %bitcast.14, bf16[16,512]{1,0:T(8,128)(2,1)S(1)} %collective-permute-done.1.outer.outer_0, ...), custom_call_target="tpu_custom_call" | custom-call | flops 100000000 | bytes 2000000 | tf_op jit(solution)/shard_map/first_layer/pallas_call | solution.py:50
  47.0 1.9 %collective-permute-start.4 = (bf16[16,512]{1,0:T(8,128)(2,1)S(1)}, bf16[16,512]{1,0:T(8,128)(2,1)S(1)}, u32[]{:S(2)}, u32[]{:S(2)}) collective-permute-start(bf16[16,512]{1,0:T(8,128)(2,1)S(1)} %get-tuple-element.53), channel_id=1, source_target_pairs={{0,504},{8,16},{16,8},{24,32},{32,24},{40,48},{48,40},{56,64},{64,... | collective-permute-start | bytes 49160 | tf_op jit(solution)/shard_map/ppermute | solution.py:333
  48.9 4.7 %collective-permute-start.5 = (bf16[16,512]{1,0:T(8,128)(2,1)S(1)}, bf16[16,512]{1,0:T(8,128)(2,1)S(1)}, u32[]{:S(2)}, u32[]{:S(2)}) collective-permute-start(bf16[16,512]{1,0:T(8,128)(2,1)S(1)} %get-tuple-element.54), channel_id=1, source_target_pairs={{0,8},{8,0},{1,9},{9,1},{2,10},{10,2},{3,11},{11,3},{4,12},{12,4},... | collective-permute-start | bytes 49160 | tf_op jit(solution)/shard_map/ppermute | solution.py:328
  54.5 2.1 %last_layer.1 = (bf16[16,512]{1,0:T(8,128)(2,1)S(1)}, bf16[16,512]{1,0:T(8,128)(2,1)S(1)}, f32[128,512]{1,0:T(8,128)S(1)}, bf16[304,512]{1,0:T(8,128)(2,1)S(1)}) custom-call(s32[1,1]{1,0:T(1,128)} %bitcast.core, bf16[128,512]{1,0:T(8,128)(2,1)S(1)} %get-tuple-element.52.rows.rows_1, bf16[16,512]{1,0:T(8,128)(2,1)S(1)} %collective-permute-done.4.outer.outer_1, ...), custom_call_target="tpu_custom_call" | custom-call | flops 100000000 | bytes 2000000 | tf_op jit(solution)/shard_map/last_layer/pallas_call | solution.py:50
  56.6 1.9 %collective-permute-start.6 = (bf16[16,512]{1,0:T(8,128)(2,1)S(1)}, bf16[16,512]{1,0:T(8,128)(2,1)S(1)}, u32[]{:S(2)}, u32[]{:S(2)}) collective-permute-start(bf16[16,512]{1,0:T(8,128)(2,1)S(1)} %get-tuple-element.59), channel_id=1, source_target_pairs={{0,504},{8,16},{16,8},{24,32},{32,24},{40,48},{48,40},{56,64},{64,... | collective-permute-start | bytes 49160 | tf_op jit(solution)/shard_map/ppermute | solution.py:333
  58.5 6.2 %collective-permute-start.7 = (bf16[16,512]{1,0:T(8,128)(2,1)S(1)}, bf16[16,512]{1,0:T(8,128)(2,1)S(1)}, u32[]{:S(2)}, u32[]{:S(2)}) collective-permute-start(bf16[16,512]{1,0:T(8,128)(2,1)S(1)} %get-tuple-element.60), channel_id=1, source_target_pairs={{0,8},{8,0},{1,9},{9,1},{2,10},{10,2},{3,11},{11,3},{4,12},{12,4},... | collective-permute-start | bytes 49160 | tf_op jit(solution)/shard_map/ppermute | solution.py:328
  64.8 1.1 last_rest.1
  66.7 3.5 %collective-permute-start.8 = (bf16[624,512]{1,0:T(8,128)(2,1)S(1)}, bf16[624,512]{1,0:T(8,128)(2,1)S(1)}, u32[]{:S(2)}, u32[]{:S(2)}) collective-permute-start(bf16[624,512]{1,0:T(8,128)(2,1)S(1)} %get-tuple-element.65.pack), channel_id=1, source_target_pairs={{0,8},{8,0},{1,9},{9,1},{2,10},{10,2},{3,11},{11,3},{4,12},{12,4},... | collective-permute-start | bytes 1916936 | tf_op jit(solution)/shard_map/ppermute | solution.py:328
  70.8 1.1 collective-permute-done.8.peer
  72.5 17.4 %all_to_all.20.parts = bf16[4,528,256]{2,1,0:T(8,128)(2,1)S(1)} all-to-all(bf16[4,528,256]{2,1,0:T(8,128)(2,1)S(1)} %terms.1), channel_id=1, replica_groups=mesh['y'=8,'zl'=4,'c'=2,'zh'=2,'x'=4] {'x'}, dimensions={0} | all-to-all | bytes 2162688 | tf_op jit(solution)/shard_map/all_to_all | solution.py:392
  90.1 22.2 %all_to_all.21.parts = bf16[64,8,384]{2,1,0:T(8,128)(2,1)S(1)} all-to-all(bf16[64,8,384]{2,1,0:T(8,128)(2,1)S(1)} %first_sum.1), channel_id=1, replica_groups=mesh['y'=8,'zl'=4,'c'=2,'zh'=2,'x'=4] {'y','zh','zl'}, dimensions={0} | all-to-all | bytes 786432 | tf_op jit(solution)/shard_map/all_to_all | solution.py:394
  113.1 6.7 %all-to-all-start.3 = ((bf16[32,8,384]{2,1,0:T(8,128)(2,1)}), bf16[32,8,384]{2,1,0:T(8,128)(2,1)S(1)}, u32[]{:S(2)}, u32[]{:S(2)}) async-start(bf16[32,8,384]{2,1,0:T(8,128)(2,1)} %second_sum.1), calls=%async_computation.3 | async-start | bytes 393216 | tf_op jit(solution)/shard_map/all_to_all | solution.py:397
  119.9 4.8 %collective-permute-start.9 = (bf16[16,512]{1,0:T(8,128)(2,1)S(1)}, bf16[16,512]{1,0:T(8,128)(2,1)S(1)}, u32[]{:S(2)}, u32[]{:S(2)}) collective-permute-start(bf16[16,512]{1,0:T(8,128)(2,1)S(1)} %get-tuple-element.77), channel_id=1, source_target_pairs={{0,504},{8,16},{16,8},{24,32},{32,24},{40,48},{48,40},{56,64},{64,... | collective-permute-start | bytes 49160 | tf_op jit(solution)/shard_map/ppermute | solution.py:333
  124.6 4.7 %collective-permute-start.10 = (bf16[16,512]{1,0:T(8,128)(2,1)S(1)}, bf16[16,512]{1,0:T(8,128)(2,1)S(1)}, u32[]{:S(2)}, u32[]{:S(2)}) collective-permute-start(bf16[16,512]{1,0:T(8,128)(2,1)S(1)} %get-tuple-element.78), channel_id=1, source_target_pairs={{0,8},{8,0},{1,9},{9,1},{2,10},{10,2},{3,11},{11,3},{4,12},{12,4},... | collective-permute-start | bytes 49160 | tf_op jit(solution)/shard_map/ppermute | solution.py:328
  130.4 4.8 %collective-permute-start.11 = (bf16[32,8,384]{2,1,0:T(8,128)(2,1)S(1)}, bf16[32,8,384]{2,1,0:T(8,128)(2,1)S(1)}, u32[]{:S(2)}, u32[]{:S(2)}) collective-permute-start(bf16[32,8,384]{2,1,0:T(8,128)(2,1)S(1)} %all-to-all-done.3.own), channel_id=1, source_target_pairs={{0,8},{8,0},{1,9},{9,1},{2,10},{10,2},{3,11},{11,3},{4,12},{12,4},... | collective-permute-start | bytes 589832 | tf_op jit(solution)/shard_map/ppermute | solution.py:328
  (33 shorter events, 8.8 us)
Async XLA Ops:
  1.6 18.3 %collective-permute-start = (bf16[2,64,512]{2,1,0:T(8,128)(2,1)S(1)}, bf16[2,64,512]{2,1,0:T(8,128)(2,1)S(1)}, u32[]{:S(2)}, u32[]{:S(2)}) collective-permute-start(bf16[2,64,512]{2,1,0:T(8,128)(2,1)S(1)} %broadcast_select_fusion), channel_id=1, source_target_pairs={{0,52},{4,48},{16,36},{20,32},{32,20},{36,16},{48,4},{52,0},{1,53}... | collective-permute-start | bytes 393224 | tf_op jit(solution)/shard_map/ppermute | solution.py:342
  21.0 4.8 %copy-start.1 = (bf16[1,128,512]{2,1,0:T(8,128)(2,1)S(1)}, bf16[1,128,512]{2,1,0:T(8,128)(2,1)}, u32[]{:S(2)}) copy-start(bf16[1,128,512]{2,1,0:T(8,128)(2,1)} %param.9) | copy-start | bytes 393220
  21.0 4.8 %copy-start.3 = (s32[1,2,8]{2,1,0:T(2,128)S(1)}, s32[1,2,8]{2,1,0:T(2,128)}, u32[]{:S(2)}) copy-start(s32[1,2,8]{2,1,0:T(2,128)} %send_rows.7) | copy-start | bytes 196
  21.0 4.8 %copy-start.4 = (s32[1,512]{1,0:T(1,128)S(1)}, s32[1,512]{1,0:T(1,128)}, u32[]{:S(2)}) copy-start(s32[1,512]{1,0:T(1,128)} %senders.1) | copy-start | bytes 6148
  21.0 4.9 %copy-start.5 = (s32[1,512]{1,0:T(1,128)S(1)}, s32[1,512]{1,0:T(1,128)}, u32[]{:S(2)}) copy-start(s32[1,512]{1,0:T(1,128)} %receivers.1) | copy-start | bytes 6148
  21.0 24.4 %copy-start.2 = (f32[2,512]{1,0:T(2,128)S(1)}, f32[2,512]{1,0:T(2,128)}, u32[]{:S(2)}) copy-start(f32[2,512]{1,0:T(2,128)} %gain.7) | copy-start | bytes 12292
  21.0 18.6 %all-to-all-start = ((bf16[4,2,2,64,512]{4,3,2,1,0:T(8,128)(2,1)}), bf16[4,2,2,64,512]{4,3,2,1,0:T(8,128)(2,1)S(1)}, u32[]{:S(2)}, u32[]{:S(2)}) async-start(bf16[4,2,2,64,512]{4,3,2,1,0:T(8,128)(2,1)} %broadcast_in_dim.12), calls=%async_computation | async-start | bytes 2097152 | tf_op jit(solution)/shard_map/all_to_all | solution.py:352
  26.1 6.6 %collective-permute-start.1 = (bf16[16,512]{1,0:T(8,128)(2,1)S(1)}, bf16[16,512]{1,0:T(8,128)(2,1)S(1)}, u32[]{:S(2)}, u32[]{:S(2)}) collective-permute-start(bf16[16,512]{1,0:T(8,128)(2,1)S(1)} %get-tuple-element.45), channel_id=1, source_target_pairs={{0,504},{8,16},{16,8},{24,32},{32,24},{40,48},{48,40},{56,64},{64,... | collective-permute-start | bytes 49160 | tf_op jit(solution)/shard_map/ppermute | solution.py:333
  28.1 5.5 %collective-permute-start.2 = (bf16[16,512]{1,0:T(8,128)(2,1)S(1)}, bf16[16,512]{1,0:T(8,128)(2,1)S(1)}, u32[]{:S(2)}, u32[]{:S(2)}) collective-permute-start(bf16[16,512]{1,0:T(8,128)(2,1)S(1)} %get-tuple-element.46), channel_id=1, source_target_pairs={{0,8},{8,0},{1,9},{9,1},{2,10},{10,2},{3,11},{11,3},{4,12},{12,4},... | collective-permute-start | bytes 49160 | tf_op jit(solution)/shard_map/ppermute | solution.py:328
  39.6 5.8 %collective-permute-start.3 = (bf16[4,2,2,64,512]{4,3,2,1,0:T(8,128)(2,1)S(1)}, bf16[4,2,2,64,512]{4,3,2,1,0:T(8,128)(2,1)S(1)}, u32[]{:S(2)}, u32[]{:S(2)}) collective-permute-start(bf16[4,2,2,64,512]{4,3,2,1,0:T(8,128)(2,1)S(1)} %all-to-all-done.own), channel_id=1, source_target_pairs={{0,8},{8,0},{1,9},{9,1},{2,10},{10,2},{3,11},{11,3},{4,12},{12,4},... | collective-permute-start | bytes 3145736 | tf_op jit(solution)/shard_map/ppermute | solution.py:328
  45.4 9.1 %copy-start = (bf16[1,128,512]{2,1,0:T(8,128)(2,1)S(1)}, bf16[1,128,512]{2,1,0:T(8,128)(2,1)}, u32[]{:S(2)}) copy-start(bf16[1,128,512]{2,1,0:T(8,128)(2,1)} %param.10) | copy-start | bytes 393220
  47.0 6.6 %collective-permute-start.4 = (bf16[16,512]{1,0:T(8,128)(2,1)S(1)}, bf16[16,512]{1,0:T(8,128)(2,1)S(1)}, u32[]{:S(2)}, u32[]{:S(2)}) collective-permute-start(bf16[16,512]{1,0:T(8,128)(2,1)S(1)} %get-tuple-element.53), channel_id=1, source_target_pairs={{0,504},{8,16},{16,8},{24,32},{32,24},{40,48},{48,40},{56,64},{64,... | collective-permute-start | bytes 49160 | tf_op jit(solution)/shard_map/ppermute | solution.py:333
  48.9 5.5 %collective-permute-start.5 = (bf16[16,512]{1,0:T(8,128)(2,1)S(1)}, bf16[16,512]{1,0:T(8,128)(2,1)S(1)}, u32[]{:S(2)}, u32[]{:S(2)}) collective-permute-start(bf16[16,512]{1,0:T(8,128)(2,1)S(1)} %get-tuple-element.54), channel_id=1, source_target_pairs={{0,8},{8,0},{1,9},{9,1},{2,10},{10,2},{3,11},{11,3},{4,12},{12,4},... | collective-permute-start | bytes 49160 | tf_op jit(solution)/shard_map/ppermute | solution.py:328
  56.6 9.3 %collective-permute-start.6 = (bf16[16,512]{1,0:T(8,128)(2,1)S(1)}, bf16[16,512]{1,0:T(8,128)(2,1)S(1)}, u32[]{:S(2)}, u32[]{:S(2)}) collective-permute-start(bf16[16,512]{1,0:T(8,128)(2,1)S(1)} %get-tuple-element.59), channel_id=1, source_target_pairs={{0,504},{8,16},{16,8},{24,32},{32,24},{40,48},{48,40},{56,64},{64,... | collective-permute-start | bytes 49160 | tf_op jit(solution)/shard_map/ppermute | solution.py:333
  58.5 7.3 %collective-permute-start.7 = (bf16[16,512]{1,0:T(8,128)(2,1)S(1)}, bf16[16,512]{1,0:T(8,128)(2,1)S(1)}, u32[]{:S(2)}, u32[]{:S(2)}) collective-permute-start(bf16[16,512]{1,0:T(8,128)(2,1)S(1)} %get-tuple-element.60), channel_id=1, source_target_pairs={{0,8},{8,0},{1,9},{9,1},{2,10},{10,2},{3,11},{11,3},{4,12},{12,4},... | collective-permute-start | bytes 49160 | tf_op jit(solution)/shard_map/ppermute | solution.py:328
  66.7 5.2 %collective-permute-start.8 = (bf16[624,512]{1,0:T(8,128)(2,1)S(1)}, bf16[624,512]{1,0:T(8,128)(2,1)S(1)}, u32[]{:S(2)}, u32[]{:S(2)}) collective-permute-start(bf16[624,512]{1,0:T(8,128)(2,1)S(1)} %get-tuple-element.65.pack), channel_id=1, source_target_pairs={{0,8},{8,0},{1,9},{9,1},{2,10},{10,2},{3,11},{11,3},{4,12},{12,4},... | collective-permute-start | bytes 1916936 | tf_op jit(solution)/shard_map/ppermute | solution.py:328
  113.1 17.3 %all-to-all-start.3 = ((bf16[32,8,384]{2,1,0:T(8,128)(2,1)}), bf16[32,8,384]{2,1,0:T(8,128)(2,1)S(1)}, u32[]{:S(2)}, u32[]{:S(2)}) async-start(bf16[32,8,384]{2,1,0:T(8,128)(2,1)} %second_sum.1), calls=%async_computation.3 | async-start | bytes 393216 | tf_op jit(solution)/shard_map/all_to_all | solution.py:397
  119.9 9.5 %collective-permute-start.9 = (bf16[16,512]{1,0:T(8,128)(2,1)S(1)}, bf16[16,512]{1,0:T(8,128)(2,1)S(1)}, u32[]{:S(2)}, u32[]{:S(2)}) collective-permute-start(bf16[16,512]{1,0:T(8,128)(2,1)S(1)} %get-tuple-element.77), channel_id=1, source_target_pairs={{0,504},{8,16},{16,8},{24,32},{32,24},{40,48},{48,40},{56,64},{64,... | collective-permute-start | bytes 49160 | tf_op jit(solution)/shard_map/ppermute | solution.py:333
  124.6 5.5 %collective-permute-start.10 = (bf16[16,512]{1,0:T(8,128)(2,1)S(1)}, bf16[16,512]{1,0:T(8,128)(2,1)S(1)}, u32[]{:S(2)}, u32[]{:S(2)}) collective-permute-start(bf16[16,512]{1,0:T(8,128)(2,1)S(1)} %get-tuple-element.78), channel_id=1, source_target_pairs={{0,8},{8,0},{1,9},{9,1},{2,10},{10,2},{3,11},{11,3},{4,12},{12,4},... | collective-permute-start | bytes 49160 | tf_op jit(solution)/shard_map/ppermute | solution.py:328
  130.4 5.8 %collective-permute-start.11 = (bf16[32,8,384]{2,1,0:T(8,128)(2,1)S(1)}, bf16[32,8,384]{2,1,0:T(8,128)(2,1)S(1)}, u32[]{:S(2)}, u32[]{:S(2)}) collective-permute-start(bf16[32,8,384]{2,1,0:T(8,128)(2,1)S(1)} %all-to-all-done.3.own), channel_id=1, source_target_pairs={{0,8},{8,0},{1,9},{9,1},{2,10},{10,2},{3,11},{11,3},{4,12},{12,4},... | collective-permute-start | bytes 589832 | tf_op jit(solution)/shard_map/ppermute | solution.py:328

commit v6 on v5

--- a/solution.py
+++ b/solution.py
@@ -286,12 +286,13 @@
     for source in range(1, 4):
         total = total + parts[source].astype(F32)
     gains = [total[512 + layer : 513 + layer, half : half + 128] for layer in range(2) for half in (0, 128)]
-    gain = jnp.concatenate(gains + [jnp.zeros((4, 128), F32)], axis=0).astype(BF)
+    gain = jnp.concatenate(gains, axis=0).astype(BF)
     for y in range(8):
         for z in range(8):
             start = z * 64 + y * 8
-            pieces[y * 8 + z, :, 0:HALF] = total[start : start + 8].astype(BF)
-            pieces[y * 8 + z, :, HALF:] = gain
+            pieces[y * 8 + z, :, 0:HALF] = total[start : start + 4].astype(BF)
+            pieces[y * 8 + z, :, HALF:D] = total[start + 4 : start + 8].astype(BF)
+            pieces[y * 8 + z, :, D:] = gain
 
 
 def second_sum_kernel(parts, copies):
@@ -313,12 +314,14 @@
         for matrix in range(4):
             out = (send_grad, recv_grad)[matrix // 2]
             for y in range(8):
-                out[matrix % 2, y * 8 : y * 8 + 8, columns] = value[y * 4 + matrix, :, 0:HALF]
+                piece = value[y * 4 + matrix]
+                out[matrix % 2, y * 8 : y * 8 + 4, columns] = piece[:, 0:HALF]
+                out[matrix % 2, y * 8 + 4 : y * 8 + 8, columns] = piece[:, HALF:D]
         for layer in range(2):
             for half in range(2):
                 start = side * HALF + half * 128
                 row = layer * 2 + half
-                gain_grad[layer : layer + 1, start : start + 128] = value[0, row : row + 1, HALF:]
+                gain_grad[layer : layer + 1, start : start + 128] = value[0, row : row + 1, D:]
 
 
 GRAPH = ("y", "zl", "c")
@@ -390,10 +393,10 @@
     peer_pack, grad_0, outer, inner = lax.optimization_barrier((peer_pack, grad_0, outer, inner))
     (chunks,) = call(terms_kernel, [((4, 528, HALF), BF)], "terms", pack, keep, peer_pack)
     parts = lax.all_to_all(chunks, ("x",), 0, 0, tiled=True)
-    (pieces,) = call(first_sum_kernel, [((PARTS, 8, HALF + 128), BF)], "first_sum", parts)
+    (pieces,) = call(first_sum_kernel, [((PARTS, 4, D + 128), BF)], "first_sum", parts)
     parts = lax.all_to_all(pieces, ("y", "zh", "zl"), 0, 0, tiled=True)
     parts, outer, inner = lax.optimization_barrier((parts, outer, inner))
-    (copies,) = call(second_sum_kernel, [((32, 8, HALF + 128), BF)], "second_sum", parts)
+    (copies,) = call(second_sum_kernel, [((32, 4, D + 128), BF)], "second_sum", parts)
     mine = lax.all_to_all(copies, ("y", "zl"), 0, 0, tiled=True)
     mine, *back = lax.optimization_barrier((mine, *exchange(outer, inner)))
     theirs = swap(mine, "c")

time: 138 us -> 136 us (0.986)
  transfers between devices with their start and end apart: 14 -> 14, of which waited for: 9 -> 8; matrix products, arithmetic and copies ran while one was open for 0% -> 0% of each run, Pallas kernels for 2% -> 2%
where the time goes in v6:
time: 136 us; the launch traced here: 135 us
  starting transfers between devices  64.4 us (47%)
  blocking collectives  38.9 us (29%)
  waiting for transfers between devices  18.7 us (14%)
  Pallas kernels  9.78 us (7%)
  between operations  1.54 us (1%)
    ppermute x7, starting transfers between devices, swap(): return lax.ppermute(value, axis, [(0, 1), (1, 0)])  32 us
    all_to_all x1, blocking collectives, shards(): parts = lax.all_to_all(pieces, ('y', 'zh', 'zl'), 0, 0, tiled=True)  21.5 us
    all_to_all x1, blocking collectives, shards(): parts = lax.all_to_all(chunks, ('x',), 0, 0, tiled=True)  17.4 us
    ppermute x1, starting transfers between devices, shards(): other = lax.ppermute(half, ('zl', 'zh'), [(i, 7 - i) for i in range(8)])  11.5 us
    ppermute x4, starting transfers between devices, exchange(): return (lax.ppermute(outer, GRAPH, pairs), swap(inner, 'c'))  10.6 us
    pallas_call x11, Pallas kernels, call(): pl.pallas_call(kernel, out_shape=[jax.ShapeDtypeStruct(s, t) for s, t in...  9.78 us
    ppermute x1, waiting for transfers between devices, shards(): other = lax.ppermute(half, ('zl', 'zh'), [(i, 7 - i) for i in range(8)])  6.75 us
    all_to_all x1, starting transfers between devices, shards(): mine = lax.all_to_all(copies, ('y', 'zl'), 0, 0, tiled=True)  6.15 us
  transfers between devices with their start and end apart: 14, of which 8 were waited for; matrix products, arithmetic and copies ran while one was open for 0% of the time, Pallas kernels for 2%

profile of v6, /device:TPU:1, one launch (start us, length us, event | category | flops | bytes accessed | tf_op | source)
XLA Modules:
  0.0 135.4 jit_solution(12161662977136686381)
XLA Ops:
  1.6 11.5 %collective-permute-start = (bf16[2,64,512]{2,1,0:T(8,128)(2,1)S(1)}, bf16[2,64,512]{2,1,0:T(8,128)(2,1)S(1)}, u32[]{:S(2)}, u32[]{:S(2)}) collective-permute-start(bf16[2,64,512]{2,1,0:T(8,128)(2,1)S(1)} %broadcast_select_fusion), channel_id=1, source_target_pairs={{0,52},{4,48},{16,36},{20,32},{32,20},{36,16},{48,4},{52,0},{1,53}... | collective-permute-start | bytes 393224 | tf_op jit(solution)/shard_map/ppermute | solution.py:345
  13.1 6.8 %collective-permute-done = bf16[2,64,512]{2,1,0:T(8,128)(2,1)S(1)} collective-permute-done((bf16[2,64,512]{2,1,0:T(8,128)(2,1)S(1)}, bf16[2,64,512]{2,1,0:T(8,128)(2,1)S(1)}, u32[]{:S(2)}, u32[]{:S(2)}) %collective-permute-start) | collective-permute-done | bytes 131104 | tf_op jit(solution)/shard_map/ppermute | solution.py:345
  19.9 1.1 broadcast_in_dim.12
  21.0 4.2 %all-to-all-start = ((bf16[4,2,2,64,512]{4,3,2,1,0:T(8,128)(2,1)}), bf16[4,2,2,64,512]{4,3,2,1,0:T(8,128)(2,1)S(1)}, u32[]{:S(2)}, u32[]{:S(2)}) async-start(bf16[4,2,2,64,512]{4,3,2,1,0:T(8,128)(2,1)} %broadcast_in_dim.12), calls=%async_computation | async-start | bytes 2097152 | tf_op jit(solution)/shard_map/all_to_all | solution.py:355
  26.1 1.9 %collective-permute-start.1 = (bf16[16,512]{1,0:T(8,128)(2,1)S(1)}, bf16[16,512]{1,0:T(8,128)(2,1)S(1)}, u32[]{:S(2)}, u32[]{:S(2)}) collective-permute-start(bf16[16,512]{1,0:T(8,128)(2,1)S(1)} %get-tuple-element.45), channel_id=1, source_target_pairs={{0,504},{8,16},{16,8},{24,32},{32,24},{40,48},{48,40},{56,64},{64,... | collective-permute-start | bytes 49160 | tf_op jit(solution)/shard_map/ppermute | solution.py:336
  28.1 4.7 %collective-permute-start.2 = (bf16[16,512]{1,0:T(8,128)(2,1)S(1)}, bf16[16,512]{1,0:T(8,128)(2,1)S(1)}, u32[]{:S(2)}, u32[]{:S(2)}) collective-permute-start(bf16[16,512]{1,0:T(8,128)(2,1)S(1)} %get-tuple-element.46), channel_id=1, source_target_pairs={{0,8},{8,0},{1,9},{9,1},{2,10},{10,2},{3,11},{11,3},{4,12},{12,4},... | collective-permute-start | bytes 49160 | tf_op jit(solution)/shard_map/ppermute | solution.py:331
  33.6 6.0 %all-to-all-done.own = bf16[4,2,2,64,512]{4,3,2,1,0:T(8,128)(2,1)S(1)} async-done(((bf16[4,2,2,64,512]{4,3,2,1,0:T(8,128)(2,1)}), bf16[4,2,2,64,512]{4,3,2,1,0:T(8,128)(2,1)S(1)}, u32[]{:S(2)}, u32[]{:S(2)}) %all-to-all-start) | async-done | bytes 1048608 | tf_op jit(solution)/shard_map/all_to_all | solution.py:355
  39.6 3.5 %collective-permute-start.3 = (bf16[4,2,2,64,512]{4,3,2,1,0:T(8,128)(2,1)S(1)}, bf16[4,2,2,64,512]{4,3,2,1,0:T(8,128)(2,1)S(1)}, u32[]{:S(2)}, u32[]{:S(2)}) collective-permute-start(bf16[4,2,2,64,512]{4,3,2,1,0:T(8,128)(2,1)S(1)} %all-to-all-done.own), channel_id=1, source_target_pairs={{0,8},{8,0},{1,9},{9,1},{2,10},{10,2},{3,11},{11,3},{4,12},{12,4},... | collective-permute-start | bytes 3145736 | tf_op jit(solution)/shard_map/ppermute | solution.py:331
  43.1 2.3 %collective-permute-done.3.peer = bf16[4,2,2,64,512]{4,3,2,1,0:T(8,128)(2,1)S(1)} collective-permute-done((bf16[4,2,2,64,512]{4,3,2,1,0:T(8,128)(2,1)S(1)}, bf16[4,2,2,64,512]{4,3,2,1,0:T(8,128)(2,1)S(1)}, u32[]{:S(2)}, u32[]{:S(2)}) %collective-permute-start.3) | collective-permute-done | bytes 1048608 | tf_op jit(solution)/shard_map/ppermute | solution.py:331
  45.4 1.6 %first_layer.1 = (bf16[128,512]{1,0:T(8,128)(2,1)S(1)}, f32[128,512]{1,0:T(8,128)S(1)}, f32[512,512]{1,0:T(8,128)S(1)}, bf16[16,512]{1,0:T(8,128)(2,1)S(1)}, bf16[16,512]{1,0:T(8,128)(2,1)S(1)}) custom-call(s32[1,1]{1,0:T(1,128)} %bitcast.core, bf16[128,512]{1,0:T(8,128)(2,1)S(1)} %bitcast.14, bf16[16,512]{1,0:T(8,128)(2,1)S(1)} %collective-permute-done.1.outer.outer_0, ...), custom_call_target="tpu_custom_call" | custom-call | flops 100000000 | bytes 2000000 | tf_op jit(solution)/shard_map/first_layer/pallas_call | solution.py:50
  47.0 1.9 %collective-permute-start.4 = (bf16[16,512]{1,0:T(8,128)(2,1)S(1)}, bf16[16,512]{1,0:T(8,128)(2,1)S(1)}, u32[]{:S(2)}, u32[]{:S(2)}) collective-permute-start(bf16[16,512]{1,0:T(8,128)(2,1)S(1)} %get-tuple-element.53), channel_id=1, source_target_pairs={{0,504},{8,16},{16,8},{24,32},{32,24},{40,48},{48,40},{56,64},{64,... | collective-permute-start | bytes 49160 | tf_op jit(solution)/shard_map/ppermute | solution.py:336
  48.9 4.7 %collective-permute-start.5 = (bf16[16,512]{1,0:T(8,128)(2,1)S(1)}, bf16[16,512]{1,0:T(8,128)(2,1)S(1)}, u32[]{:S(2)}, u32[]{:S(2)}) collective-permute-start(bf16[16,512]{1,0:T(8,128)(2,1)S(1)} %get-tuple-element.54), channel_id=1, source_target_pairs={{0,8},{8,0},{1,9},{9,1},{2,10},{10,2},{3,11},{11,3},{4,12},{12,4},... | collective-permute-start | bytes 49160 | tf_op jit(solution)/shard_map/ppermute | solution.py:331
  54.5 2.1 %last_layer.1 = (bf16[16,512]{1,0:T(8,128)(2,1)S(1)}, bf16[16,512]{1,0:T(8,128)(2,1)S(1)}, f32[128,512]{1,0:T(8,128)S(1)}, bf16[304,512]{1,0:T(8,128)(2,1)S(1)}) custom-call(s32[1,1]{1,0:T(1,128)} %bitcast.core, bf16[128,512]{1,0:T(8,128)(2,1)S(1)} %get-tuple-element.52.rows.rows_1, bf16[16,512]{1,0:T(8,128)(2,1)S(1)} %collective-permute-done.4.outer.outer_1, ...), custom_call_target="tpu_custom_call" | custom-call | flops 100000000 | bytes 2000000 | tf_op jit(solution)/shard_map/last_layer/pallas_call | solution.py:50
  56.6 1.9 %collective-permute-start.6 = (bf16[16,512]{1,0:T(8,128)(2,1)S(1)}, bf16[16,512]{1,0:T(8,128)(2,1)S(1)}, u32[]{:S(2)}, u32[]{:S(2)}) collective-permute-start(bf16[16,512]{1,0:T(8,128)(2,1)S(1)} %get-tuple-element.59), channel_id=1, source_target_pairs={{0,504},{8,16},{16,8},{24,32},{32,24},{40,48},{48,40},{56,64},{64,... | collective-permute-start | bytes 49160 | tf_op jit(solution)/shard_map/ppermute | solution.py:336
  58.5 6.2 %collective-permute-start.7 = (bf16[16,512]{1,0:T(8,128)(2,1)S(1)}, bf16[16,512]{1,0:T(8,128)(2,1)S(1)}, u32[]{:S(2)}, u32[]{:S(2)}) collective-permute-start(bf16[16,512]{1,0:T(8,128)(2,1)S(1)} %get-tuple-element.60), channel_id=1, source_target_pairs={{0,8},{8,0},{1,9},{9,1},{2,10},{10,2},{3,11},{11,3},{4,12},{12,4},... | collective-permute-start | bytes 49160 | tf_op jit(solution)/shard_map/ppermute | solution.py:331
  64.8 1.1 last_rest.1
  66.7 3.5 %collective-permute-start.8 = (bf16[624,512]{1,0:T(8,128)(2,1)S(1)}, bf16[624,512]{1,0:T(8,128)(2,1)S(1)}, u32[]{:S(2)}, u32[]{:S(2)}) collective-permute-start(bf16[624,512]{1,0:T(8,128)(2,1)S(1)} %get-tuple-element.65.pack), channel_id=1, source_target_pairs={{0,8},{8,0},{1,9},{9,1},{2,10},{10,2},{3,11},{11,3},{4,12},{12,4},... | collective-permute-start | bytes 1916936 | tf_op jit(solution)/shard_map/ppermute | solution.py:331
  70.8 1.1 collective-permute-done.8.peer
  72.5 17.4 %all_to_all.20.parts = bf16[4,528,256]{2,1,0:T(8,128)(2,1)S(1)} all-to-all(bf16[4,528,256]{2,1,0:T(8,128)(2,1)S(1)} %terms.1), channel_id=1, replica_groups=mesh['y'=8,'zl'=4,'c'=2,'zh'=2,'x'=4] {'x'}, dimensions={0} | all-to-all | bytes 2162688 | tf_op jit(solution)/shard_map/all_to_all | solution.py:395
  90.2 21.5 %all_to_all.21.parts = bf16[64,4,640]{2,1,0:T(4,128)(2,1)S(1)} all-to-all(bf16[64,4,640]{2,1,0:T(4,128)(2,1)S(1)} %first_sum.1), channel_id=1, replica_groups=mesh['y'=8,'zl'=4,'c'=2,'zh'=2,'x'=4] {'y','zh','zl'}, dimensions={0} | all-to-all | bytes 655360 | tf_op jit(solution)/shard_map/all_to_all | solution.py:397
  112.4 6.1 %all-to-all-start.3 = ((bf16[32,4,640]{2,1,0:T(4,128)(2,1)}), bf16[32,4,640]{2,1,0:T(4,128)(2,1)S(1)}, u32[]{:S(2)}, u32[]{:S(2)}) async-start(bf16[32,4,640]{2,1,0:T(4,128)(2,1)} %second_sum.1), calls=%async_computation.3 | async-start | bytes 327680 | tf_op jit(solution)/shard_map/all_to_all | solution.py:400
  118.5 4.9 %collective-permute-start.9 = (bf16[16,512]{1,0:T(8,128)(2,1)S(1)}, bf16[16,512]{1,0:T(8,128)(2,1)S(1)}, u32[]{:S(2)}, u32[]{:S(2)}) collective-permute-start(bf16[16,512]{1,0:T(8,128)(2,1)S(1)} %get-tuple-element.77), channel_id=1, source_target_pairs={{0,504},{8,16},{16,8},{24,32},{32,24},{40,48},{48,40},{56,64},{64,... | collective-permute-start | bytes 49160 | tf_op jit(solution)/shard_map/ppermute | solution.py:336
  123.4 4.6 %collective-permute-start.10 = (bf16[16,512]{1,0:T(8,128)(2,1)S(1)}, bf16[16,512]{1,0:T(8,128)(2,1)S(1)}, u32[]{:S(2)}, u32[]{:S(2)}) collective-permute-start(bf16[16,512]{1,0:T(8,128)(2,1)S(1)} %get-tuple-element.78), channel_id=1, source_target_pairs={{0,8},{8,0},{1,9},{9,1},{2,10},{10,2},{3,11},{11,3},{4,12},{12,4},... | collective-permute-start | bytes 49160 | tf_op jit(solution)/shard_map/ppermute | solution.py:331
  128.8 4.7 %collective-permute-start.11 = (bf16[32,4,640]{2,1,0:T(4,128)(2,1)S(1)}, bf16[32,4,640]{2,1,0:T(4,128)(2,1)S(1)}, u32[]{:S(2)}, u32[]{:S(2)}) collective-permute-start(bf16[32,4,640]{2,1,0:T(4,128)(2,1)S(1)} %all-to-all-done.3.own), channel_id=1, source_target_pairs={{0,8},{8,0},{1,9},{9,1},{2,10},{10,2},{3,11},{11,3},{4,12},{12,4},... | collective-permute-start | bytes 491528 | tf_op jit(solution)/shard_map/ppermute | solution.py:331
  (33 shorter events, 8.5 us)
Async XLA Ops:
  1.6 18.3 %collective-permute-start = (bf16[2,64,512]{2,1,0:T(8,128)(2,1)S(1)}, bf16[2,64,512]{2,1,0:T(8,128)(2,1)S(1)}, u32[]{:S(2)}, u32[]{:S(2)}) collective-permute-start(bf16[2,64,512]{2,1,0:T(8,128)(2,1)S(1)} %broadcast_select_fusion), channel_id=1, source_target_pairs={{0,52},{4,48},{16,36},{20,32},{32,20},{36,16},{48,4},{52,0},{1,53}... | collective-permute-start | bytes 393224 | tf_op jit(solution)/shard_map/ppermute | solution.py:345
  21.0 4.8 %copy-start.1 = (bf16[1,128,512]{2,1,0:T(8,128)(2,1)S(1)}, bf16[1,128,512]{2,1,0:T(8,128)(2,1)}, u32[]{:S(2)}) copy-start(bf16[1,128,512]{2,1,0:T(8,128)(2,1)} %param.9) | copy-start | bytes 393220
  21.0 4.8 %copy-start.3 = (s32[1,2,8]{2,1,0:T(2,128)S(1)}, s32[1,2,8]{2,1,0:T(2,128)}, u32[]{:S(2)}) copy-start(s32[1,2,8]{2,1,0:T(2,128)} %send_rows.7) | copy-start | bytes 196
  21.0 4.8 %copy-start.4 = (s32[1,512]{1,0:T(1,128)S(1)}, s32[1,512]{1,0:T(1,128)}, u32[]{:S(2)}) copy-start(s32[1,512]{1,0:T(1,128)} %senders.1) | copy-start | bytes 6148
  21.0 4.9 %copy-start.5 = (s32[1,512]{1,0:T(1,128)S(1)}, s32[1,512]{1,0:T(1,128)}, u32[]{:S(2)}) copy-start(s32[1,512]{1,0:T(1,128)} %receivers.1) | copy-start | bytes 6148
  21.0 24.4 %copy-start.2 = (f32[2,512]{1,0:T(2,128)S(1)}, f32[2,512]{1,0:T(2,128)}, u32[]{:S(2)}) copy-start(f32[2,512]{1,0:T(2,128)} %gain.7) | copy-start | bytes 12292
  21.0 18.6 %all-to-all-start = ((bf16[4,2,2,64,512]{4,3,2,1,0:T(8,128)(2,1)}), bf16[4,2,2,64,512]{4,3,2,1,0:T(8,128)(2,1)S(1)}, u32[]{:S(2)}, u32[]{:S(2)}) async-start(bf16[4,2,2,64,512]{4,3,2,1,0:T(8,128)(2,1)} %broadcast_in_dim.12), calls=%async_computation | async-start | bytes 2097152 | tf_op jit(solution)/shard_map/all_to_all | solution.py:355
  26.1 6.6 %collective-permute-start.1 = (bf16[16,512]{1,0:T(8,128)(2,1)S(1)}, bf16[16,512]{1,0:T(8,128)(2,1)S(1)}, u32[]{:S(2)}, u32[]{:S(2)}) collective-permute-start(bf16[16,512]{1,0:T(8,128)(2,1)S(1)} %get-tuple-element.45), channel_id=1, source_target_pairs={{0,504},{8,16},{16,8},{24,32},{32,24},{40,48},{48,40},{56,64},{64,... | collective-permute-start | bytes 49160 | tf_op jit(solution)/shard_map/ppermute | solution.py:336
  28.1 5.5 %collective-permute-start.2 = (bf16[16,512]{1,0:T(8,128)(2,1)S(1)}, bf16[16,512]{1,0:T(8,128)(2,1)S(1)}, u32[]{:S(2)}, u32[]{:S(2)}) collective-permute-start(bf16[16,512]{1,0:T(8,128)(2,1)S(1)} %get-tuple-element.46), channel_id=1, source_target_pairs={{0,8},{8,0},{1,9},{9,1},{2,10},{10,2},{3,11},{11,3},{4,12},{12,4},... | collective-permute-start | bytes 49160 | tf_op jit(solution)/shard_map/ppermute | solution.py:331
  39.6 5.8 %collective-permute-start.3 = (bf16[4,2,2,64,512]{4,3,2,1,0:T(8,128)(2,1)S(1)}, bf16[4,2,2,64,512]{4,3,2,1,0:T(8,128)(2,1)S(1)}, u32[]{:S(2)}, u32[]{:S(2)}) collective-permute-start(bf16[4,2,2,64,512]{4,3,2,1,0:T(8,128)(2,1)S(1)} %all-to-all-done.own), channel_id=1, source_target_pairs={{0,8},{8,0},{1,9},{9,1},{2,10},{10,2},{3,11},{11,3},{4,12},{12,4},... | collective-permute-start | bytes 3145736 | tf_op jit(solution)/shard_map/ppermute | solution.py:331
  45.4 9.1 %copy-start = (bf16[1,128,512]{2,1,0:T(8,128)(2,1)S(1)}, bf16[1,128,512]{2,1,0:T(8,128)(2,1)}, u32[]{:S(2)}) copy-start(bf16[1,128,512]{2,1,0:T(8,128)(2,1)} %param.10) | copy-start | bytes 393220
  47.0 6.6 %collective-permute-start.4 = (bf16[16,512]{1,0:T(8,128)(2,1)S(1)}, bf16[16,512]{1,0:T(8,128)(2,1)S(1)}, u32[]{:S(2)}, u32[]{:S(2)}) collective-permute-start(bf16[16,512]{1,0:T(8,128)(2,1)S(1)} %get-tuple-element.53), channel_id=1, source_target_pairs={{0,504},{8,16},{16,8},{24,32},{32,24},{40,48},{48,40},{56,64},{64,... | collective-permute-start | bytes 49160 | tf_op jit(solution)/shard_map/ppermute | solution.py:336
  48.9 5.5 %collective-permute-start.5 = (bf16[16,512]{1,0:T(8,128)(2,1)S(1)}, bf16[16,512]{1,0:T(8,128)(2,1)S(1)}, u32[]{:S(2)}, u32[]{:S(2)}) collective-permute-start(bf16[16,512]{1,0:T(8,128)(2,1)S(1)} %get-tuple-element.54), channel_id=1, source_target_pairs={{0,8},{8,0},{1,9},{9,1},{2,10},{10,2},{3,11},{11,3},{4,12},{12,4},... | collective-permute-start | bytes 49160 | tf_op jit(solution)/shard_map/ppermute | solution.py:331
  56.6 9.3 %collective-permute-start.6 = (bf16[16,512]{1,0:T(8,128)(2,1)S(1)}, bf16[16,512]{1,0:T(8,128)(2,1)S(1)}, u32[]{:S(2)}, u32[]{:S(2)}) collective-permute-start(bf16[16,512]{1,0:T(8,128)(2,1)S(1)} %get-tuple-element.59), channel_id=1, source_target_pairs={{0,504},{8,16},{16,8},{24,32},{32,24},{40,48},{48,40},{56,64},{64,... | collective-permute-start | bytes 49160 | tf_op jit(solution)/shard_map/ppermute | solution.py:336
  58.5 7.3 %collective-permute-start.7 = (bf16[16,512]{1,0:T(8,128)(2,1)S(1)}, bf16[16,512]{1,0:T(8,128)(2,1)S(1)}, u32[]{:S(2)}, u32[]{:S(2)}) collective-permute-start(bf16[16,512]{1,0:T(8,128)(2,1)S(1)} %get-tuple-element.60), channel_id=1, source_target_pairs={{0,8},{8,0},{1,9},{9,1},{2,10},{10,2},{3,11},{11,3},{4,12},{12,4},... | collective-permute-start | bytes 49160 | tf_op jit(solution)/shard_map/ppermute | solution.py:331
  66.7 5.2 %collective-permute-start.8 = (bf16[624,512]{1,0:T(8,128)(2,1)S(1)}, bf16[624,512]{1,0:T(8,128)(2,1)S(1)}, u32[]{:S(2)}, u32[]{:S(2)}) collective-permute-start(bf16[624,512]{1,0:T(8,128)(2,1)S(1)} %get-tuple-element.65.pack), channel_id=1, source_target_pairs={{0,8},{8,0},{1,9},{9,1},{2,10},{10,2},{3,11},{11,3},{4,12},{12,4},... | collective-permute-start | bytes 1916936 | tf_op jit(solution)/shard_map/ppermute | solution.py:331
  112.4 16.4 %all-to-all-start.3 = ((bf16[32,4,640]{2,1,0:T(4,128)(2,1)}), bf16[32,4,640]{2,1,0:T(4,128)(2,1)S(1)}, u32[]{:S(2)}, u32[]{:S(2)}) async-start(bf16[32,4,640]{2,1,0:T(4,128)(2,1)} %second_sum.1), calls=%async_computation.3 | async-start | bytes 327680 | tf_op jit(solution)/shard_map/all_to_all | solution.py:400
  118.5 9.5 %collective-permute-start.9 = (bf16[16,512]{1,0:T(8,128)(2,1)S(1)}, bf16[16,512]{1,0:T(8,128)(2,1)S(1)}, u32[]{:S(2)}, u32[]{:S(2)}) collective-permute-start(bf16[16,512]{1,0:T(8,128)(2,1)S(1)} %get-tuple-element.77), channel_id=1, source_target_pairs={{0,504},{8,16},{16,8},{24,32},{32,24},{40,48},{48,40},{56,64},{64,... | collective-permute-start | bytes 49160 | tf_op jit(solution)/shard_map/ppermute | solution.py:336
  123.4 5.4 %collective-permute-start.10 = (bf16[16,512]{1,0:T(8,128)(2,1)S(1)}, bf16[16,512]{1,0:T(8,128)(2,1)S(1)}, u32[]{:S(2)}, u32[]{:S(2)}) collective-permute-start(bf16[16,512]{1,0:T(8,128)(2,1)S(1)} %get-tuple-element.78), channel_id=1, source_target_pairs={{0,8},{8,0},{1,9},{9,1},{2,10},{10,2},{3,11},{11,3},{4,12},{12,4},... | collective-permute-start | bytes 49160 | tf_op jit(solution)/shard_map/ppermute | solution.py:331
  128.8 5.7 %collective-permute-start.11 = (bf16[32,4,640]{2,1,0:T(4,128)(2,1)S(1)}, bf16[32,4,640]{2,1,0:T(4,128)(2,1)S(1)}, u32[]{:S(2)}, u32[]{:S(2)}) collective-permute-start(bf16[32,4,640]{2,1,0:T(4,128)(2,1)S(1)} %all-to-all-done.3.own), channel_id=1, source_target_pairs={{0,8},{8,0},{1,9},{9,1},{2,10},{10,2},{3,11},{11,3},{4,12},{12,4},... | collective-permute-start | bytes 491528 | tf_op jit(solution)/shard_map/ppermute | solution.py:331

commit v7 on v5

--- a/solution.py
+++ b/solution.py
@@ -286,12 +286,14 @@
     for source in range(1, 4):
         total = total + parts[source].astype(F32)
     gains = [total[512 + layer : 513 + layer, half : half + 128] for layer in range(2) for half in (0, 128)]
-    gain = jnp.concatenate(gains + [jnp.zeros((4, 128), F32)], axis=0).astype(BF)
+    gain = [jnp.concatenate(gains[2 * layer : 2 * layer + 2], axis=0).astype(BF) for layer in range(2)]
     for y in range(8):
         for z in range(8):
             start = z * 64 + y * 8
-            pieces[y * 8 + z, :, 0:HALF] = total[start : start + 8].astype(BF)
-            pieces[y * 8 + z, :, HALF:] = gain
+            for pair in range(4):
+                rows = total[start + 2 * pair : start + 2 * pair + 2]
+                pieces[y * 8 + z, :, pair * HALF : (pair + 1) * HALF] = rows.astype(BF)
+            pieces[y * 8 + z, :, 2 * D :] = gain[y % 2]
 
 
 def second_sum_kernel(parts, copies):
@@ -313,12 +315,14 @@
         for matrix in range(4):
             out = (send_grad, recv_grad)[matrix // 2]
             for y in range(8):
-                out[matrix % 2, y * 8 : y * 8 + 8, columns] = value[y * 4 + matrix, :, 0:HALF]
+                piece = value[y * 4 + matrix]
+                for pair in range(4):
+                    start = y * 8 + 2 * pair
+                    out[matrix % 2, start : start + 2, columns] = piece[:, pair * HALF : (pair + 1) * HALF]
         for layer in range(2):
             for half in range(2):
                 start = side * HALF + half * 128
-                row = layer * 2 + half
-                gain_grad[layer : layer + 1, start : start + 128] = value[0, row : row + 1, HALF:]
+                gain_grad[layer : layer + 1, start : start + 128] = value[layer * 4, half : half + 1, 2 * D :]
 
 
 GRAPH = ("y", "zl", "c")
@@ -390,10 +394,10 @@
     peer_pack, grad_0, outer, inner = lax.optimization_barrier((peer_pack, grad_0, outer, inner))
     (chunks,) = call(terms_kernel, [((4, 528, HALF), BF)], "terms", pack, keep, peer_pack)
     parts = lax.all_to_all(chunks, ("x",), 0, 0, tiled=True)
-    (pieces,) = call(first_sum_kernel, [((PARTS, 8, HALF + 128), BF)], "first_sum", parts)
+    (pieces,) = call(first_sum_kernel, [((PARTS, 2, 2 * D + 128), BF)], "first_sum", parts)
     parts = lax.all_to_all(pieces, ("y", "zh", "zl"), 0, 0, tiled=True)
     parts, outer, inner = lax.optimization_barrier((parts, outer, inner))
-    (copies,) = call(second_sum_kernel, [((32, 8, HALF + 128), BF)], "second_sum", parts)
+    (copies,) = call(second_sum_kernel, [((32, 2, 2 * D + 128), BF)], "second_sum", parts)
     mine = lax.all_to_all(copies, ("y", "zl"), 0, 0, tiled=True)
     mine, *back = lax.optimization_barrier((mine, *exchange(outer, inner)))
     theirs = swap(mine, "c")

time: 138 us -> 135 us (0.978)
    all_to_all x1, starting transfers between devices: 6.72 us -> 5.22 us  [shards(): mine = lax.all_to_all(copies, ('y', 'zl'), 0, 0, tiled=True)]
  transfers between devices with their start and end apart: 14 -> 14, of which waited for: 9 -> 8; matrix products, arithmetic and copies ran while one was open for 0% -> 0% of each run, Pallas kernels for 2% -> 2%
where the time goes in v7:
time: 135 us
  starting transfers between devices  64.1 us (47%)
  blocking collectives  38.5 us (29%)
  waiting for transfers between devices  18.6 us (14%)
  Pallas kernels  9.87 us (7%)
  between operations  1.54 us (1%)
    ppermute x7, starting transfers between devices, swap(): return lax.ppermute(value, axis, [(0, 1), (1, 0)])  31.8 us
    all_to_all x1, blocking collectives, shards(): parts = lax.all_to_all(pieces, ('y', 'zh', 'zl'), 0, 0, tiled=True)  21.1 us
    all_to_all x1, blocking collectives, shards(): parts = lax.all_to_all(chunks, ('x',), 0, 0, tiled=True)  17.4 us
    ppermute x1, starting transfers between devices, shards(): other = lax.ppermute(half, ('zl', 'zh'), [(i, 7 - i) for i in range(8)])  11.5 us
    ppermute x4, starting transfers between devices, exchange(): return (lax.ppermute(outer, GRAPH, pairs), swap(inner, 'c'))  11.4 us
    pallas_call x11, Pallas kernels, call(): pl.pallas_call(kernel, out_shape=[jax.ShapeDtypeStruct(s, t) for s, t in...  9.87 us
    ppermute x1, waiting for transfers between devices, shards(): other = lax.ppermute(half, ('zl', 'zh'), [(i, 7 - i) for i in range(8)])  6.75 us
    all_to_all x1, waiting for transfers between devices, shards(): own = lax.all_to_all(copies, ('x',), 0, 0, tiled=True)  6 us
  transfers between devices with their start and end apart: 14, of which 8 were waited for; matrix products, arithmetic and copies ran while one was open for 0% of the time, Pallas kernels for 2%

profile of v7, /device:TPU:1, one launch (start us, length us, event | category | flops | bytes accessed | tf_op | source)
XLA Modules:
  0.0 134.8 jit_solution(3986995255558854312)
XLA Ops:
  1.6 11.5 %collective-permute-start = (bf16[2,64,512]{2,1,0:T(8,128)(2,1)S(1)}, bf16[2,64,512]{2,1,0:T(8,128)(2,1)S(1)}, u32[]{:S(2)}, u32[]{:S(2)}) collective-permute-start(bf16[2,64,512]{2,1,0:T(8,128)(2,1)S(1)} %broadcast_select_fusion), channel_id=1, source_target_pairs={{0,52},{4,48},{16,36},{20,32},{32,20},{36,16},{48,4},{52,0},{1,53}... | collective-permute-start | bytes 393224 | tf_op jit(solution)/shard_map/ppermute | solution.py:346
  13.1 6.8 %collective-permute-done = bf16[2,64,512]{2,1,0:T(8,128)(2,1)S(1)} collective-permute-done((bf16[2,64,512]{2,1,0:T(8,128)(2,1)S(1)}, bf16[2,64,512]{2,1,0:T(8,128)(2,1)S(1)}, u32[]{:S(2)}, u32[]{:S(2)}) %collective-permute-start) | collective-permute-done | bytes 131104 | tf_op jit(solution)/shard_map/ppermute | solution.py:346
  19.9 1.1 broadcast_in_dim.12
  21.0 4.2 %all-to-all-start = ((bf16[4,2,2,64,512]{4,3,2,1,0:T(8,128)(2,1)}), bf16[4,2,2,64,512]{4,3,2,1,0:T(8,128)(2,1)S(1)}, u32[]{:S(2)}, u32[]{:S(2)}) async-start(bf16[4,2,2,64,512]{4,3,2,1,0:T(8,128)(2,1)} %broadcast_in_dim.12), calls=%async_computation | async-start | bytes 2097152 | tf_op jit(solution)/shard_map/all_to_all | solution.py:356
  26.1 1.9 %collective-permute-start.1 = (bf16[16,512]{1,0:T(8,128)(2,1)S(1)}, bf16[16,512]{1,0:T(8,128)(2,1)S(1)}, u32[]{:S(2)}, u32[]{:S(2)}) collective-permute-start(bf16[16,512]{1,0:T(8,128)(2,1)S(1)} %get-tuple-element.45), channel_id=1, source_target_pairs={{0,504},{8,16},{16,8},{24,32},{32,24},{40,48},{48,40},{56,64},{64,... | collective-permute-start | bytes 49160 | tf_op jit(solution)/shard_map/ppermute | solution.py:337
  28.1 4.7 %collective-permute-start.2 = (bf16[16,512]{1,0:T(8,128)(2,1)S(1)}, bf16[16,512]{1,0:T(8,128)(2,1)S(1)}, u32[]{:S(2)}, u32[]{:S(2)}) collective-permute-start(bf16[16,512]{1,0:T(8,128)(2,1)S(1)} %get-tuple-element.46), channel_id=1, source_target_pairs={{0,8},{8,0},{1,9},{9,1},{2,10},{10,2},{3,11},{11,3},{4,12},{12,4},... | collective-permute-start | bytes 49160 | tf_op jit(solution)/shard_map/ppermute | solution.py:332
  33.6 6.0 %all-to-all-done.own = bf16[4,2,2,64,512]{4,3,2,1,0:T(8,128)(2,1)S(1)} async-done(((bf16[4,2,2,64,512]{4,3,2,1,0:T(8,128)(2,1)}), bf16[4,2,2,64,512]{4,3,2,1,0:T(8,128)(2,1)S(1)}, u32[]{:S(2)}, u32[]{:S(2)}) %all-to-all-start) | async-done | bytes 1048608 | tf_op jit(solution)/shard_map/all_to_all | solution.py:356
  39.6 3.5 %collective-permute-start.3 = (bf16[4,2,2,64,512]{4,3,2,1,0:T(8,128)(2,1)S(1)}, bf16[4,2,2,64,512]{4,3,2,1,0:T(8,128)(2,1)S(1)}, u32[]{:S(2)}, u32[]{:S(2)}) collective-permute-start(bf16[4,2,2,64,512]{4,3,2,1,0:T(8,128)(2,1)S(1)} %all-to-all-done.own), channel_id=1, source_target_pairs={{0,8},{8,0},{1,9},{9,1},{2,10},{10,2},{3,11},{11,3},{4,12},{12,4},... | collective-permute-start | bytes 3145736 | tf_op jit(solution)/shard_map/ppermute | solution.py:332
  43.1 2.3 %collective-permute-done.3.peer = bf16[4,2,2,64,512]{4,3,2,1,0:T(8,128)(2,1)S(1)} collective-permute-done((bf16[4,2,2,64,512]{4,3,2,1,0:T(8,128)(2,1)S(1)}, bf16[4,2,2,64,512]{4,3,2,1,0:T(8,128)(2,1)S(1)}, u32[]{:S(2)}, u32[]{:S(2)}) %collective-permute-start.3) | collective-permute-done | bytes 1048608 | tf_op jit(solution)/shard_map/ppermute | solution.py:332
  45.4 1.6 %first_layer.1 = (bf16[128,512]{1,0:T(8,128)(2,1)S(1)}, f32[128,512]{1,0:T(8,128)S(1)}, f32[512,512]{1,0:T(8,128)S(1)}, bf16[16,512]{1,0:T(8,128)(2,1)S(1)}, bf16[16,512]{1,0:T(8,128)(2,1)S(1)}) custom-call(s32[1,1]{1,0:T(1,128)} %bitcast.core, bf16[128,512]{1,0:T(8,128)(2,1)S(1)} %bitcast.14, bf16[16,512]{1,0:T(8,128)(2,1)S(1)} %collective-permute-done.1.outer.outer_0, ...), custom_call_target="tpu_custom_call" | custom-call | flops 100000000 | bytes 2000000 | tf_op jit(solution)/shard_map/first_layer/pallas_call | solution.py:50
  47.0 1.9 %collective-permute-start.4 = (bf16[16,512]{1,0:T(8,128)(2,1)S(1)}, bf16[16,512]{1,0:T(8,128)(2,1)S(1)}, u32[]{:S(2)}, u32[]{:S(2)}) collective-permute-start(bf16[16,512]{1,0:T(8,128)(2,1)S(1)} %get-tuple-element.53), channel_id=1, source_target_pairs={{0,504},{8,16},{16,8},{24,32},{32,24},{40,48},{48,40},{56,64},{64,... | collective-permute-start | bytes 49160 | tf_op jit(solution)/shard_map/ppermute | solution.py:337
  48.9 4.7 %collective-permute-start.5 = (bf16[16,512]{1,0:T(8,128)(2,1)S(1)}, bf16[16,512]{1,0:T(8,128)(2,1)S(1)}, u32[]{:S(2)}, u32[]{:S(2)}) collective-permute-start(bf16[16,512]{1,0:T(8,128)(2,1)S(1)} %get-tuple-element.54), channel_id=1, source_target_pairs={{0,8},{8,0},{1,9},{9,1},{2,10},{10,2},{3,11},{11,3},{4,12},{12,4},... | collective-permute-start | bytes 49160 | tf_op jit(solution)/shard_map/ppermute | solution.py:332
  54.5 2.1 %last_layer.1 = (bf16[16,512]{1,0:T(8,128)(2,1)S(1)}, bf16[16,512]{1,0:T(8,128)(2,1)S(1)}, f32[128,512]{1,0:T(8,128)S(1)}, bf16[304,512]{1,0:T(8,128)(2,1)S(1)}) custom-call(s32[1,1]{1,0:T(1,128)} %bitcast.core, bf16[128,512]{1,0:T(8,128)(2,1)S(1)} %get-tuple-element.52.rows.rows_1, bf16[16,512]{1,0:T(8,128)(2,1)S(1)} %collective-permute-done.4.outer.outer_1, ...), custom_call_target="tpu_custom_call" | custom-call | flops 100000000 | bytes 2000000 | tf_op jit(solution)/shard_map/last_layer/pallas_call | solution.py:50
  56.6 1.9 %collective-permute-start.6 = (bf16[16,512]{1,0:T(8,128)(2,1)S(1)}, bf16[16,512]{1,0:T(8,128)(2,1)S(1)}, u32[]{:S(2)}, u32[]{:S(2)}) collective-permute-start(bf16[16,512]{1,0:T(8,128)(2,1)S(1)} %get-tuple-element.59), channel_id=1, source_target_pairs={{0,504},{8,16},{16,8},{24,32},{32,24},{40,48},{48,40},{56,64},{64,... | collective-permute-start | bytes 49160 | tf_op jit(solution)/shard_map/ppermute | solution.py:337
  58.5 6.2 %collective-permute-start.7 = (bf16[16,512]{1,0:T(8,128)(2,1)S(1)}, bf16[16,512]{1,0:T(8,128)(2,1)S(1)}, u32[]{:S(2)}, u32[]{:S(2)}) collective-permute-start(bf16[16,512]{1,0:T(8,128)(2,1)S(1)} %get-tuple-element.60), channel_id=1, source_target_pairs={{0,8},{8,0},{1,9},{9,1},{2,10},{10,2},{3,11},{11,3},{4,12},{12,4},... | collective-permute-start | bytes 49160 | tf_op jit(solution)/shard_map/ppermute | solution.py:332
  64.8 1.1 last_rest.1
  66.7 3.5 %collective-permute-start.8 = (bf16[624,512]{1,0:T(8,128)(2,1)S(1)}, bf16[624,512]{1,0:T(8,128)(2,1)S(1)}, u32[]{:S(2)}, u32[]{:S(2)}) collective-permute-start(bf16[624,512]{1,0:T(8,128)(2,1)S(1)} %get-tuple-element.65.pack), channel_id=1, source_target_pairs={{0,8},{8,0},{1,9},{9,1},{2,10},{10,2},{3,11},{11,3},{4,12},{12,4},... | collective-permute-start | bytes 1916936 | tf_op jit(solution)/shard_map/ppermute | solution.py:332
  70.8 1.1 collective-permute-done.8.peer
  72.5 17.4 %all_to_all.20.parts = bf16[4,528,256]{2,1,0:T(8,128)(2,1)S(1)} all-to-all(bf16[4,528,256]{2,1,0:T(8,128)(2,1)S(1)} %terms.1), channel_id=1, replica_groups=mesh['y'=8,'zl'=4,'c'=2,'zh'=2,'x'=4] {'x'}, dimensions={0} | all-to-all | bytes 2162688 | tf_op jit(solution)/shard_map/all_to_all | solution.py:396
  90.2 21.1 %all_to_all.21.parts = bf16[64,2,1152]{2,1,0:T(2,128)(2,1)S(1)} all-to-all(bf16[64,2,1152]{2,1,0:T(2,128)(2,1)S(1)} %first_sum.1), channel_id=1, replica_groups=mesh['y'=8,'zl'=4,'c'=2,'zh'=2,'x'=4] {'y','zh','zl'}, dimensions={0} | all-to-all | bytes 589824 | tf_op jit(solution)/shard_map/all_to_all | solution.py:398
  112.0 5.2 %all-to-all-start.3 = ((bf16[32,2,1152]{2,1,0:T(2,128)(2,1)}), bf16[32,2,1152]{2,1,0:T(2,128)(2,1)S(1)}, u32[]{:S(2)}, u32[]{:S(2)}) async-start(bf16[32,2,1152]{2,1,0:T(2,128)(2,1)} %second_sum.1), calls=%async_computation.3 | async-start | bytes 294912 | tf_op jit(solution)/shard_map/all_to_all | solution.py:401
  117.3 5.7 %collective-permute-start.9 = (bf16[16,512]{1,0:T(8,128)(2,1)S(1)}, bf16[16,512]{1,0:T(8,128)(2,1)S(1)}, u32[]{:S(2)}, u32[]{:S(2)}) collective-permute-start(bf16[16,512]{1,0:T(8,128)(2,1)S(1)} %get-tuple-element.77), channel_id=1, source_target_pairs={{0,504},{8,16},{16,8},{24,32},{32,24},{40,48},{48,40},{56,64},{64,... | collective-permute-start | bytes 49160 | tf_op jit(solution)/shard_map/ppermute | solution.py:337
  122.9 3.8 %collective-permute-start.10 = (bf16[16,512]{1,0:T(8,128)(2,1)S(1)}, bf16[16,512]{1,0:T(8,128)(2,1)S(1)}, u32[]{:S(2)}, u32[]{:S(2)}) collective-permute-start(bf16[16,512]{1,0:T(8,128)(2,1)S(1)} %get-tuple-element.78), channel_id=1, source_target_pairs={{0,8},{8,0},{1,9},{9,1},{2,10},{10,2},{3,11},{11,3},{4,12},{12,4},... | collective-permute-start | bytes 49160 | tf_op jit(solution)/shard_map/ppermute | solution.py:332
  127.5 5.4 %collective-permute-start.11 = (bf16[32,2,1152]{2,1,0:T(2,128)(2,1)S(1)}, bf16[32,2,1152]{2,1,0:T(2,128)(2,1)S(1)}, u32[]{:S(2)}, u32[]{:S(2)}) collective-permute-start(bf16[32,2,1152]{2,1,0:T(2,128)(2,1)S(1)} %all-to-all-done.3.own), channel_id=1, source_target_pairs={{0,8},{8,0},{1,9},{9,1},{2,10},{10,2},{3,11},{11,3},{4,12},{12,4},... | collective-permute-start | bytes 442376 | tf_op jit(solution)/shard_map/ppermute | solution.py:332
  (33 shorter events, 8.6 us)
Async XLA Ops:
  1.6 18.3 %collective-permute-start = (bf16[2,64,512]{2,1,0:T(8,128)(2,1)S(1)}, bf16[2,64,512]{2,1,0:T(8,128)(2,1)S(1)}, u32[]{:S(2)}, u32[]{:S(2)}) collective-permute-start(bf16[2,64,512]{2,1,0:T(8,128)(2,1)S(1)} %broadcast_select_fusion), channel_id=1, source_target_pairs={{0,52},{4,48},{16,36},{20,32},{32,20},{36,16},{48,4},{52,0},{1,53}... | collective-permute-start | bytes 393224 | tf_op jit(solution)/shard_map/ppermute | solution.py:346
  21.0 4.8 %copy-start.1 = (bf16[1,128,512]{2,1,0:T(8,128)(2,1)S(1)}, bf16[1,128,512]{2,1,0:T(8,128)(2,1)}, u32[]{:S(2)}) copy-start(bf16[1,128,512]{2,1,0:T(8,128)(2,1)} %param.9) | copy-start | bytes 393220
  21.0 4.8 %copy-start.3 = (s32[1,2,8]{2,1,0:T(2,128)S(1)}, s32[1,2,8]{2,1,0:T(2,128)}, u32[]{:S(2)}) copy-start(s32[1,2,8]{2,1,0:T(2,128)} %send_rows.7) | copy-start | bytes 196
  21.0 4.8 %copy-start.4 = (s32[1,512]{1,0:T(1,128)S(1)}, s32[1,512]{1,0:T(1,128)}, u32[]{:S(2)}) copy-start(s32[1,512]{1,0:T(1,128)} %senders.1) | copy-start | bytes 6148
  21.0 4.9 %copy-start.5 = (s32[1,512]{1,0:T(1,128)S(1)}, s32[1,512]{1,0:T(1,128)}, u32[]{:S(2)}) copy-start(s32[1,512]{1,0:T(1,128)} %receivers.1) | copy-start | bytes 6148
  21.0 24.4 %copy-start.2 = (f32[2,512]{1,0:T(2,128)S(1)}, f32[2,512]{1,0:T(2,128)}, u32[]{:S(2)}) copy-start(f32[2,512]{1,0:T(2,128)} %gain.7) | copy-start | bytes 12292
  21.0 18.6 %all-to-all-start = ((bf16[4,2,2,64,512]{4,3,2,1,0:T(8,128)(2,1)}), bf16[4,2,2,64,512]{4,3,2,1,0:T(8,128)(2,1)S(1)}, u32[]{:S(2)}, u32[]{:S(2)}) async-start(bf16[4,2,2,64,512]{4,3,2,1,0:T(8,128)(2,1)} %broadcast_in_dim.12), calls=%async_computation | async-start | bytes 2097152 | tf_op jit(solution)/shard_map/all_to_all | solution.py:356
  26.1 6.6 %collective-permute-start.1 = (bf16[16,512]{1,0:T(8,128)(2,1)S(1)}, bf16[16,512]{1,0:T(8,128)(2,1)S(1)}, u32[]{:S(2)}, u32[]{:S(2)}) collective-permute-start(bf16[16,512]{1,0:T(8,128)(2,1)S(1)} %get-tuple-element.45), channel_id=1, source_target_pairs={{0,504},{8,16},{16,8},{24,32},{32,24},{40,48},{48,40},{56,64},{64,... | collective-permute-start | bytes 49160 | tf_op jit(solution)/shard_map/ppermute | solution.py:337
  28.1 5.5 %collective-permute-start.2 = (bf16[16,512]{1,0:T(8,128)(2,1)S(1)}, bf16[16,512]{1,0:T(8,128)(2,1)S(1)}, u32[]{:S(2)}, u32[]{:S(2)}) collective-permute-start(bf16[16,512]{1,0:T(8,128)(2,1)S(1)} %get-tuple-element.46), channel_id=1, source_target_pairs={{0,8},{8,0},{1,9},{9,1},{2,10},{10,2},{3,11},{11,3},{4,12},{12,4},... | collective-permute-start | bytes 49160 | tf_op jit(solution)/shard_map/ppermute | solution.py:332
  39.6 5.8 %collective-permute-start.3 = (bf16[4,2,2,64,512]{4,3,2,1,0:T(8,128)(2,1)S(1)}, bf16[4,2,2,64,512]{4,3,2,1,0:T(8,128)(2,1)S(1)}, u32[]{:S(2)}, u32[]{:S(2)}) collective-permute-start(bf16[4,2,2,64,512]{4,3,2,1,0:T(8,128)(2,1)S(1)} %all-to-all-done.own), channel_id=1, source_target_pairs={{0,8},{8,0},{1,9},{9,1},{2,10},{10,2},{3,11},{11,3},{4,12},{12,4},... | collective-permute-start | bytes 3145736 | tf_op jit(solution)/shard_map/ppermute | solution.py:332
  45.4 9.1 %copy-start = (bf16[1,128,512]{2,1,0:T(8,128)(2,1)S(1)}, bf16[1,128,512]{2,1,0:T(8,128)(2,1)}, u32[]{:S(2)}) copy-start(bf16[1,128,512]{2,1,0:T(8,128)(2,1)} %param.10) | copy-start | bytes 393220
  47.0 6.6 %collective-permute-start.4 = (bf16[16,512]{1,0:T(8,128)(2,1)S(1)}, bf16[16,512]{1,0:T(8,128)(2,1)S(1)}, u32[]{:S(2)}, u32[]{:S(2)}) collective-permute-start(bf16[16,512]{1,0:T(8,128)(2,1)S(1)} %get-tuple-element.53), channel_id=1, source_target_pairs={{0,504},{8,16},{16,8},{24,32},{32,24},{40,48},{48,40},{56,64},{64,... | collective-permute-start | bytes 49160 | tf_op jit(solution)/shard_map/ppermute | solution.py:337
  48.9 5.5 %collective-permute-start.5 = (bf16[16,512]{1,0:T(8,128)(2,1)S(1)}, bf16[16,512]{1,0:T(8,128)(2,1)S(1)}, u32[]{:S(2)}, u32[]{:S(2)}) collective-permute-start(bf16[16,512]{1,0:T(8,128)(2,1)S(1)} %get-tuple-element.54), channel_id=1, source_target_pairs={{0,8},{8,0},{1,9},{9,1},{2,10},{10,2},{3,11},{11,3},{4,12},{12,4},... | collective-permute-start | bytes 49160 | tf_op jit(solution)/shard_map/ppermute | solution.py:332
  56.6 9.3 %collective-permute-start.6 = (bf16[16,512]{1,0:T(8,128)(2,1)S(1)}, bf16[16,512]{1,0:T(8,128)(2,1)S(1)}, u32[]{:S(2)}, u32[]{:S(2)}) collective-permute-start(bf16[16,512]{1,0:T(8,128)(2,1)S(1)} %get-tuple-element.59), channel_id=1, source_target_pairs={{0,504},{8,16},{16,8},{24,32},{32,24},{40,48},{48,40},{56,64},{64,... | collective-permute-start | bytes 49160 | tf_op jit(solution)/shard_map/ppermute | solution.py:337
  58.5 7.3 %collective-permute-start.7 = (bf16[16,512]{1,0:T(8,128)(2,1)S(1)}, bf16[16,512]{1,0:T(8,128)(2,1)S(1)}, u32[]{:S(2)}, u32[]{:S(2)}) collective-permute-start(bf16[16,512]{1,0:T(8,128)(2,1)S(1)} %get-tuple-element.60), channel_id=1, source_target_pairs={{0,8},{8,0},{1,9},{9,1},{2,10},{10,2},{3,11},{11,3},{4,12},{12,4},... | collective-permute-start | bytes 49160 | tf_op jit(solution)/shard_map/ppermute | solution.py:332
  66.7 5.2 %collective-permute-start.8 = (bf16[624,512]{1,0:T(8,128)(2,1)S(1)}, bf16[624,512]{1,0:T(8,128)(2,1)S(1)}, u32[]{:S(2)}, u32[]{:S(2)}) collective-permute-start(bf16[624,512]{1,0:T(8,128)(2,1)S(1)} %get-tuple-element.65.pack), channel_id=1, source_target_pairs={{0,8},{8,0},{1,9},{9,1},{2,10},{10,2},{3,11},{11,3},{4,12},{12,4},... | collective-permute-start | bytes 1916936 | tf_op jit(solution)/shard_map/ppermute | solution.py:332
  112.0 15.5 %all-to-all-start.3 = ((bf16[32,2,1152]{2,1,0:T(2,128)(2,1)}), bf16[32,2,1152]{2,1,0:T(2,128)(2,1)S(1)}, u32[]{:S(2)}, u32[]{:S(2)}) async-start(bf16[32,2,1152]{2,1,0:T(2,128)(2,1)} %second_sum.1), calls=%async_computation.3 | async-start | bytes 294912 | tf_op jit(solution)/shard_map/all_to_all | solution.py:401
  117.3 9.5 %collective-permute-start.9 = (bf16[16,512]{1,0:T(8,128)(2,1)S(1)}, bf16[16,512]{1,0:T(8,128)(2,1)S(1)}, u32[]{:S(2)}, u32[]{:S(2)}) collective-permute-start(bf16[16,512]{1,0:T(8,128)(2,1)S(1)} %get-tuple-element.77), channel_id=1, source_target_pairs={{0,504},{8,16},{16,8},{24,32},{32,24},{40,48},{48,40},{56,64},{64,... | collective-permute-start | bytes 49160 | tf_op jit(solution)/shard_map/ppermute | solution.py:337
  122.9 4.6 %collective-permute-start.10 = (bf16[16,512]{1,0:T(8,128)(2,1)S(1)}, bf16[16,512]{1,0:T(8,128)(2,1)S(1)}, u32[]{:S(2)}, u32[]{:S(2)}) collective-permute-start(bf16[16,512]{1,0:T(8,128)(2,1)S(1)} %get-tuple-element.78), channel_id=1, source_target_pairs={{0,8},{8,0},{1,9},{9,1},{2,10},{10,2},{3,11},{11,3},{4,12},{12,4},... | collective-permute-start | bytes 49160 | tf_op jit(solution)/shard_map/ppermute | solution.py:332
  127.5 6.4 %collective-permute-start.11 = (bf16[32,2,1152]{2,1,0:T(2,128)(2,1)S(1)}, bf16[32,2,1152]{2,1,0:T(2,128)(2,1)S(1)}, u32[]{:S(2)}, u32[]{:S(2)}) collective-permute-start(bf16[32,2,1152]{2,1,0:T(2,128)(2,1)S(1)} %all-to-all-done.3.own), channel_id=1, source_target_pairs={{0,8},{8,0},{1,9},{9,1},{2,10},{10,2},{3,11},{11,3},{4,12},{12,4},... | collective-permute-start | bytes 442376 | tf_op jit(solution)/shard_map/ppermute | solution.py:332
